TPU v7x, 32 devices: a whole 2x2x4 slice. The times are simulated.
32 devices in a mesh: shard: 4 (over z), ctx: 4 (over x, core), tp: 2 (over y).
Axes of the slice: x: 2, y: 2, z: 4, core: 2. Of those that a mesh axis runs over, the one named last changes fastest.
Arguments:
- x_in: bfloat16 [1024, 4, 512], P(('ctx', 'tp'), 'shard'), may hold values from -6 to 6
- w_qkv: bfloat16 [2, 3, 512, 512], P(None, None, 'shard', 'tp'), may hold values from -0.25 to 0.25
- b_qv: bfloat16 [2, 2, 8, 64], P(None, None, 'tp', 'shard'), may hold values from -3 to 3
- w_proj: bfloat16 [2, 512, 512], P(None, 'tp', 'shard'), may hold values from -1.5 to 1.5
- w_fc1: bfloat16 [2, 512, 2048], P(None, 'shard', 'tp'), may hold values from -0.25 to 0.25
- b_fc1: bfloat16 [2, 32, 64], P(None, 'tp', 'shard'), may hold values from -3 to 3
- w_fc2: bfloat16 [2, 2048, 512], P(None, 'tp', 'shard'), may hold values from -0.125 to 0.125
- gains: bfloat16 [2, 2, 512], P(None, None, 'shard'), may hold values from 0.099609375 to 1.8984375
- biases: bfloat16 [2, 4, 512], P(None, None, 'shard'), may hold values from -3 to 3
- cotangent: bfloat16 [1024, 4, 512], P(('ctx', 'tp'), 'shard'), may hold values from -6 to 6
Outputs:
- activations: bfloat16 [1024, 4, 512], P(('ctx', 'tp'), 'shard')
- grad_x: float32 [1024, 4, 512], P(('ctx', 'tp'), 'shard')
- grad_w_qkv: float32 [2, 3, 512, 512], P(None, None, 'shard', 'tp')
- grad_b_qv: float32 [2, 2, 8, 64], P(None, None, 'tp', 'shard')
- grad_w_proj: float32 [2, 512, 512], P(None, 'tp', 'shard')
- grad_w_fc1: float32 [2, 512, 2048], P(None, 'shard', 'tp')
- grad_b_fc1: float32 [2, 32, 64], P(None, 'tp', 'shard')
- grad_w_fc2: float32 [2, 2048, 512], P(None, 'tp', 'shard')
- grad_gains: float32 [2, 2, 512], P(None, None, 'shard')
- grad_biases: float32 [2, 4, 512], P(None, None, 'shard')
All inputs are finite; a program needn't handle non-finite values.
Results may differ from a plain program's by a relative error of at most 0.017.
Values may be sent and summed in bfloat16 or wider, within the bound.
No kernel may reach another device: no remote copies, remote signals or barrier semaphores. Data moves between devices by JAX's collectives and lax.ppermute only.
A program may use at most 128 MiB of HBM per device.

v0:
```python
import functools
import math

import jax
import jax.numpy as jnp
from jax import lax
from jax.experimental import pallas as pl
from jax.experimental.pallas import tpu as pltpu
from jax.sharding import PartitionSpec as P

epsilon = 1e-05
masked_value = -1e30
lanes = 128
f32 = jnp.float32
bf16 = jnp.bfloat16


def normalize(values):
    center = jnp.mean(values, axis=-1, keepdims=True)
    shifted = values - center
    scale_inv = lax.rsqrt(jnp.mean(shifted * shifted, axis=-1, keepdims=True) + epsilon)
    return (shifted * scale_inv, scale_inv)


def norm_back(grad_norm, normed, scale_inv):
    mean_grad = jnp.mean(grad_norm, axis=-1, keepdims=True)
    mean_prod = jnp.mean(grad_norm * normed, axis=-1, keepdims=True)
    return scale_inv * (grad_norm - mean_grad - normed * mean_prod)


def gelu_tanh(values):
    return jax.nn.gelu(values, approximate=True)


def dot(pattern, left, right):
    return jnp.einsum(pattern, left, right, preferred_element_type=f32)


def to_rows(array):
    rows, columns = array.shape[-2:]
    if columns % lanes or rows % 16:
        return array.reshape(-1, lanes)
    tiles = array.reshape(-1, rows, columns // lanes, lanes)
    return jnp.swapaxes(tiles, 1, 2).reshape(-1, lanes)


def from_rows(packed, shape):
    rows, columns = shape[-2:]
    lead = packed.shape[:-2]
    if columns % lanes or rows % 16:
        return packed.reshape(lead + tuple(shape))
    count = math.prod(shape[:-2])
    tiles = packed.reshape(lead + (count, columns // lanes, rows, lanes))
    return jnp.swapaxes(tiles, -3, -2).reshape(lead + tuple(shape))


def small_rows(arrays):
    flat = jnp.concatenate([array.reshape(-1) for array in arrays])
    size = -(-flat.shape[0] // (64 * lanes)) * 64 * lanes
    return jnp.pad(flat, (0, size - flat.shape[0])).reshape(-1, lanes)


def join(gathered, axis):
    moved = jnp.moveaxis(gathered, 0, axis)
    shape = moved.shape
    return moved.reshape(shape[:axis] + (shape[axis] * shape[axis + 1],) + shape[axis + 2 :])


def split(whole, axis, shards):
    shape = whole.shape
    parts = whole.reshape(shape[:axis] + (shards, shape[axis] // shards) + shape[axis + 1 :])
    return jnp.moveaxis(parts, axis, 0)


def swap_tp(values):
    return lax.ppermute(values, "tp", [(0, 1), (1, 0)])


def swap_core(values):
    return lax.ppermute(values, "ctx", [(0, 1), (1, 0), (2, 3), (3, 2)])


def swap_x(values):
    return lax.ppermute(values, "ctx", [(0, 2), (2, 0), (1, 3), (3, 1)])


def swap_both(values):
    return lax.ppermute(values, "ctx", [(0, 3), (3, 0), (1, 2), (2, 1)])


def other_half(values):
    half = values.shape[0] // 2
    return jnp.concatenate([values[half:], values[:half]])


def gather_packed(packed, shards):
    quarter = packed.shape[0] // 4
    own = lax.dynamic_slice_in_dim(packed, lax.axis_index("ctx") * quarter, quarter, 0)
    return lax.all_gather(own, ("shard", "ctx"), axis=0, tiled=True).reshape(
        shards, packed.shape[0], lanes
    )


def halves(values, bit):
    half = values.shape[1] // 2
    keep = lax.dynamic_slice_in_dim(values, bit * half, half, 1)
    send = lax.dynamic_slice_in_dim(values, (1 - bit) * half, half, 1)
    return keep, send


def paired(own, other, bit):
    return jnp.where(
        bit == 0, jnp.concatenate([own, other]), jnp.concatenate([other, own])
    )


def reduce_packed(packed):
    place = lax.axis_index("ctx")
    core, chip = place % 2, place // 2
    keep, send = halves(packed, core)
    half = (keep.astype(f32) + swap_core(send).astype(f32)).astype(bf16)
    keep, send = halves(half, chip)
    quarter = (keep.astype(f32) + swap_x(send).astype(f32)).astype(bf16)
    parts = lax.all_to_all(quarter, "shard", split_axis=0, concat_axis=0, tiled=True)
    total = jnp.sum(parts.astype(f32), axis=0).astype(bf16)
    both = paired(total, swap_x(total), chip)
    return paired(both, swap_core(both), core)


def positions(offsets, tp_place, chunk, block):
    half = block // 2
    return chunk * block + (offsets + tp_place * half) % block


def attention_mask(block):
    place, tp_place = lax.axis_index("ctx"), lax.axis_index("tp")
    offsets = jnp.arange(block, dtype=jnp.int32)
    rows = positions(offsets, tp_place, place, block)
    keys = jnp.concatenate([positions(offsets, tp_place, place ^ j, block) for j in range(4)])
    return keys[None, :] <= rows[:, None]


def head_split(values, heads):
    return values.reshape(values.shape[0], heads, values.shape[1] // heads)


def attend(queries, key_all, value_all, mask, heads):
    scale_factor = (queries.shape[1] // heads) ** (-0.5)
    scores = dot("qhe,khe->hqk", head_split(queries, heads), head_split(key_all, heads))
    scores = jnp.where(mask, scores * scale_factor, masked_value)
    row_top = jnp.max(scores, axis=-1, keepdims=True)
    exponent = jnp.exp(scores - row_top)
    totals = jnp.sum(exponent, axis=-1, keepdims=True)
    probs = (exponent / totals).astype(bf16)
    out = dot("hqk,khe->qhe", probs, head_split(value_all, heads))
    return out.reshape(queries.shape).astype(bf16), row_top + jnp.log(totals)


def attend_back(queries, key_all, value_all, mask, heads, log_sums, grad_out):
    scale_factor = (queries.shape[1] // heads) ** (-0.5)
    query_heads, key_heads = head_split(queries, heads), head_split(key_all, heads)
    grad_heads = head_split(grad_out, heads)
    scores = dot("qhe,khe->hqk", query_heads, key_heads)
    scores = jnp.where(mask, scores * scale_factor, masked_value)
    probs = jnp.exp(scores - log_sums)
    grad_probs = dot("qhe,khe->hqk", grad_heads, head_split(value_all, heads))
    row_dot = jnp.sum(probs * grad_probs, axis=-1, keepdims=True)
    grad_scores = (probs * (grad_probs - row_dot)).astype(bf16)
    grad_q = dot("hqk,khe->qhe", grad_scores, key_heads) * scale_factor
    grad_k = dot("hqk,qhe->khe", grad_scores, query_heads) * scale_factor
    grad_v = dot("hqk,qhe->khe", probs.astype(bf16), grad_heads)
    return (
        grad_q.reshape(queries.shape).astype(bf16),
        jnp.concatenate(
            [grad_k.reshape(key_all.shape), grad_v.reshape(key_all.shape)], axis=1
        ).astype(bf16),
    )


def body_any(x_in, w_qkv, b_qv, w_proj, w_fc1, b_fc1, w_fc2, gains, biases, cotangent):
    depth = w_qkv.shape[0]
    shards = lax.axis_size("shard")
    own_rows, width = x_in.shape[0], x_in.shape[2]
    block = 2 * own_rows
    heads = b_qv.shape[2]
    half_width = w_qkv.shape[3]
    hidden = w_fc1.shape[2]

    small_shapes = [gains.shape, biases.shape, b_qv.shape, b_fc1.shape]
    small = small_rows([gains, biases, b_qv, b_fc1])
    group_a0 = jnp.concatenate([small, to_rows(w_qkv[0])])
    group_b0 = jnp.concatenate([to_rows(w_proj[0]), to_rows(w_fc1[0]), to_rows(w_fc2[0])])
    rest = []
    for index in range(1, depth):
        rest += [to_rows(w_qkv[index]), to_rows(w_proj[index]), to_rows(w_fc1[index]), to_rows(w_fc2[index])]
    group_rest = jnp.concatenate(rest)

    gathered_a0 = gather_packed(group_a0, shards)
    gathered_b0 = gather_packed(group_b0, shards)
    gathered_rest = gather_packed(group_rest, shards)

    def cutter(gathered, start):
        place = [start]

        def take(shape, axis):
            rows = math.prod(shape) // lanes
            piece = from_rows(gathered[:, place[0] : place[0] + rows], shape)
            place[0] += rows
            return join(piece, axis)

        return take

    shape_qkv, shape_proj = w_qkv.shape[1:], w_proj.shape[1:]
    shape_fc1, shape_fc2 = w_fc1.shape[1:], w_fc2.shape[1:]
    take_a, take_b, take_r = cutter(gathered_a0, small.shape[0]), cutter(gathered_b0, 0), cutter(gathered_rest, 0)
    weights = []
    for index in range(depth):
        take_q, take_o = (take_a, take_b) if index == 0 else (take_r, take_r)
        weights.append(
            (take_q(shape_qkv, 1), take_o(shape_proj, 1), take_o(shape_fc1, 0), take_o(shape_fc2, 1))
        )
    flat = gathered_a0[:, : small.shape[0]].reshape(shards, -1)
    vectors, start = [], 0
    for shape in small_shapes:
        size = math.prod(shape)
        piece = flat[:, start : start + size].reshape((shards,) + shape)
        vectors.append(join(piece, len(shape) - 1).astype(f32))
        start += size
    gain_all, bias_all, b_qv_all, b_fc1_all = vectors

    mask = attention_mask(block)
    x_own = x_in[:, 0]
    state = jnp.concatenate([x_own, swap_tp(x_own)]).astype(f32)
    g_own = cotangent[:, 0]
    grad_state = jnp.concatenate([g_own, swap_tp(g_own)]).astype(f32)

    stored = []
    for index in range(depth):
        w_query, w_out, w_first, w_second = weights[index]
        normed_in, scale_in = normalize(state)
        low_in = (normed_in * gain_all[index, 0] + bias_all[index, 0]).astype(bf16)
        bias_q = b_qv_all[index, 0].reshape(half_width)
        bias_v = b_qv_all[index, 1].reshape(half_width)
        queries = (dot("rd,df->rf", low_in, w_query[0]) + bias_q).astype(bf16)
        keys = dot("rd,df->rf", low_in, w_query[1]).astype(bf16)
        values = (dot("rd,df->rf", low_in, w_query[2]) + bias_v).astype(bf16)
        kv_own = jnp.concatenate([keys, values], axis=1)
        kv_chip = swap_x(kv_own)
        kv_all = jnp.concatenate([kv_own, swap_core(kv_own), kv_chip, swap_core(kv_chip)])
        key_all, value_all = kv_all[:, :half_width], kv_all[:, half_width:]
        attn, log_sums = attend(queries, key_all, value_all, mask, heads)
        attn_other = other_half(swap_tp(attn))
        w_out_other = swap_tp(w_out)
        middle = (
            state
            + dot("rf,fd->rd", attn, w_out)
            + dot("rf,fd->rd", attn_other, w_out_other)
            + bias_all[index, 1]
        )
        normed_mid, scale_mid = normalize(middle)
        low_mid = (normed_mid * gain_all[index, 1] + bias_all[index, 2]).astype(bf16)
        pre_act = dot("rd,df->rf", low_mid, w_first) + b_fc1_all[index].reshape(hidden)
        act = gelu_tanh(pre_act).astype(bf16)
        partial = dot("rf,fd->rd", act, w_second)
        if index == depth - 1:
            received = swap_tp(partial[own_rows:].astype(bf16)).astype(f32)
            output = middle[:own_rows] + partial[:own_rows] + received + bias_all[index, 3]
        else:
            received = other_half(swap_tp(partial.astype(bf16))).astype(f32)
            state = middle + partial + received + bias_all[index, 3]
        stored.append(
            (normed_in, scale_in, low_in, queries, key_all, value_all, log_sums, attn,
             normed_mid, scale_mid, low_mid, pre_act, act)
        )
    output = output.astype(bf16)[:, None]

    results = [None] * depth
    for index in reversed(range(depth)):
        w_query, w_out, w_first, w_second = weights[index]
        (normed_in, scale_in, low_in, queries, key_all, value_all, log_sums, attn,
         normed_mid, scale_mid, low_mid, pre_act, act) = stored[index]
        grad_bias_mlp = jnp.sum(grad_state, axis=0)
        grad_low = grad_state.astype(bf16)
        grad_hidden = dot("rd,fd->rf", grad_low, w_second)
        unused, gelu_pull = jax.vjp(gelu_tanh, pre_act)
        grad_pre = gelu_pull(grad_hidden)[0].astype(bf16)
        grad_w_second = dot("rf,rd->fd", act, grad_low)
        grad_w_first = dot("rd,rf->df", low_mid, grad_pre)
        grad_b_first = jnp.sum(grad_pre, axis=0, dtype=f32)
        partial = dot("rf,df->rd", grad_pre, w_first)
        mlp_rows = jnp.concatenate(
            [
                jax.vmap(to_rows)(split(grad_w_first.astype(bf16), 0, shards)),
                jax.vmap(to_rows)(split(grad_w_second.astype(bf16), 1, shards)),
            ],
            axis=1,
        )
        mlp_total = reduce_packed(mlp_rows)
        grad_mid = partial + other_half(swap_tp(partial.astype(bf16))).astype(f32)
        grad_gain_mid = jnp.sum(grad_mid * normed_mid, axis=0)
        grad_beta_mid = jnp.sum(grad_mid, axis=0)
        grad_middle = grad_state + norm_back(grad_mid * gain_all[index, 1], normed_mid, scale_mid)
        grad_bias_attn = jnp.sum(grad_middle, axis=0)
        grad_low = grad_middle.astype(bf16)
        grad_attn = dot("rd,fd->rf", grad_low, w_out).astype(bf16)
        grad_w_out = dot("rf,rd->fd", attn, grad_low)
        grad_q, grad_kv = attend_back(
            queries, key_all, value_all, mask, heads, log_sums, grad_attn
        )
        part = grad_kv.reshape(4, block, 2 * half_width)
        sent = swap_core(jnp.stack([part[1], part[3]])).astype(f32)
        mine = part[0].astype(f32) + sent[0]
        chip = (part[2].astype(f32) + sent[1]).astype(bf16)
        grad_kv = (mine + swap_x(chip).astype(f32)).astype(bf16)
        grad_qkv = jnp.stack([grad_q, grad_kv[:, :half_width], grad_kv[:, half_width:]])
        grad_w_query = dot("rd,crf->cdf", low_in, grad_qkv)
        grad_b_query = jnp.sum(grad_qkv[0::2], axis=1, dtype=f32)
        partial = dot("crf,cdf->rd", grad_qkv, w_query)
        grad_in = partial + other_half(swap_tp(partial.astype(bf16))).astype(f32)
        grad_gain_in = jnp.sum(grad_in * normed_in, axis=0)
        grad_beta_in = jnp.sum(grad_in, axis=0)
        grad_state = grad_middle + norm_back(grad_in * gain_all[index, 0], normed_in, scale_in)

        vectors = [
            jnp.stack([grad_gain_in, grad_gain_mid]),
            jnp.stack([grad_beta_in, grad_bias_attn, grad_beta_mid, grad_bias_mlp]),
            grad_b_query.reshape(2, heads, half_width // heads),
            grad_b_first.reshape(b_fc1_all.shape[1:]),
        ]
        parts = [split(vector, vector.ndim - 1, shards) for vector in vectors]
        part_shapes = [part.shape[1:] for part in parts]
        attn_rows = jnp.concatenate(
            [
                jax.vmap(to_rows)(split(grad_w_query.astype(bf16), 1, shards)),
                jax.vmap(to_rows)(split(grad_w_out.astype(bf16), 1, shards)),
                jax.vmap(lambda *own: small_rows(own))(*parts).astype(bf16),
            ],
            axis=1,
        )
        attn_total = reduce_packed(attn_rows)

        def pieces(total, shapes):
            place, out = 0, []
            for shape in shapes:
                rows = math.prod(shape) // lanes
                out.append(from_rows(total[place : place + rows], shape).astype(f32))
                place += rows
            return out, total[place:].reshape(-1)

        (out_fc1, out_fc2), unused = pieces(mlp_total, [shape_fc1, shape_fc2])
        (out_qkv, out_proj), tail = pieces(attn_total, [shape_qkv, shape_proj])
        small_out, start = [], 0
        for shape in part_shapes:
            size = math.prod(shape)
            small_out.append(tail[start : start + size].reshape(shape).astype(f32))
            start += size
        results[index] = (
            out_qkv, small_out[2], out_proj, out_fc1, small_out[3], out_fc2, small_out[0], small_out[1]
        )
    stacked = tuple(
        jnp.stack([results[index][member] for index in range(depth)]) for member in range(8)
    )
    return (output, grad_state[:own_rows, None]) + stacked


def compiler_params():
    return pltpu.CompilerParams(vmem_limit_bytes=56 * 2**20)


def whole(array):
    zeros = (0,) * array.ndim
    return pl.BlockSpec(array.shape, lambda i: zeros)


def rows_at(array, rows, start, lead=None, first=0):
    lead = array.shape[0] if lead is None else lead
    return pl.BlockSpec((lead, rows, lanes), lambda i: (first, start // rows, 0))


def run(kernel, outs, place, operands, scratch=(), flops=2**20, after=()):
    arrays, specs = [], []
    count = 1 + len(operands)

    def inner(*refs):
        kernel(*refs[:count], *refs[count + len(after) :])

    for operand in operands:
        array, spec = operand if isinstance(operand, tuple) else (operand, whole(operand))
        arrays.append(array)
        specs.append(spec)
    out_shape = [jax.ShapeDtypeStruct(shape, kind) for shape, kind in outs]
    after = list(after)
    arrays += after
    specs += [pl.BlockSpec(memory_space=pl.ANY)] * len(after)
    call = pl.pallas_call(
        inner,
        grid=(1,),
        out_shape=out_shape,
        in_specs=[pl.BlockSpec(memory_space=pltpu.SMEM)] + specs,
        out_specs=[whole(shape) for shape in out_shape],
        scratch_shapes=list(scratch),
        compiler_params=compiler_params(),
        cost_estimate=pl.CostEstimate(flops=flops, bytes_accessed=1024, transcendentals=0),
    )
    return list(call(place, *arrays))


def mm(left, right):
    return lax.dot_general(left, right, (((1,), (0,)), ((), ())), preferred_element_type=f32)


def mm_nt(left, right):
    return lax.dot_general(left, right, (((1,), (1,)), ((), ())), preferred_element_type=f32)


def mm_tn(left, right):
    return lax.dot_general(left, right, (((0,), (0,)), ((), ())), preferred_element_type=f32)


def lane_join(parts):
    return jnp.concatenate(parts, axis=1)


def row_join(parts):
    return jnp.concatenate(parts, axis=0)


class Pieces:
    def __init__(self, refs, place):
        self.refs, self.place = refs, place

    def tile(self, k, p, start, rows):
        if len(self.refs) == 1:
            z, c = self.place[0], self.place[1]
            return self.refs[0][(z - k + 4) % 4, p ^ c, start : start + rows]
        if k == 0:
            return self.refs[0][p, start : start + rows]
        return self.refs[1 + p][k - 1, start : start + rows]


def first_block(pieces, p):
    return row_join(
        [lane_join([pieces.tile(k, p, j * 128, 128) for j in range(2)]) for k in range(4)]
    )


def second_block(pieces, p):
    return lane_join([pieces.tile(k, p, 0, 256) for k in range(4)])


def small_row(small_local, small_far, row):
    parts = [small_local[0, row : row + 1]] + [small_far[k, row : row + 1] for k in range(3)]
    return lane_join(parts).astype(f32)


def spread(small_local, small_far, row, place_z, half, later=None):
    def rows_from(row):
        return row_join(
            [small_local[0, row : row + 1]] + [small_far[k, row : row + 1] for k in range(3)]
        ).astype(f32)

    source = rows_from(row)
    if later is not None:
        source = jnp.where(later == 0, source, rows_from(row + 1))
    source = source.astype(bf16)
    take = lax.broadcasted_iota(jnp.int32, (128, 256), 0)
    lane = lax.broadcasted_iota(jnp.int32, (128, 256), 1)
    wanted = half * 64 + (lane // 64) * 16 + lane % 16
    table = (take == wanted).astype(f32).astype(bf16)
    rows = mm(source, table)
    chunk = lax.broadcasted_iota(jnp.int32, (4, 256), 0)
    lane = lax.broadcasted_iota(jnp.int32, (4, 256), 1)
    keep = (lane % 64) // 16 == (place_z - chunk + 4) % 4
    return jnp.sum(jnp.where(keep, rows, 0.0), axis=0, keepdims=True)


def pack_kernel(kinds):
    def kernel(place, *refs):
        c = place[1]
        out, send = refs[-2:]
        start = 0
        for ref, kind in zip(refs, kinds):
            for q in range(4):
                to = q ^ c
                if kind == "first":
                    for j in range(2):
                        column = (2 * q + j) * 128
                        out[to, start + j * 128 : start + (j + 1) * 128] = ref[0, :, column : column + 128]
                elif kind == "second":
                    out[to, start : start + 256] = ref[0, q * 256 : (q + 1) * 256]
                elif kind == "proj":
                    out[to, start : start + 64] = ref[0, q * 64 : (q + 1) * 64]
                elif kind == "qkv":
                    for tile in range(6):
                        row = start + tile * 32
                        column = (tile % 2) * 128
                        out[to, row : row + 32] = ref[0, tile // 2, q * 32 : (q + 1) * 32, column : column + 128]
                else:
                    out[to, start : start + 32] = ref[...]
            start += kind_rows[kind]
        send[...] = out[0]

    return kernel


def quarter_pack_kernel(kinds):
    def kernel(place, *refs):
        out = refs[-1]
        for q in range(4):

            @pl.when(place[1] == q)
            def write(q=q):
                start = 0
                for ref, kind in zip(refs, kinds):
                    if kind == "first":
                        for j in range(2):
                            column = (2 * q + j) * 128
                            out[start + j * 128 : start + (j + 1) * 128] = ref[0, :, column : column + 128]
                    elif kind == "second":
                        out[start : start + 256] = ref[0, q * 256 : (q + 1) * 256]
                    elif kind == "proj":
                        out[start : start + 64] = ref[0, q * 64 : (q + 1) * 64]
                    else:
                        for tile in range(6):
                            row = start + tile * 32
                            column = (tile % 2) * 128
                            out[row : row + 32] = ref[0, tile // 2, q * 32 : (q + 1) * 32, column : column + 128]
                    start += kind_rows[kind]

    return kernel


kind_rows = {"first": 256, "second": 256, "proj": 64, "qkv": 192, "small": 32}


def pack(place, kinds, arrays, index, after=(), whole_quarters=True):
    rows = sum(kind_rows[kind] for kind in kinds)
    operands = []
    for kind, array in zip(kinds, arrays):
        if kind == "small":
            operands.append(array)
        else:
            block = (1,) + array.shape[1:]
            at = (index,) + (0,) * (array.ndim - 1)
            operands.append((array, pl.BlockSpec(block, lambda i, at=at: at)))
    if not whole_quarters:
        return run(quarter_pack_kernel(kinds), [((rows, lanes), bf16)], place, operands, after=after)[0]
    return run(
        pack_kernel(kinds), [((4, rows, lanes), bf16), ((rows, lanes), bf16)], place, operands, after=after
    )


def gather(quarter):
    full = lax.all_gather(quarter, ("shard", "ctx"), axis=0)
    return full.reshape((4, 4) + quarter.shape)


def gathered_rows(array, rows, start):
    return [(array, pl.BlockSpec((4, 4, rows, lanes), lambda i: (0, 0, start // rows, 0)))]


def shift(values, step):
    return lax.ppermute(values, "shard", [(z, (z + step) % 4) for z in range(4)])


def far_chunks(send):
    return [shift(send, k) for k in (1, 2, 3)]


def stack_kernel(place, one, two, three, out):
    for k, ref in enumerate((one, two, three)):
        out[k] = ref[...]


def stack(place, got, after=()):
    return run(stack_kernel, [((3,) + got[0].shape, bf16)], place, got, after=after)[0]


def pieces_of(group, rows, start):
    return [(array, rows_at(array, rows, start)) for array in group]


def small_of(group):
    return [(group[0], rows_at(group[0], 32, 256, lead=1)), (group[1], rows_at(group[1], 32, 256))]


def query_kernel(index, first_layer):
    def kernel(place, *refs):
        c = place[1]
        if first_layer:
            own, peer, small_local, small_far = refs[:4]
            pieces = Pieces(refs[4:9], place)
            grad_out = refs[14]
            grad_out[...] = row_join([own[128:], peer[128:]]).astype(f32)
            state_out, low_out, q_out, kv_out, w_out = refs[9:14]
            state = row_join([own[:128], peer[:128]]).astype(f32)
        else:
            middle, mine, other, small_local, small_far = refs[:5]
            pieces = Pieces(refs[5:6], place)
            state_out, low_out, q_out, kv_out, w_out = refs[6:]
            received = row_join([other[128:], other[:128]])
            state = (
                middle[...]
                + mine[...].astype(f32)
                + received.astype(f32)
                + small_row(small_local, small_far, 4 + 4 * (index - 1) + 3)
            )
        for k in range(4):
            for p in range(4):
                for tile in range(6):
                    w_out[k, p ^ c, :, tile * 128 : (tile + 1) * 128] = pieces.tile(k, p, tile * 32, 32)
        state_out[...] = state
        normed, scale = normalize(state)
        low = (
            normed * small_row(small_local, small_far, 2 * index)
            + small_row(small_local, small_far, 4 + 4 * index)
        ).astype(bf16)
        low_out[...] = low
        w_all = w_out[...].reshape(512, 768)
        row = 12 + index
        bias_q = spread(small_local, small_far, row, place[0], 0)
        bias_v = spread(small_local, small_far, row, place[0], 1)
        kv_out[:, :256] = mm(low, w_all[:, 256:512]).astype(bf16)
        kv_out[:, 256:] = (mm(low, w_all[:, 512:]) + bias_v).astype(bf16)
        q_out[...] = (mm(low, w_all[:, :256]) + bias_q).astype(bf16)

    return kernel


def seen(place, j):
    c, t = place[1], place[2]
    if j:
        return None
    row = lax.broadcasted_iota(jnp.int32, (256, 256), 0) ^ (t * 128)
    key = lax.broadcasted_iota(jnp.int32, (256, 256), 1) ^ (t * 128)
    return key <= row


def masked_scores(query, chunks, own_mask, place):
    parts = []
    for j in range(4):
        scores = mm_nt(query, chunks[j]) * 0.125
        if j == 0:
            scores = jnp.where(own_mask, scores, masked_value)
        else:
            scores = jnp.where((place[1] ^ j) < place[1], scores, masked_value)
        parts.append(scores)
    return parts


def attend_kernel(count, place, *refs):
    c = place[1]
    q, chunks = refs[0], refs[1:5]
    pieces = Pieces(refs[5 : 5 + count], place)
    attn_out, lse_out, partial_out, w_out = refs[5 + count :]
    for k in range(4):
        for p in range(4):
            w_out[p ^ c, :, k * 128 : (k + 1) * 128] = pieces.tile(k, p, 0, 64)
    own_mask = seen(place, 0)
    results = []
    for head in range(4):
        low, high = head * 64, (head + 1) * 64
        parts = masked_scores(q[:, low:high], [chunk[:, low:high] for chunk in chunks], own_mask, place)
        scores = lane_join(parts)
        top = jnp.max(scores, axis=1, keepdims=True)
        exponent = jnp.exp(scores - top)
        total = jnp.sum(exponent, axis=1, keepdims=True)
        values = row_join([chunk[:, 256 + low : 256 + high] for chunk in chunks])
        results.append(mm(exponent.astype(bf16), values) / total)
        lse_out[:, head : head + 1] = top + jnp.log(total)
    attn = lane_join(results).astype(bf16)
    attn_out[...] = attn
    partial_out[...] = mm(attn, w_out[...].reshape(256, 512)).astype(bf16)


def mlp_kernel(index):
    def kernel(place, *refs):
        state, mine, other, small_local, small_far = refs[:5]
        first, second = Pieces(refs[5:6], place), Pieces(refs[6:7], place)
        middle_out, low_out, pre_out, partial_out = refs[7:]
        received = row_join([other[128:], other[:128]])
        middle = (
            state[...]
            + mine[...].astype(f32)
            + received.astype(f32)
            + small_row(small_local, small_far, 4 + 4 * index + 1)
        )
        middle_out[...] = middle
        normed, scale = normalize(middle)
        low = (
            normed * small_row(small_local, small_far, 2 * index + 1)
            + small_row(small_local, small_far, 4 + 4 * index + 2)
        ).astype(bf16)
        low_out[...] = low
        total = None
        for p in range(4):
            q = p ^ place[1]
            bias = spread(small_local, small_far, 14 + 2 * index, place[0], q % 2, q // 2)
            pre = mm(low, first_block(first, p)) + bias
            pre_out[:, p * 256 : (p + 1) * 256] = pre
            act = gelu_tanh(pre).astype(bf16)
            part = mm(act, second_block(second, p))
            total = part if total is None else total + part
        partial_out[...] = total.astype(bf16)

    return kernel


root = math.sqrt(2 / math.pi)


def mlp_back(grad, pre_ref, low_ref, first, second, place, outs):
    partial_out, bias_out, b_first_out, keep, send = outs
    grad_low = grad.astype(bf16)
    bias_out[...] = jnp.sum(grad, axis=0, keepdims=True)
    total = None
    for p in range(4):
        pre = pre_ref[:, p * 256 : (p + 1) * 256]
        square = pre * pre
        wave = jnp.tanh(root * pre * (1 + 0.044715 * square))
        half = 0.5 * (1 + wave)
        act = (pre * half).astype(bf16)
        slope = half + 0.5 * pre * (1 - wave * wave) * root * (1 + 3 * 0.044715 * square)
        w_second = second_block(second, p)
        grad_pre = mm_nt(grad_low, w_second) * slope
        grad_pre_low = grad_pre.astype(bf16)
        b_first_out[p ^ place[1]] = jnp.sum(grad_pre_low.astype(f32), axis=0, keepdims=True)
        part = mm_nt(grad_pre_low, first_block(first, p))
        total = part if total is None else total + part
        to = keep if p % 2 == 0 else send
        grad_first = mm_tn(low_ref[...], grad_pre_low).astype(bf16)
        grad_second = mm_tn(act, grad_low).astype(bf16)
        for k in range(4):
            for j in range(2):
                to[p // 2, k, j * 128 : (j + 1) * 128] = grad_first[
                    k * 128 : (k + 1) * 128, j * 128 : (j + 1) * 128
                ]
            to[p // 2, k, 256:512] = grad_second[:, k * 128 : (k + 1) * 128]
    partial_out[...] = total.astype(bf16)


def norm_step(grad_out, gain, values):
    normed, scale = normalize(values)
    sums = row_join(
        [
            jnp.sum(grad_out * normed, axis=0, keepdims=True),
            jnp.sum(grad_out, axis=0, keepdims=True),
        ]
    )
    return norm_back(grad_out * gain, normed, scale), sums


def received_sum(mine, other):
    return mine[...].astype(f32) + row_join([other[128:], other[:128]]).astype(f32)


def top_kernel(place, *refs):
    grad, pre, low = refs[:3]
    first, second = Pieces(refs[3:4], place), Pieces(refs[4:5], place)
    mlp_back(grad[...], pre, low, first, second, place, refs[5:])


def lower_kernel(index):
    def kernel(place, *refs):
        grad_mid, mine, other, state, small_local, small_far, pre, low = refs[:8]
        first, second = Pieces(refs[8:9], place), Pieces(refs[9:10], place)
        grad_out, sums_out = refs[10:12]
        grad, sums = norm_step(
            received_sum(mine, other), small_row(small_local, small_far, 2 * (index + 1)), state[...]
        )
        sums_out[...] = sums
        grad = grad_mid[...] + grad
        grad_out[...] = grad
        mlp_back(grad, pre, low, first, second, place, refs[12:])

    return kernel


def attend_back_kernel(index):
    def kernel(place, *refs):
        mine, other, middle, grad_state, small_local, small_far = refs[:6]
        attn, w_out, q = refs[6:9]
        chunks, lse = refs[9:13], refs[13]
        grad_out, sums_out, gw_out, dq_out, keep, send = refs[14:]
        grad, sums = norm_step(
            received_sum(mine, other), small_row(small_local, small_far, 2 * index + 1), middle[...]
        )
        grad = grad_state[...] + grad
        grad_out[...] = grad
        sums_out[0:2] = sums
        sums_out[2:3] = jnp.sum(grad, axis=0, keepdims=True)
        grad_low = grad.astype(bf16)
        grad_attn = mm_nt(grad_low, w_out[...].reshape(256, 512)).astype(bf16)
        gw_out[...] = mm_tn(attn[...], grad_low).astype(bf16).reshape(4, 64, 512)
        own_mask = seen(place, 0)
        dq_all = []
        dk_all = [[] for j in range(4)]
        dv_all = [[] for j in range(4)]
        for head in range(4):
            low, high = head * 64, (head + 1) * 64
            query, grad_head = q[:, low:high], grad_attn[:, low:high]
            keys = [chunk[:, low:high] for chunk in chunks]
            row_dot = jnp.sum(
                grad_head.astype(f32) * attn[:, low:high].astype(f32), axis=1, keepdims=True
            )
            log_sum = lse[:, head : head + 1]
            parts = masked_scores(query, keys, own_mask, place)
            dq = None
            for j in range(4):
                probs = jnp.exp(parts[j] - log_sum)
                grad_probs = mm_nt(grad_head, chunks[j][:, 256 + low : 256 + high])
                grad_scores = (probs * (grad_probs - row_dot)).astype(bf16)
                part = mm(grad_scores, keys[j])
                dq = part if dq is None else dq + part
                dk_all[j].append(mm_tn(grad_scores, query) * 0.125)
                dv_all[j].append(mm_tn(probs.astype(bf16), grad_head))
            dq_all.append(dq * 0.125)
        dq_out[...] = lane_join(dq_all).astype(bf16)
        for j in range(4):
            to = keep if j % 2 == 0 else send
            to[j // 2, :, :256] = lane_join(dk_all[j]).astype(bf16)
            to[j // 2, :, 256:] = lane_join(dv_all[j]).astype(bf16)

    return kernel


def halve_kernel(place, keep, got, own_out, send_out):
    own_out[...] = (keep[0].astype(f32) + got[0].astype(f32)).astype(bf16)
    send_out[...] = (keep[1].astype(f32) + got[1].astype(f32)).astype(bf16)


def halve_in_order(place, keep, got, out):
    z, chip = place[0], place[1] // 2
    for half in range(2):
        for k in range(4):
            total = keep[half, k].astype(f32) + got[half, k].astype(f32)
            out[half ^ chip, (z - k + 4) % 4] = total.astype(bf16)


def query_back_kernel(place, *refs):
    dq, dkv, got, low, w_ref, gw_ref = refs[:6]
    partial_out, b_out, keep, send, scratch = refs[6:]
    c = place[1]
    grad_kv = (dkv[...].astype(f32) + got[...].astype(f32)).astype(bf16)
    grad_qkv = lane_join([dq[...], grad_kv])
    partial_out[...] = mm_nt(grad_qkv, w_ref[...].reshape(512, 768)).astype(bf16)
    b_out[0:1] = jnp.sum(dq[...].astype(f32), axis=0, keepdims=True)
    b_out[1:2] = jnp.sum(grad_kv[:, 256:].astype(f32), axis=0, keepdims=True)
    scratch[...] = mm_tn(low[...], grad_qkv).astype(bf16).reshape(4, 4, 32, 768)
    for p in range(4):
        to = keep if p % 2 == 0 else send
        for k in range(4):
            for tile in range(6):
                to[p // 2, k, tile * 32 : (tile + 1) * 32] = scratch[
                    k, p ^ c, :, tile * 128 : (tile + 1) * 128
                ]
            to[p // 2, k, 192:256] = gw_ref[p ^ c, :, k * 128 : (k + 1) * 128]


def four_kernel(place, one, two, three, four, out):
    out[...] = (one[...] + two[...]) + (three[...] + four[...])


def quarter_kernel(place, own, got, *outs):
    for k in range(4):
        outs[k][...] = (own[k].astype(f32) + got[k].astype(f32)).astype(bf16)


def total_kernel(place, own, one, two, three, out):
    total = own[...].astype(f32) + one[...].astype(f32)
    out[...] = (total + (two[...].astype(f32) + three[...].astype(f32))).astype(bf16)


class Chain:
    def __init__(self, place, keep, send):
        self.place, self.rows = place, keep.shape[2]
        self.state = [keep, send]

    def halve(self, after=()):
        keep, send = self.state
        self.state = run(
            halve_kernel, [((4, self.rows, lanes), bf16)] * 2, self.place, [keep, swap_core(send)], flops=2**20, after=after
        )

    def quarter(self, after=()):
        own, send = self.state
        self.state = run(
            quarter_kernel, [((self.rows, lanes), bf16)] * 4, self.place, [own, swap_x(send)], flops=2**20, after=after
        )

    def total(self, after=()):
        got = [shift(self.state[k], 4 - k) for k in (1, 2, 3)]
        self.state = run(
            total_kernel, [((self.rows, lanes), bf16)], self.place, [self.state[0]] + got, flops=2**20, after=after
        )

    def collect(self):
        (total,) = self.state
        chip = swap_x(total)
        return [total, swap_core(total), chip, swap_core(chip)]


def spread_sum(place, keep, send, after=()):
    rows = keep.shape[2]
    (both,) = run(
        halve_in_order, [((2, 4, rows, lanes), bf16)], place, [keep, swap_core(send)], after=after
    )
    mine = lax.psum_scatter(both, "ctx", scatter_dimension=0, axis_index_groups=[[0, 2], [1, 3]])
    mine = lax.psum_scatter(mine, "shard", scatter_dimension=0)
    return both, lax.all_gather(mine, "ctx", axis=0)


def fill(place, refs, scratch):
    for p in range(4):
        if len(refs) == 1:
            scratch[p ^ place[1]] = refs[0][p].astype(f32)
        else:
            scratch[p] = refs[p][...].astype(f32)


def hidden_out_kernel(place, *refs):
    c = place[1]
    first_out, second_out, scratch = refs[-3:]
    fill(place, refs[:-3], scratch)
    for q in range(4):
        for j in range(2):
            column = (2 * q + j) * 128
            first_out[0, :, column : column + 128] = scratch[q ^ c, j * 128 : (j + 1) * 128]
        second_out[0, q * 256 : (q + 1) * 256] = scratch[q ^ c, 256:]


def heads_out_kernel(place, *refs):
    c = place[1]
    qkv_out, proj_out, scratch = refs[-3:]
    fill(place, refs[:-3], scratch)
    for q in range(4):
        for tile in range(6):
            column = (tile % 2) * 128
            qkv_out[0, tile // 2, q * 32 : (q + 1) * 32, column : column + 128] = scratch[
                q ^ c, tile * 32 : (tile + 1) * 32
            ]
        proj_out[0, q * 64 : (q + 1) * 64] = scratch[q ^ c, 192:]


def layer_out(kernel, place, totals, layer, shapes, before, after):
    rows = totals[0].shape[-2]
    extra = list(before) + list(after)
    count = 1 + len(totals)

    def inner(*refs):
        kernel(*refs[:count], *refs[count + len(extra) :])

    def block(shape):
        at = (layer,) + (0,) * (len(shape) - 1)
        return pl.BlockSpec((1,) + tuple(shape[1:]), lambda i: at)

    return list(
        pl.pallas_call(
            inner,
            grid=(1,),
            out_shape=[jax.ShapeDtypeStruct(shape, f32) for shape in shapes],
            in_specs=[pl.BlockSpec(memory_space=pltpu.SMEM)]
            + [whole(total) for total in totals]
            + [pl.BlockSpec(memory_space=pl.ANY)] * len(extra),
            out_specs=[block(shape) for shape in shapes],
            scratch_shapes=[pltpu.VMEM((4, rows, lanes), f32)],
            input_output_aliases={count + i: i for i in range(len(before))},
            compiler_params=compiler_params(),
            cost_estimate=pl.CostEstimate(flops=2**20, bytes_accessed=1024, transcendentals=0),
        )(place, *totals, *extra)
    )


def hidden_out(place, totals, layer, shape_one, shape_two, before, after=()):
    return layer_out(hidden_out_kernel, place, totals, layer, (shape_one, shape_two), before, after)


def heads_out(place, totals, layer, shape_one, shape_two, before, after=()):
    return layer_out(heads_out_kernel, place, totals, layer, (shape_one, shape_two), before, after)


def last_kernel(place, *refs):
    grad_mid, mine, other, state, small_local, small_far = refs[:6]
    sums_in = refs[6]
    sums_mid, bias_mlp, b_query, b_first = refs[7:9], refs[9:11], refs[11:13], refs[13:15]
    grad_out, out = refs[15:]
    grad, sums = norm_step(received_sum(mine, other), small_row(small_local, small_far, 0), state[...])
    grad_out[...] = grad_mid[:128] + grad[:128]
    for layer in range(2):
        inner = sums if layer == 0 else sums_in[...]
        mid = sums_mid[layer]
        rows = [
            (2 * layer, inner[0:1]),
            (2 * layer + 1, mid[0:1]),
            (4 + 4 * layer, inner[1:2]),
            (5 + 4 * layer, mid[2:3]),
            (6 + 4 * layer, mid[1:2]),
            (7 + 4 * layer, bias_mlp[layer][...]),
        ]
        for k in range(4):
            for row, value in rows:
                out[k, row : row + 1] = value[:, k * 128 : (k + 1) * 128]
            for channel in range(2):
                for j in range(2):
                    row = 12 + 4 * layer + 2 * channel + j
                    out[k, row : row + 1] = b_query[layer][channel : channel + 1, j * 128 : (j + 1) * 128]
            for q in range(4):
                for j in range(2):
                    row = 20 + 8 * layer + 2 * q + j
                    out[k, row : row + 1] = b_first[layer][q, :, j * 128 : (j + 1) * 128]
    out[:, 36:] = jnp.zeros((4, 4, lanes), f32)


def turn(values, place_z, back):
    rows = values.shape[0]
    chunks = values.reshape(rows, 4, lanes)
    order = (place_z - jnp.arange(4)) % 4
    return jnp.concatenate(
        [lax.dynamic_slice_in_dim(values, order[k] * lanes, lanes, 1) for k in range(4)], axis=1
    )


def body_four(x_in, w_qkv, b_qv, w_proj, w_fc1, b_fc1, w_fc2, gains, biases, cotangent):
    z, c, t = lax.axis_index("shard"), lax.axis_index("ctx"), lax.axis_index("tp")
    place = jnp.stack([z, c, t]).astype(jnp.int32)
    flat = jnp.concatenate([array.reshape(-1) for array in (gains, biases, b_qv, b_fc1)])
    small = jnp.pad(flat, (0, 32 * lanes - flat.shape[0])).reshape(32, lanes)

    local_a, send_a = pack(place, ("qkv", "proj", "small"), (w_qkv, w_proj, small), 0)
    pair_own = turn(jnp.concatenate([x_in[:, 0], cotangent[:, 0]]), z, False)
    pair_peer = swap_tp(pair_own)
    got_a = far_chunks(send_a)
    far_a = stack(place, got_a)
    chip_a = swap_x(far_a)
    group_a0 = [local_a, far_a, swap_core(far_a), chip_a, swap_core(chip_a)]
    send_b = pack(place, ("first", "second"), (w_fc1, w_fc2), 0, after=[far_a], whole_quarters=False)
    kinds = ("first", "second", "proj", "qkv")
    send_1 = pack(
        place, kinds, (w_fc1, w_fc2, w_proj, w_qkv), 1, after=[far_a, send_b], whole_quarters=False
    )
    full_b, full_1 = gather(send_b), gather(send_1)

    small_parts = small_of(group_a0)
    parts = {
        "qkv": [pieces_of(group_a0, 192, 0), gathered_rows(full_1, 192, 576)],
        "proj": [pieces_of(group_a0, 64, 192), gathered_rows(full_1, 64, 512)],
        "first": [gathered_rows(full_b, 256, 0), gathered_rows(full_1, 256, 0)],
        "second": [gathered_rows(full_b, 256, 256), gathered_rows(full_1, 256, 256)],
    }
    square, wide = (256, 512), (256, 256)
    saved = []
    for layer in range(2):
        source = [pair_own, pair_peer] if layer == 0 else [middle, partial, swap_tp(partial)]
        more = [(square, f32)] if layer == 0 else []
        state, low_in, q, kv, w_all, *passed = run(
            query_kernel(layer, layer == 0),
            [(square, f32), (square, bf16), (wide, bf16), (square, bf16), ((4, 4, 32, 768), bf16)] + more,
            place,
            source + small_parts + parts["qkv"][layer],
        )
        if layer == 0:
            g_all = passed[0]
        kv_chip = swap_x(kv)
        chunks = [kv, swap_core(kv), kv_chip, swap_core(kv_chip)]
        attn, lse, partial, w_out = run(
            functools.partial(attend_kernel, len(parts["proj"][layer])),
            [(wide, bf16), ((256, lanes), f32), (square, bf16), ((4, 64, 512), bf16)],
            place,
            [q] + chunks + parts["proj"][layer],
        )
        middle, low_mid, pre, partial = run(
            mlp_kernel(layer),
            [(square, f32), (square, bf16), ((256, 1024), f32), (square, bf16)],
            place,
            [state, partial, swap_tp(partial)] + small_parts + parts["first"][layer] + parts["second"][layer],
        )
        saved.append((state, low_in, q, chunks, w_all, attn, lse, w_out, middle, low_mid, pre))

    received = swap_tp(partial[128:]).astype(f32)
    output = None
    bias_last = jnp.concatenate([small_parts[0][0][0, 267:268], small_parts[1][0][:, 267]]).reshape(1, 512)
    output = middle[:128] + partial[:128].astype(f32) + received + bias_last.astype(f32)
    output = turn(output.astype(bf16), z, True)[:, None]

    hidden_outs = [
        (square, bf16),
        ((1, 512), f32),
        ((4, 1, 256), f32),
        ((2, 4, 512, lanes), bf16),
        ((2, 4, 512, lanes), bf16),
    ]
    sums_mid, bias_mlp, b_query, b_first = [0, 0], [0, 0], [0, 0], [0, 0]
    hidden = [None, None]
    for layer in (1, 0):
        state, low_in, q, chunks, w_all, attn, lse, w_out, middle, low_mid, pre = saved[layer]
        tail = [pre, low_mid] + parts["first"][layer] + parts["second"][layer]
        if layer == 1:
            grad_state = g_all
            partial, bias_mlp[1], b_first[1], keep, send = run(
                top_kernel, hidden_outs, place, [grad_state] + tail
            )
        else:
            half, heads_total = spread_sum(place, keep, send)
            grad_state, sums_in, partial, bias_mlp[0], b_first[0], keep, send = run(
                lower_kernel(0),
                [(square, f32), ((2, 512), f32)] + hidden_outs,
                place,
                [grad_mid, partial, swap_tp(partial), saved[1][0]] + small_parts + tail,
                after=[half],
            )
        half, hidden[layer] = spread_sum(place, keep, send)
        grad_mid, sums_mid[layer], gw_out, dq, keep, send = run(
            attend_back_kernel(layer),
            [
                (square, f32),
                ((3, 512), f32),
                ((4, 64, 512), bf16),
                (wide, bf16),
                ((2, 256, 512), bf16),
                ((2, 256, 512), bf16),
            ],
            place,
            [partial, swap_tp(partial), middle, grad_state] + small_parts + [attn, w_out, q] + chunks + [lse],
            after=[half],
        )
        dkv, chip = run(halve_kernel, [(square, bf16)] * 2, place, [keep, swap_core(send)])
        partial, b_query[layer], keep, send = run(
            query_back_kernel,
            [
                (square, bf16),
                ((2, 256), f32),
                ((2, 4, 256, lanes), bf16),
                ((2, 4, 256, lanes), bf16),
            ],
            place,
            [dq, dkv, swap_x(chip), low_in, w_all, gw_out],
            scratch=[pltpu.VMEM((4, 4, 32, 768), bf16)],
            after=[output] if layer == 1 else [],
        )
    last = Chain(place, keep, send)
    last.halve()
    grad_x, sums = run(
        last_kernel,
        [((128, 512), f32), ((4, 40, lanes), f32)],
        place,
        [grad_mid, partial, swap_tp(partial), saved[0][0]]
        + small_parts
        + [sums_in]
        + sums_mid
        + bias_mlp
        + b_query
        + b_first,
        after=last.state,
    )
    last.quarter(after=[grad_x])
    grad_x = turn(grad_x, z, True)[:, None]
    (sums,) = run(
        four_kernel,
        [((4, 40, lanes), f32)],
        place,
        [sums, swap_core(sums), swap_x(sums), swap_both(sums)],
        after=last.state,
    )
    last.total(after=[sums])
    outs_heads = heads_out(
        place, [heads_total], 1, w_qkv.shape, w_proj.shape, [], after=last.state
    )
    outs_hidden = hidden_out(place, [hidden[1]], 1, w_fc1.shape, w_fc2.shape, [], after=last.state)
    grad_fc1, grad_fc2 = hidden_out(place, [hidden[0]], 0, w_fc1.shape, w_fc2.shape, outs_hidden)
    got = [shift(sums[k], 4 - k) for k in (1, 2, 3)]
    total = sums[0] + got[0] + got[1] + got[2]
    grad_gains = total[:4].reshape(gains.shape)
    grad_biases = total[4:12].reshape(biases.shape)
    rest_q = total[12:20].reshape(2, 2, 4, 64)
    rest_f = total[20:36].reshape(2, 16, 64)
    grad_b_qv = lax.dynamic_slice_in_dim(rest_q, z * 16, 16, 3)
    grad_b_fc1 = lax.dynamic_slice_in_dim(rest_f, z * 16, 16, 2)

    grad_qkv, grad_proj = heads_out(place, last.collect(), 0, w_qkv.shape, w_proj.shape, outs_heads)
    return (
        output, grad_x, grad_qkv, grad_b_qv, grad_proj, grad_fc1, grad_b_fc1, grad_fc2, grad_gains, grad_biases
    )


def body(*args):
    x_in, w_qkv, b_qv, w_proj, w_fc1 = args[:5]
    expected = ((128, 1, 512), (2, 3, 128, 256), (2, 2, 4, 16), (2, 256, 128), (2, 128, 1024))
    sizes = (lax.axis_size("shard"), lax.axis_size("ctx"), lax.axis_size("tp"))
    shapes = tuple(array.shape for array in (x_in, w_qkv, b_qv, w_proj, w_fc1))
    if sizes == (4, 4, 2) and shapes == expected:
        return body_four(*args)
    return body_any(*args)


def solution(mesh):
    return jax.shard_map(
        body,
        mesh=mesh,
        in_specs=(
            P(("ctx", "tp"), "shard", None),
            P(None, None, "shard", "tp"),
            P(None, None, "tp", "shard"),
            P(None, "tp", "shard"),
            P(None, "shard", "tp"),
            P(None, "tp", "shard"),
            P(None, "tp", "shard"),
            P(None, None, "shard"),
            P(None, None, "shard"),
            P(("ctx", "tp"), "shard", None),
        ),
        out_specs=(
            P(("ctx", "tp"), "shard", None),
            P(("ctx", "tp"), "shard", None),
            P(None, None, "shard", "tp"),
            P(None, None, "tp", "shard"),
            P(None, "tp", "shard"),
            P(None, "shard", "tp"),
            P(None, "tp", "shard"),
            P(None, "tp", "shard"),
            P(None, None, "shard"),
            P(None, None, "shard"),
        ),
        check_vma=False,
    )
```

profile of v0, /device:TPU:0, one launch (start us, length us, event | category | flops | bytes accessed | tf_op | source)
XLA Modules:
  0.0 368.0 jit_solution(6316956896030436654)
XLA Ops:
  36.7 5.3 %collective-permute-done.5.refs_8_.refs_9_ = bf16[3,288,128]{2,1,0:T(8,128)(2,1)S(1)} collective-permute-done((bf16[3,288,128]{2,1,0:T(8,128)(2,1)S(1)}, bf16[3,288,128]{2,1,0:T(8,128)(2,1)S(1)}, u32[]{:S(2)}, u32[]{:S(2)}) %collective-permute-start.5) | collective-permute-done | bytes 221216 | tf_op jit(solution)/shard_map/ppermute | solution.py:84
  48.6 7.3 %collective-permute-done.8.refs_4_.refs_12_ = bf16[256,512]{1,0:T(8,128)(2,1)S(1)} collective-permute-done((bf16[256,512]{1,0:T(8,128)(2,1)}, bf16[256,512]{1,0:T(8,128)(2,1)S(1)}, u32[]{:S(2)}, u32[]{:S(2)}) %collective-permute-start.8) | collective-permute-done | bytes 262176 | tf_op jit(solution)/shard_map/ppermute | solution.py:84
  58.1 4.8 %shard_map.180 = (bf16[256,256]{1,0:T(8,128)(2,1)}, f32[256,128]{1,0:T(8,128)}, bf16[256,512]{1,0:T(8,128)(2,1)}, bf16[4,64,512]{2,1,0:T(8,128)(2,1)}) custom-call(s32[3]{0:T(128)} %pad_add_fusion.refs_0_, bf16[256,256]{1,0:T(8,128)(2,1)} %get-tuple-element.94.refs_1_.refs_9_, bf16[256,512]{1,0:T(8,128)(2,1)} %get-tuple-element.95.refs_2_.refs_10_, ...), custom_call_target="tpu_custom_call" | custom-call | flops 1048576 | bytes 1024 | tf_op jit(solution)/shard_map/pallas_call | solution.py:405
  64.0 7.4 %collective-permute-done.10.refs_3_ = bf16[256,512]{1,0:T(8,128)(2,1)S(1)} collective-permute-done((bf16[256,512]{1,0:T(8,128)(2,1)}, bf16[256,512]{1,0:T(8,128)(2,1)S(1)}, u32[]{:S(2)}, u32[]{:S(2)}) %collective-permute-start.10) | collective-permute-done | bytes 262176 | tf_op jit(solution)/shard_map/ppermute | solution.py:76
  72.1 4.3 %shard_map.182 = (f32[256,512]{1,0:T(8,128)}, bf16[256,512]{1,0:T(8,128)(2,1)}, f32[256,1024]{1,0:T(8,128)}, bf16[256,512]{1,0:T(8,128)(2,1)}) custom-call(s32[3]{0:T(128)} %pad_add_fusion.refs_0_, f32[256,512]{1,0:T(8,128)} %get-tuple-element.93.refs_1_.refs_4_, bf16[256,512]{1,0:T(8,128)(2,1)} %get-tuple-element.96.refs_2_, bf16[256,512]{1,0:T(8,128)(2,1)} %copy-done.29, ...), custom_call_target="tpu_custom_call" | custom-call | flops 1048576 | bytes 1024 | tf_op jit(solution)/shard_map/pallas_call | solution.py:405
  77.6 6.5 %collective-permute-done.11.refs_3_ = bf16[256,512]{1,0:T(8,128)(2,1)S(1)} collective-permute-done((bf16[256,512]{1,0:T(8,128)(2,1)}, bf16[256,512]{1,0:T(8,128)(2,1)S(1)}, u32[]{:S(2)}, u32[]{:S(2)}) %collective-permute-start.11) | collective-permute-done | bytes 262176 | tf_op jit(solution)/shard_map/ppermute | solution.py:76
  84.1 33.2 %all-gather.7.cloned.1.call-done = bf16[12288,128]{1,0:T(8,128)(2,1)} async-done(((bf16[768,128]{1,0:T(8,128)(2,1)}), bf16[12288,128]{1,0:T(8,128)(2,1)}) %all-gather.7.cloned.1.call-update) | async-done | bytes 3145744 | tf_op jit(solution)/shard_map/all_gather | solution.py:554
  121.0 8.1 %collective-permute-done.13.refs_4_.refs_12_ = bf16[256,512]{1,0:T(8,128)(2,1)S(1)} collective-permute-done((bf16[256,512]{1,0:T(8,128)(2,1)}, bf16[256,512]{1,0:T(8,128)(2,1)S(1)}, u32[]{:S(2)}, u32[]{:S(2)}) %collective-permute-start.13) | collective-permute-done | bytes 262176 | tf_op jit(solution)/shard_map/ppermute | solution.py:84
  131.4 4.9 %shard_map.185 = (bf16[256,256]{1,0:T(8,128)(2,1)}, f32[256,128]{1,0:T(8,128)}, bf16[256,512]{1,0:T(8,128)(2,1)}, bf16[4,64,512]{2,1,0:T(8,128)(2,1)}) custom-call(s32[3]{0:T(128)} %pad_add_fusion.refs_0_, bf16[256,256]{1,0:T(8,128)(2,1)} %get-tuple-element.100.refs_1_.refs_9_, bf16[256,512]{1,0:T(8,128)(2,1)} %get-tuple-element.101.refs_2_.refs_10_, ...), custom_call_target="tpu_custom_call" | custom-call | flops 1048576 | bytes 1024 | tf_op jit(solution)/shard_map/pallas_call | solution.py:405
  137.8 7.1 %collective-permute-done.15.refs_3_ = bf16[256,512]{1,0:T(8,128)(2,1)S(1)} collective-permute-done((bf16[256,512]{1,0:T(8,128)(2,1)}, bf16[256,512]{1,0:T(8,128)(2,1)S(1)}, u32[]{:S(2)}, u32[]{:S(2)}) %collective-permute-start.15) | collective-permute-done | bytes 262176 | tf_op jit(solution)/shard_map/ppermute | solution.py:76
  149.9 5.3 %shard_map.187 = (bf16[256,512]{1,0:T(8,128)(2,1)}, f32[1,512]{1,0:T(1,128)}, f32[4,1,256]{2,1,0:T(1,128)}, bf16[2,4,512,128]{3,2,1,0:T(8,128)(2,1)}, bf16[2,4,512,128]{3,2,1,0:T(8,128)(2,1)}) custom-call(s32[3]{0:T(128)} %pad_add_fusion.refs_0_, f32[256,512]{1,0:T(8,128)} %get-tuple-element.105.refs_1_.refs_4_, f32[256,1024]{1,0:T(8,128)} %get-tuple-element.106.refs_2_, ...), custom_call_target="tpu_custom_call" | custom-call | flops 1048576 | bytes 1024 | tf_op jit(solution)/shard_map/pallas_call | solution.py:405
  164.8 9.2 %shard_map.189 = (f32[256,512]{1,0:T(8,128)}, f32[3,512]{1,0:T(4,128)}, bf16[4,64,512]{2,1,0:T(8,128)(2,1)}, bf16[256,256]{1,0:T(8,128)(2,1)}, bf16[2,256,512]{2...) custom-call(s32[3]{0:T(128)} %pad_add_fusion.refs_0_, bf16[256,512]{1,0:T(8,128)(2,1)} %get-tuple-element.108.refs_1_, ...), custom_call_target="tpu_custom_call" | custom-call | flops 1048576 | bytes 1024 | tf_op jit(solution)/shard_map/pallas_call | solution.py:405
  181.5 7.0 %collective-permute-done.20.refs_3_ = bf16[256,512]{1,0:T(8,128)(2,1)S(1)} collective-permute-done((bf16[256,512]{1,0:T(8,128)(2,1)}, bf16[256,512]{1,0:T(8,128)(2,1)S(1)}, u32[]{:S(2)}, u32[]{:S(2)}) %collective-permute-start.20) | collective-permute-done | bytes 262176 | tf_op jit(solution)/shard_map/ppermute | solution.py:84
  198.0 12.0 %reduce-scatter.7.cloned.1.call-done = bf16[1,4,256,128]{3,2,1,0:T(8,128)(2,1)} async-done(((bf16[2,4,256,128]{3,2,1,0:T(8,128)(2,1)}), bf16[1,4,256,128]{3,2,1,0:T(8,128)(2,1)}) %reduce-scatter.7.cloned.1.call-update) | async-done | bytes 262160 | tf_op jit(solution)/shard_map/reduce_scatter | solution.py:908
  211.6 6.6 %collective-permute-done.21.refs_3_ = bf16[256,512]{1,0:T(8,128)(2,1)S(1)} collective-permute-done((bf16[256,512]{1,0:T(8,128)(2,1)S(1)}, bf16[256,512]{1,0:T(8,128)(2,1)S(1)}, u32[]{:S(2)}, u32[]{:S(2)}) %collective-permute-start.21) | collective-permute-done | bytes 262176 | tf_op jit(solution)/shard_map/ppermute | solution.py:76
  218.9 6.0 %shard_map.193 = (f32[256,512]{1,0:T(8,128)}, f32[2,512]{1,0:T(2,128)}, bf16[256,512]{1,0:T(8,128)(2,1)}, f32[1,512]{1,0:T(1,128)}, f32[4,1,256]{2,1,0:T(1,128)}...) custom-call(s32[3]{0:T(128)} %pad_add_fusion.refs_0_, f32[256,512]{1,0:T(8,128)} %get-tuple-element.114.refs_1_, ...), custom_call_target="tpu_custom_call" | custom-call | flops 1048576 | bytes 1024 | tf_op jit(solution)/shard_map/pallas_call | solution.py:405
  224.9 7.6 %reduce-scatter.15.cloned.1.call-done = bf16[1,4,512,128]{3,2,1,0:T(8,128)(2,1)} async-done(((bf16[2,4,512,128]{3,2,1,0:T(8,128)(2,1)}), bf16[1,4,512,128]{3,2,1,0:T(8,128)(2,1)}) %reduce-scatter.15.cloned.1.call-update) | async-done | bytes 524304 | tf_op jit(solution)/shard_map/reduce_scatter | solution.py:908
  238.2 6.6 %collective-permute-done.23.refs_2_ = bf16[256,512]{1,0:T(8,128)(2,1)S(1)} collective-permute-done((bf16[256,512]{1,0:T(8,128)(2,1)S(1)}, bf16[256,512]{1,0:T(8,128)(2,1)S(1)}, u32[]{:S(2)}, u32[]{:S(2)}) %collective-permute-start.23) | collective-permute-done | bytes 262176 | tf_op jit(solution)/shard_map/ppermute | solution.py:76
  245.5 9.2 %shard_map.195 = (f32[256,512]{1,0:T(8,128)}, f32[3,512]{1,0:T(4,128)}, bf16[4,64,512]{2,1,0:T(8,128)(2,1)}, bf16[256,256]{1,0:T(8,128)(2,1)}, bf16[2,256,512]{2...) custom-call(s32[3]{0:T(128)} %pad_add_fusion.refs_0_, bf16[256,512]{1,0:T(8,128)(2,1)} %get-tuple-element.128.refs_1_, ...), custom_call_target="tpu_custom_call" | custom-call | flops 1048576 | bytes 1024 | tf_op jit(solution)/shard_map/pallas_call | solution.py:405
  260.1 8.1 %collective-permute-done.26.refs_3_ = bf16[256,512]{1,0:T(8,128)(2,1)S(1)} collective-permute-done((bf16[256,512]{1,0:T(8,128)(2,1)}, bf16[256,512]{1,0:T(8,128)(2,1)S(1)}, u32[]{:S(2)}, u32[]{:S(2)}) %collective-permute-start.26) | collective-permute-done | bytes 262176 | tf_op jit(solution)/shard_map/ppermute | solution.py:84
  273.5 6.6 %all_gather.25.refs_1_ = bf16[4,256,128]{2,1,0:T(8,128)(2,1)} all-gather(bf16[1,256,128]{2,1,0:T(8,128)(2,1)} %reduce-scatter.9.cloned.1.call-done), channel_id=1, replica_groups=mesh['shard'=4,'ctx'=4,'tp'=2] {'ctx'}, dimensions={0}, use_global_device_ids=true | all-gather | bytes 327680 | tf_op jit(solution)/shard_map/all_gather | solution.py:910
  284.5 20.1 %all_gather.27.refs_1_ = bf16[4,512,128]{2,1,0:T(8,128)(2,1)} all-gather(bf16[1,512,128]{2,1,0:T(8,128)(2,1)} %reduce-scatter.17.cloned.1.call-done), channel_id=1, replica_groups=mesh['shard'=4,'ctx'=4,'tp'=2] {'ctx'}, dimensions={0}, use_global_device_ids=true | all-gather | bytes 655360 | tf_op jit(solution)/shard_map/all_gather | solution.py:910
  329.4 5.9 %collective-permute-done.31.refs_3_ = bf16[256,128]{1,0:T(8,128)(2,1)S(1)} collective-permute-done((bf16[256,128]{1,0:T(8,128)(2,1)}, bf16[256,128]{1,0:T(8,128)(2,1)S(1)}, u32[]{:S(2)}, u32[]{:S(2)}) %collective-permute-start.31) | collective-permute-done | bytes 65568 | tf_op jit(solution)/shard_map/ppermute | solution.py:563
  349.8 9.2 %all_gather.26.refs_1_ = bf16[4,512,128]{2,1,0:T(8,128)(2,1)} all-gather(bf16[1,512,128]{2,1,0:T(8,128)(2,1)} %reduce-scatter.13.cloned.1.call-done), channel_id=1, replica_groups=mesh['shard'=4,'ctx'=4,'tp'=2] {'ctx'}, dimensions={0}, use_global_device_ids=true | all-gather | bytes 655360 | tf_op jit(solution)/shard_map/all_gather | solution.py:910
  (240 shorter events, 142.7 us)
Async XLA Ops:
  7.2 64.2 %all-gather.5.cloned.1.call-start = ((), (), s32[]{:S(2)}) async-start(), calls=%async_computation.12 | async-start | bytes 2228224 | tf_op jit(solution)/shard_map/all_gather | solution.py:554
  28.1 89.2 %all-gather.7.cloned.1.call-start = ((), (), s32[]{:S(2)}) async-start(), calls=%async_computation.13 | async-start | bytes 3342336 | tf_op jit(solution)/shard_map/all_gather | solution.py:554
  30.0 180.0 %reduce-scatter.7.cloned.1.call-start = ((), (), s32[]{:S(2)}) async-start(), calls=%async_computation.6 | async-start | bytes 786432 | tf_op jit(solution)/shard_map/reduce_scatter | solution.py:908
  33.3 8.7 %collective-permute-start.5 = (bf16[3,288,128]{2,1,0:T(8,128)(2,1)S(1)}, bf16[3,288,128]{2,1,0:T(8,128)(2,1)S(1)}, u32[]{:S(2)}, u32[]{:S(2)}) collective-permute-start(bf16[3,288,128]{2,1,0:T(8,128)(2,1)S(1)} %copy-done), channel_id=1, source_target_pairs={{0,4},{4,0},{2,6},{6,2},{1,5},{5,1},{3,7},{7,3},{8,12},{12,8},{10,... | collective-permute-start | bytes 663560 | tf_op jit(solution)/shard_map/ppermute | solution.py:84
  47.3 8.6 %collective-permute-start.8 = (bf16[256,512]{1,0:T(8,128)(2,1)}, bf16[256,512]{1,0:T(8,128)(2,1)S(1)}, u32[]{:S(2)}, u32[]{:S(2)}) collective-permute-start(bf16[256,512]{1,0:T(8,128)(2,1)} %get-tuple-element.95.refs_2_.refs_10_), channel_id=1, source_target_pairs={{0,4},{4,0},{2,6},{6,2},{1,5},{5,1},{3,7},{7,3},{8,12},{12,8},{10,... | collective-permute-start | bytes 786440 | tf_op jit(solution)/shard_map/ppermute | solution.py:84
  62.9 8.5 %collective-permute-start.10 = (bf16[256,512]{1,0:T(8,128)(2,1)}, bf16[256,512]{1,0:T(8,128)(2,1)S(1)}, u32[]{:S(2)}, u32[]{:S(2)}) collective-permute-start(bf16[256,512]{1,0:T(8,128)(2,1)} %get-tuple-element.96.refs_2_), channel_id=1, source_target_pairs={{0,1},{1,0},{2,3},{3,2},{4,5},{5,4},{6,7},{7,6},{8,9},{9,8},{10,11... | collective-permute-start | bytes 786440 | tf_op jit(solution)/shard_map/ppermute | solution.py:76
  120.5 8.7 %collective-permute-start.13 = (bf16[256,512]{1,0:T(8,128)(2,1)}, bf16[256,512]{1,0:T(8,128)(2,1)S(1)}, u32[]{:S(2)}, u32[]{:S(2)}) collective-permute-start(bf16[256,512]{1,0:T(8,128)(2,1)} %get-tuple-element.101.refs_2_.refs_10_), channel_id=1, source_target_pairs={{0,4},{4,0},{2,6},{6,2},{1,5},{5,1},{3,7},{7,3},{8,12},{12,8},{10,... | collective-permute-start | bytes 786440 | tf_op jit(solution)/shard_map/ppermute | solution.py:84
  121.0 8.1 %collective-permute-start.12 = (bf16[256,512]{1,0:T(8,128)(2,1)}, bf16[256,512]{1,0:T(8,128)(2,1)S(1)}, u32[]{:S(2)}, u32[]{:S(2)}) collective-permute-start(bf16[256,512]{1,0:T(8,128)(2,1)} %get-tuple-element.101.refs_2_.refs_10_), channel_id=1, source_target_pairs={{0,2},{2,0},{4,6},{6,4},{1,3},{3,1},{5,7},{7,5},{8,10},{10,8},{12,... | collective-permute-start | bytes 786440 | tf_op jit(solution)/shard_map/ppermute | solution.py:80
  136.3 8.6 %collective-permute-start.15 = (bf16[256,512]{1,0:T(8,128)(2,1)}, bf16[256,512]{1,0:T(8,128)(2,1)S(1)}, u32[]{:S(2)}, u32[]{:S(2)}) collective-permute-start(bf16[256,512]{1,0:T(8,128)(2,1)} %get-tuple-element.102.refs_2_), channel_id=1, source_target_pairs={{0,1},{1,0},{2,3},{3,2},{4,5},{5,4},{6,7},{7,6},{8,9},{9,8},{10,11... | collective-permute-start | bytes 786440 | tf_op jit(solution)/shard_map/ppermute | solution.py:76
  155.2 8.9 %collective-permute-start.17 = (bf16[256,512]{1,0:T(8,128)(2,1)}, bf16[256,512]{1,0:T(8,128)(2,1)S(1)}, u32[]{:S(2)}, u32[]{:S(2)}) collective-permute-start(bf16[256,512]{1,0:T(8,128)(2,1)} %get-tuple-element.108.refs_1_), channel_id=1, source_target_pairs={{0,1},{1,0},{2,3},{3,2},{4,5},{5,4},{6,7},{7,6},{8,9},{9,8},{10,11... | collective-permute-start | bytes 786440 | tf_op jit(solution)/shard_map/ppermute | solution.py:76
  179.9 8.6 %collective-permute-start.20 = (bf16[256,512]{1,0:T(8,128)(2,1)}, bf16[256,512]{1,0:T(8,128)(2,1)S(1)}, u32[]{:S(2)}, u32[]{:S(2)}) collective-permute-start(bf16[256,512]{1,0:T(8,128)(2,1)} %get-tuple-element.119), channel_id=1, source_target_pairs={{0,4},{4,0},{2,6},{6,2},{1,5},{5,1},{3,7},{7,3},{8,12},{12,8},{10,... | collective-permute-start | bytes 786440 | tf_op jit(solution)/shard_map/ppermute | solution.py:84
  197.4 35.1 %reduce-scatter.15.cloned.1.call-start = ((), (), s32[]{:S(2)}) async-start(), calls=%async_computation.10 | async-start | bytes 1572864 | tf_op jit(solution)/shard_map/reduce_scatter | solution.py:908
  198.0 75.6 %reduce-scatter.9.cloned.1.call-start = ((), (), s32[]{:S(2)}) async-start(), calls=%async_computation.7 | async-start | bytes 327680 | tf_op jit(solution)/shard_map/reduce_scatter | solution.py:909
  210.0 74.5 %reduce-scatter.17.cloned.1.call-start = ((), (), s32[]{:S(2)}) async-start(), calls=%async_computation.11 | async-start | bytes 655360 | tf_op jit(solution)/shard_map/reduce_scatter | solution.py:909
  232.5 77.1 %reduce-scatter.11.cloned.1.call-start = ((), (), s32[]{:S(2)}) async-start(), calls=%async_computation.8 | async-start | bytes 1572864 | tf_op jit(solution)/shard_map/reduce_scatter | solution.py:908
  236.4 113.4 %reduce-scatter.13.cloned.1.call-start = ((), (), s32[]{:S(2)}) async-start(), calls=%async_computation.9 | async-start | bytes 655360 | tf_op jit(solution)/shard_map/reduce_scatter | solution.py:909
  236.7 8.1 %collective-permute-start.23 = (bf16[256,512]{1,0:T(8,128)(2,1)S(1)}, bf16[256,512]{1,0:T(8,128)(2,1)S(1)}, u32[]{:S(2)}, u32[]{:S(2)}) collective-permute-start(bf16[256,512]{1,0:T(8,128)(2,1)S(1)} %copy-done.20), channel_id=1, source_target_pairs={{0,1},{1,0},{2,3},{3,2},{4,5},{5,4},{6,7},{7,6},{8,9},{9,8},{10,11... | collective-permute-start | bytes 786440 | tf_op jit(solution)/shard_map/ppermute | solution.py:76
  259.6 8.6 %collective-permute-start.26 = (bf16[256,512]{1,0:T(8,128)(2,1)}, bf16[256,512]{1,0:T(8,128)(2,1)S(1)}, u32[]{:S(2)}, u32[]{:S(2)}) collective-permute-start(bf16[256,512]{1,0:T(8,128)(2,1)} %get-tuple-element.140), channel_id=1, source_target_pairs={{0,4},{4,0},{2,6},{6,2},{1,5},{5,1},{3,7},{7,3},{8,12},{12,8},{10,... | collective-permute-start | bytes 786440 | tf_op jit(solution)/shard_map/ppermute | solution.py:84
  272.0 8.1 %collective-permute-start.28 = (bf16[2,4,256,128]{3,2,1,0:T(8,128)(2,1)}, bf16[2,4,256,128]{3,2,1,0:T(8,128)(2,1)S(1)}, u32[]{:S(2)}, u32[]{:S(2)}) collective-permute-start(bf16[2,4,256,128]{3,2,1,0:T(8,128)(2,1)} %get-tuple-element.155), channel_id=1, source_target_pairs={{0,2},{2,0},{4,6},{6,4},{1,3},{3,1},{5,7},{7,5},{8,10},{10,8},{12,... | collective-permute-start | bytes 1572872 | tf_op jit(solution)/shard_map/ppermute | solution.py:80
  272.0 32.5 %collective-permute-start.27 = (bf16[256,512]{1,0:T(8,128)(2,1)}, bf16[256,512]{1,0:T(8,128)(2,1)S(1)}, u32[]{:S(2)}, u32[]{:S(2)}) collective-permute-start(bf16[256,512]{1,0:T(8,128)(2,1)} %get-tuple-element.144.refs_2_), channel_id=1, source_target_pairs={{0,1},{1,0},{2,3},{3,2},{4,5},{5,4},{6,7},{7,6},{8,9},{9,8},{10,11... | collective-permute-start | bytes 786440 | tf_op jit(solution)/shard_map/ppermute | solution.py:76
  283.0 27.7 %collective-permute-start.29 = (bf16[4,256,128]{2,1,0:T(8,128)(2,1)}, bf16[4,256,128]{2,1,0:T(8,128)(2,1)S(1)}, u32[]{:S(2)}, u32[]{:S(2)}) collective-permute-start(bf16[4,256,128]{2,1,0:T(8,128)(2,1)} %get-tuple-element.157.refs_17_), channel_id=1, source_target_pairs={{0,4},{4,0},{2,6},{6,2},{1,5},{5,1},{3,7},{7,3},{8,12},{12,8},{10,... | collective-permute-start | bytes 786440 | tf_op jit(solution)/shard_map/ppermute | solution.py:84
  317.7 8.3 %collective-permute-start.41 = (f32[40,128]{1,0:T(8,128)S(1)}, f32[40,128]{1,0:T(8,128)S(1)}, u32[]{:S(2)}, u32[]{:S(2)}) collective-permute-start(f32[40,128]{1,0:T(8,128)S(1)} %get-tuple-element.215), channel_id=1, source_target_pairs={{0,8},{8,16},{16,24},{24,0},{1,9},{9,17},{17,25},{25,1},{2,10},{10... | collective-permute-start | bytes 61448 | tf_op jit(solution)/shard_map/ppermute | solution.py:563
  324.5 10.8 %collective-permute-start.31 = (bf16[256,128]{1,0:T(8,128)(2,1)}, bf16[256,128]{1,0:T(8,128)(2,1)S(1)}, u32[]{:S(2)}, u32[]{:S(2)}) collective-permute-start(bf16[256,128]{1,0:T(8,128)(2,1)} %get-tuple-element.161.refs_7_), channel_id=1, source_target_pairs={{0,16},{8,24},{16,0},{24,8},{1,17},{9,25},{17,1},{25,9},{2,18},{10... | collective-permute-start | bytes 196616 | tf_op jit(solution)/shard_map/ppermute | solution.py:563
  326.0 9.3 %collective-permute-start.32 = (bf16[256,128]{1,0:T(8,128)(2,1)}, bf16[256,128]{1,0:T(8,128)(2,1)S(1)}, u32[]{:S(2)}, u32[]{:S(2)}) collective-permute-start(bf16[256,128]{1,0:T(8,128)(2,1)} %get-tuple-element.162.refs_8_), channel_id=1, source_target_pairs={{0,8},{8,16},{16,24},{24,0},{1,9},{9,17},{17,25},{25,1},{2,10},{10... | collective-permute-start | bytes 196616 | tf_op jit(solution)/shard_map/ppermute | solution.py:563
  (73 other events, 388.5 us)
Sparse Core Ops, SparseCore 0:
  28.2 42.5 all-gather.4
  73.1 44.1 all-gather.6
  197.5 12.4 reduce-scatter.6
  212.2 20.3 reduce-scatter.14
  234.6 19.6 reduce-scatter.8
  256.6 19.8 reduce-scatter.16
  278.8 26.8 reduce-scatter.10
  309.8 23.9 reduce-scatter.12
where the time goes:
time: 369 us; the launch traced here: 368 us
  waiting for transfers between devices  150 us (41%)
  Pallas kernels  96.9 us (26%)
  starting transfers between devices  37.8 us (10%)
  blocking collectives  36 us (10%)
  local copies, waits for them, and re-layouts  27 us (7%)
  between operations  17.1 us (5%)
    pallas_call x26, Pallas kernels, run(): return list(call(place, *arrays))  89 us
    ppermute x8, waiting for transfers between devices, swap_x(): return lax.ppermute(values, 'ctx', [(0, 2), (2, 0), (1, 3), (3, 1)])  38.2 us
    ppermute x9, waiting for transfers between devices, swap_tp(): return lax.ppermute(values, 'tp', [(0, 1), (1, 0)])  37.2 us
    all_gather x3, blocking collectives, spread_sum(): return (both, lax.all_gather(mine, 'ctx', axis=0))  36 us
    all_gather x2, waiting for transfers between devices, gather(): full = lax.all_gather(quarter, ('shard', 'ctx'), axis=0)  33.2 us
    reduce_scatter x3, waiting for transfers between devices, spread_sum(): lax.psum_scatter(both, 'ctx', scatter_dimension=0, axis_index_groups=[[0,...  19.6 us
    unnamed x96, local copies, waits for them, and re-layouts  18.1 us
    ppermute x9, starting transfers between devices, shift(): lax.ppermute(values, 'shard', [(z, (z + step) % 4) for z in range(4)])  14.8 us
  transfers between devices with their start and end apart: 50, of which 28 were waited for; matrix products, arithmetic and copies ran while one was open for 3% of the time, Pallas kernels for 16%

commit v1 on v0

--- a/solution.py
+++ b/solution.py
@@ -536,12 +536,12 @@
 def pack(place, kinds, arrays, index, after=(), whole_quarters=True):
     rows = sum(kind_rows[kind] for kind in kinds)
     operands = []
-    for kind, array in zip(kinds, arrays):
+    for kind, array, at in zip(kinds, arrays, index):
         if kind == "small":
             operands.append(array)
         else:
             block = (1,) + array.shape[1:]
-            at = (index,) + (0,) * (array.ndim - 1)
+            at = (at,) + (0,) * (array.ndim - 1)
             operands.append((array, pl.BlockSpec(block, lambda i, at=at: at)))
     if not whole_quarters:
         return run(quarter_pack_kernel(kinds), [((rows, lanes), bf16)], place, operands, after=after)[0]
@@ -710,7 +710,7 @@
 
 
 def mlp_back(grad, pre_ref, low_ref, first, second, place, outs):
-    partial_out, bias_out, b_first_out, keep, send = outs
+    partial_out, bias_out, b_first_out, keep, *sends = outs
     grad_low = grad.astype(bf16)
     bias_out[...] = jnp.sum(grad, axis=0, keepdims=True)
     total = None
@@ -727,15 +727,15 @@
         b_first_out[p ^ place[1]] = jnp.sum(grad_pre_low.astype(f32), axis=0, keepdims=True)
         part = mm_nt(grad_pre_low, first_block(first, p))
         total = part if total is None else total + part
-        to = keep if p % 2 == 0 else send
+        to = keep.at[p // 2] if p % 2 == 0 else sends[p // 2]
         grad_first = mm_tn(low_ref[...], grad_pre_low).astype(bf16)
         grad_second = mm_tn(act, grad_low).astype(bf16)
         for k in range(4):
             for j in range(2):
-                to[p // 2, k, j * 128 : (j + 1) * 128] = grad_first[
+                to[k, j * 128 : (j + 1) * 128] = grad_first[
                     k * 128 : (k + 1) * 128, j * 128 : (j + 1) * 128
                 ]
-            to[p // 2, k, 256:512] = grad_second[:, k * 128 : (k + 1) * 128]
+            to[k, 256:512] = grad_second[:, k * 128 : (k + 1) * 128]
     partial_out[...] = total.astype(bf16)
 
 
@@ -829,17 +829,26 @@
     send_out[...] = (keep[1].astype(f32) + got[1].astype(f32)).astype(bf16)
 
 
-def halve_in_order(place, keep, got, out):
-    z, chip = place[0], place[1] // 2
-    for half in range(2):
-        for k in range(4):
-            total = keep[half, k].astype(f32) + got[half, k].astype(f32)
-            out[half ^ chip, (z - k + 4) % 4] = total.astype(bf16)
+def halve_groups_kernel(place, *refs):
+    own_out, send_out = refs[-2:]
+    start = 0
+    for keep, one, two in zip(refs[:-2:3], refs[1:-2:3], refs[2:-2:3]):
+        rows = keep.shape[2]
+        for half, got, out in ((0, one, own_out), (1, two, send_out)):
+            total = keep[half].astype(f32) + got[...].astype(f32)
+            out[:, start : start + rows] = total.astype(bf16)
+        start += rows
+
+
+def quarter_in_order(place, own, got, out):
+    for k in range(4):
+        total = own[k].astype(f32) + got[k].astype(f32)
+        out[(place[0] - k + 4) % 4] = total.astype(bf16)
 
 
 def query_back_kernel(place, *refs):
     dq, dkv, got, low, w_ref, gw_ref = refs[:6]
-    partial_out, b_out, keep, send, scratch = refs[6:]
+    partial_out, b_out, keep, *sends, scratch = refs[6:]
     c = place[1]
     grad_kv = (dkv[...].astype(f32) + got[...].astype(f32)).astype(bf16)
     grad_qkv = lane_join([dq[...], grad_kv])
@@ -848,80 +857,64 @@
     b_out[1:2] = jnp.sum(grad_kv[:, 256:].astype(f32), axis=0, keepdims=True)
     scratch[...] = mm_tn(low[...], grad_qkv).astype(bf16).reshape(4, 4, 32, 768)
     for p in range(4):
-        to = keep if p % 2 == 0 else send
+        to = keep.at[p // 2] if p % 2 == 0 else sends[p // 2]
         for k in range(4):
             for tile in range(6):
-                to[p // 2, k, tile * 32 : (tile + 1) * 32] = scratch[
+                to[k, tile * 32 : (tile + 1) * 32] = scratch[
                     k, p ^ c, :, tile * 128 : (tile + 1) * 128
                 ]
-            to[p // 2, k, 192:256] = gw_ref[p ^ c, :, k * 128 : (k + 1) * 128]
-
-
-def four_kernel(place, one, two, three, four, out):
-    out[...] = (one[...] + two[...]) + (three[...] + four[...])
-
-
-def quarter_kernel(place, own, got, *outs):
+            to[k, 192:256] = gw_ref[p ^ c, :, k * 128 : (k + 1) * 128]
+
+
+def last_quarter_kernel(place, own, got, sums, one, two, three, *outs):
     for k in range(4):
-        outs[k][...] = (own[k].astype(f32) + got[k].astype(f32)).astype(bf16)
-
-
-def total_kernel(place, own, one, two, three, out):
+        outs[k][:256] = (own[k].astype(f32) + got[k].astype(f32)).astype(bf16)
+        total = (sums[k] + one[k]) + (two[k] + three[k])
+        outs[k][256:] = total.astype(bf16)
+
+
+def last_total_kernel(place, own, one, two, three, out, small_out):
     total = own[...].astype(f32) + one[...].astype(f32)
-    out[...] = (total + (two[...].astype(f32) + three[...].astype(f32))).astype(bf16)
-
-
-class Chain:
-    def __init__(self, place, keep, send):
-        self.place, self.rows = place, keep.shape[2]
-        self.state = [keep, send]
-
-    def halve(self, after=()):
-        keep, send = self.state
-        self.state = run(
-            halve_kernel, [((4, self.rows, lanes), bf16)] * 2, self.place, [keep, swap_core(send)], flops=2**20, after=after
-        )
-
-    def quarter(self, after=()):
-        own, send = self.state
-        self.state = run(
-            quarter_kernel, [((self.rows, lanes), bf16)] * 4, self.place, [own, swap_x(send)], flops=2**20, after=after
-        )
-
-    def total(self, after=()):
-        got = [shift(self.state[k], 4 - k) for k in (1, 2, 3)]
-        self.state = run(
-            total_kernel, [((self.rows, lanes), bf16)], self.place, [self.state[0]] + got, flops=2**20, after=after
-        )
-
-    def collect(self):
-        (total,) = self.state
-        chip = swap_x(total)
-        return [total, swap_core(total), chip, swap_core(chip)]
-
-
-def spread_sum(place, keep, send, after=()):
-    rows = keep.shape[2]
-    (both,) = run(
-        halve_in_order, [((2, 4, rows, lanes), bf16)], place, [keep, swap_core(send)], after=after
-    )
-    mine = lax.psum_scatter(both, "ctx", scatter_dimension=0, axis_index_groups=[[0, 2], [1, 3]])
-    mine = lax.psum_scatter(mine, "shard", scatter_dimension=0)
-    return both, lax.all_gather(mine, "ctx", axis=0)
-
-
-def fill(place, refs, scratch):
+    total = total + (two[...].astype(f32) + three[...].astype(f32))
+    out[...] = total[:256].astype(bf16)
+    small_out[...] = total[256:]
+
+
+def halve(place, groups, after=()):
+    operands = []
+    for keep, one, two in groups:
+        operands += [keep, swap_core(one), swap_core(two)]
+    rows = sum(group[0].shape[2] for group in groups)
+    return run(halve_groups_kernel, [((4, rows, lanes), bf16)] * 2, place, operands, after=after)
+
+
+def quarter(place, own, send, after=()):
+    (both,) = run(quarter_in_order, [(own.shape, bf16)], place, [own, swap_x(send)], after=after)
+    return both
+
+
+def copy_kernel(place, source, out):
+    out[...] = source[...]
+
+
+def hand_on(place, array, after):
+    return run(copy_kernel, [(array.shape, bf16)], place, [array], after=after)[0]
+
+
+def collect(total):
+    chip = swap_x(total)
+    return [total, swap_core(total), chip, swap_core(chip)]
+
+
+def fill(refs, scratch):
     for p in range(4):
-        if len(refs) == 1:
-            scratch[p ^ place[1]] = refs[0][p].astype(f32)
-        else:
-            scratch[p] = refs[p][...].astype(f32)
+        scratch[p] = refs[p][...].astype(f32)
 
 
 def hidden_out_kernel(place, *refs):
     c = place[1]
     first_out, second_out, scratch = refs[-3:]
-    fill(place, refs[:-3], scratch)
+    fill(refs, scratch)
     for q in range(4):
         for j in range(2):
             column = (2 * q + j) * 128
@@ -932,7 +925,7 @@
 def heads_out_kernel(place, *refs):
     c = place[1]
     qkv_out, proj_out, scratch = refs[-3:]
-    fill(place, refs[:-3], scratch)
+    fill(refs, scratch)
     for q in range(4):
         for tile in range(6):
             column = (tile % 2) * 128
@@ -942,8 +935,7 @@
         proj_out[0, q * 64 : (q + 1) * 64] = scratch[q ^ c, 192:]
 
 
-def layer_out(kernel, place, totals, layer, shapes, before, after):
-    rows = totals[0].shape[-2]
+def layer_out(kernel, rows, place, totals, layer, shapes, before, start, after):
     extra = list(before) + list(after)
     count = 1 + len(totals)
 
@@ -960,7 +952,7 @@
             grid=(1,),
             out_shape=[jax.ShapeDtypeStruct(shape, f32) for shape in shapes],
             in_specs=[pl.BlockSpec(memory_space=pltpu.SMEM)]
-            + [whole(total) for total in totals]
+            + [pl.BlockSpec((rows, lanes), lambda i: (start // rows, 0))] * 4
             + [pl.BlockSpec(memory_space=pl.ANY)] * len(extra),
             out_specs=[block(shape) for shape in shapes],
             scratch_shapes=[pltpu.VMEM((4, rows, lanes), f32)],
@@ -971,12 +963,14 @@
     )
 
 
-def hidden_out(place, totals, layer, shape_one, shape_two, before, after=()):
-    return layer_out(hidden_out_kernel, place, totals, layer, (shape_one, shape_two), before, after)
-
-
-def heads_out(place, totals, layer, shape_one, shape_two, before, after=()):
-    return layer_out(heads_out_kernel, place, totals, layer, (shape_one, shape_two), before, after)
+def hidden_out(place, totals, layer, shape_one, shape_two, before, start, after=()):
+    shapes = (shape_one, shape_two)
+    return layer_out(hidden_out_kernel, 512, place, totals, layer, shapes, before, start, after)
+
+
+def heads_out(place, totals, layer, shape_one, shape_two, before, start, after=()):
+    shapes = (shape_one, shape_two)
+    return layer_out(heads_out_kernel, 256, place, totals, layer, shapes, before, start, after)
 
 
 def last_kernel(place, *refs):
@@ -1008,7 +1002,7 @@
                 for j in range(2):
                     row = 20 + 8 * layer + 2 * q + j
                     out[k, row : row + 1] = b_first[layer][q, :, j * 128 : (j + 1) * 128]
-    out[:, 36:] = jnp.zeros((4, 4, lanes), f32)
+    out[:, 36:] = jnp.zeros((4, 12, lanes), f32)
 
 
 def turn(values, place_z, back):
@@ -1026,26 +1020,24 @@
     flat = jnp.concatenate([array.reshape(-1) for array in (gains, biases, b_qv, b_fc1)])
     small = jnp.pad(flat, (0, 32 * lanes - flat.shape[0])).reshape(32, lanes)
 
-    local_a, send_a = pack(place, ("qkv", "proj", "small"), (w_qkv, w_proj, small), 0)
+    kinds = ("qkv", "proj", "first", "second", "first", "second")
+    send = pack(
+        place, kinds, (w_qkv, w_proj, w_fc1, w_fc2, w_fc1, w_fc2), (1, 1, 0, 0, 1, 1), whole_quarters=False
+    )
+    full = gather(send)
+    local_a, send_a = pack(place, ("qkv", "proj", "small"), (w_qkv, w_proj, small), (0, 0, 0))
     pair_own = turn(jnp.concatenate([x_in[:, 0], cotangent[:, 0]]), z, False)
     pair_peer = swap_tp(pair_own)
     got_a = far_chunks(send_a)
     far_a = stack(place, got_a)
     chip_a = swap_x(far_a)
     group_a0 = [local_a, far_a, swap_core(far_a), chip_a, swap_core(chip_a)]
-    send_b = pack(place, ("first", "second"), (w_fc1, w_fc2), 0, after=[far_a], whole_quarters=False)
-    kinds = ("first", "second", "proj", "qkv")
-    send_1 = pack(
-        place, kinds, (w_fc1, w_fc2, w_proj, w_qkv), 1, after=[far_a, send_b], whole_quarters=False
-    )
-    full_b, full_1 = gather(send_b), gather(send_1)
-
     small_parts = small_of(group_a0)
     parts = {
-        "qkv": [pieces_of(group_a0, 192, 0), gathered_rows(full_1, 192, 576)],
-        "proj": [pieces_of(group_a0, 64, 192), gathered_rows(full_1, 64, 512)],
-        "first": [gathered_rows(full_b, 256, 0), gathered_rows(full_1, 256, 0)],
-        "second": [gathered_rows(full_b, 256, 256), gathered_rows(full_1, 256, 256)],
+        "qkv": [pieces_of(group_a0, 192, 0), gathered_rows(full, 192, 0)],
+        "proj": [pieces_of(group_a0, 64, 192), gathered_rows(full, 64, 192)],
+        "first": [gathered_rows(full, 256, 256), gathered_rows(full, 256, 768)],
+        "second": [gathered_rows(full, 256, 512), gathered_rows(full, 256, 1024)],
     }
     square, wide = (256, 512), (256, 256)
     saved = []
@@ -1087,7 +1079,8 @@
         ((1, 512), f32),
         ((4, 1, 256), f32),
         ((2, 4, 512, lanes), bf16),
-        ((2, 4, 512, lanes), bf16),
+        ((4, 512, lanes), bf16),
+        ((4, 512, lanes), bf16),
     ]
     sums_mid, bias_mlp, b_query, b_first = [0, 0], [0, 0], [0, 0], [0, 0]
     hidden = [None, None]
@@ -1096,19 +1089,26 @@
         tail = [pre, low_mid] + parts["first"][layer] + parts["second"][layer]
         if layer == 1:
             grad_state = g_all
-            partial, bias_mlp[1], b_first[1], keep, send = run(
+            partial, bias_mlp[1], b_first[1], *grads = run(
                 top_kernel, hidden_outs, place, [grad_state] + tail
             )
         else:
-            half, heads_total = spread_sum(place, keep, send)
-            grad_state, sums_in, partial, bias_mlp[0], b_first[0], keep, send = run(
+            own, far = halve(place, [first_grads, grads])
+            grad_state, sums_in, partial, bias_mlp[0], b_first[0], *grads = run(
                 lower_kernel(0),
                 [(square, f32), ((2, 512), f32)] + hidden_outs,
                 place,
                 [grad_mid, partial, swap_tp(partial), saved[1][0]] + small_parts + tail,
-                after=[half],
+                after=[own],
             )
-        half, hidden[layer] = spread_sum(place, keep, send)
+            both = quarter(place, own, far, after=[partial])
+            upper = lax.psum_scatter(both, "shard", scatter_dimension=0)
+        behind = []
+        if layer == 1:
+            first_grads = grads
+        else:
+            own, far = halve(place, [grads])
+            behind = [both, own]
         grad_mid, sums_mid[layer], gw_out, dq, keep, send = run(
             attend_back_kernel(layer),
             [
@@ -1121,27 +1121,31 @@
             ],
             place,
             [partial, swap_tp(partial), middle, grad_state] + small_parts + [attn, w_out, q] + chunks + [lse],
-            after=[half],
-        )
-        dkv, chip = run(halve_kernel, [(square, bf16)] * 2, place, [keep, swap_core(send)])
-        partial, b_query[layer], keep, send = run(
+            after=behind,
+        )
+        if layer == 0:
+            both = quarter(place, own, far, after=[keep])
+            lower = lax.psum_scatter(both, "shard", scatter_dimension=0)
+            behind = [both]
+        dkv, chip = run(halve_kernel, [(square, bf16)] * 2, place, [keep, swap_core(send)], after=behind)
+        partial, b_query[layer], *grads = run(
             query_back_kernel,
             [
                 (square, bf16),
                 ((2, 256), f32),
                 ((2, 4, 256, lanes), bf16),
-                ((2, 4, 256, lanes), bf16),
+                ((4, 256, lanes), bf16),
+                ((4, 256, lanes), bf16),
             ],
             place,
             [dq, dkv, swap_x(chip), low_in, w_all, gw_out],
             scratch=[pltpu.VMEM((4, 4, 32, 768), bf16)],
             after=[output] if layer == 1 else [],
         )
-    last = Chain(place, keep, send)
-    last.halve()
+    own, far = halve(place, [grads])
     grad_x, sums = run(
         last_kernel,
-        [((128, 512), f32), ((4, 40, lanes), f32)],
+        [((128, 512), f32), ((4, 48, lanes), f32)],
         place,
         [grad_mid, partial, swap_tp(partial), saved[0][0]]
         + small_parts
@@ -1150,25 +1154,23 @@
         + bias_mlp
         + b_query
         + b_first,
-        after=last.state,
-    )
-    last.quarter(after=[grad_x])
+        after=[own],
+    )
+    pieces = run(
+        last_quarter_kernel,
+        [((304, lanes), bf16)] * 4,
+        place,
+        [own, swap_x(far), sums, swap_core(sums), swap_x(sums), swap_both(sums)],
+    )
     grad_x = turn(grad_x, z, True)[:, None]
-    (sums,) = run(
-        four_kernel,
-        [((4, 40, lanes), f32)],
-        place,
-        [sums, swap_core(sums), swap_x(sums), swap_both(sums)],
-        after=last.state,
-    )
-    last.total(after=[sums])
-    outs_heads = heads_out(
-        place, [heads_total], 1, w_qkv.shape, w_proj.shape, [], after=last.state
-    )
-    outs_hidden = hidden_out(place, [hidden[1]], 1, w_fc1.shape, w_fc2.shape, [], after=last.state)
-    grad_fc1, grad_fc2 = hidden_out(place, [hidden[0]], 0, w_fc1.shape, w_fc2.shape, outs_hidden)
-    got = [shift(sums[k], 4 - k) for k in (1, 2, 3)]
-    total = sums[0] + got[0] + got[1] + got[2]
+    got = [shift(pieces[k], 4 - k) for k in (1, 2, 3)]
+    last, total = run(
+        last_total_kernel, [((256, lanes), bf16), ((48, lanes), f32)], place, [pieces[0]] + got
+    )
+    upper_parts, lower_parts = collect(upper), collect(hand_on(place, lower, [last]))
+    outs_heads = heads_out(place, upper_parts, 1, w_qkv.shape, w_proj.shape, [], 512, after=[last])
+    outs_hidden = hidden_out(place, upper_parts, 1, w_fc1.shape, w_fc2.shape, [], 0, after=[last])
+    grad_fc1, grad_fc2 = hidden_out(place, lower_parts, 0, w_fc1.shape, w_fc2.shape, outs_hidden, 0)
     grad_gains = total[:4].reshape(gains.shape)
     grad_biases = total[4:12].reshape(biases.shape)
     rest_q = total[12:20].reshape(2, 2, 4, 64)
@@ -1176,7 +1178,7 @@
     grad_b_qv = lax.dynamic_slice_in_dim(rest_q, z * 16, 16, 3)
     grad_b_fc1 = lax.dynamic_slice_in_dim(rest_f, z * 16, 16, 2)
 
-    grad_qkv, grad_proj = heads_out(place, last.collect(), 0, w_qkv.shape, w_proj.shape, outs_heads)
+    grad_qkv, grad_proj = heads_out(place, collect(last), 0, w_qkv.shape, w_proj.shape, outs_heads, 0)
     return (
         output, grad_x, grad_qkv, grad_b_qv, grad_proj, grad_fc1, grad_b_fc1, grad_fc2, grad_gains, grad_biases
     )

time: 369 us -> 306 us (0.83)
  blocking collectives: 36 us -> 0 us
  waiting for transfers between devices: 150 us -> 120 us
    all_gather x3 -> x0, blocking collectives: 36 us -> none  [spread_sum(): return (both, lax.all_gather(mine, 'ctx', axis=0))]
    all_gather x2 -> x1, waiting for transfers between devices: 33.2 us -> 5.82 us  [gather(): full = lax.all_gather(quarter, ('shard', 'ctx'), axis=0)]
    ppermute x8 -> x12, waiting for transfers between devices: 38.2 us -> 58 us  [swap_x(): return lax.ppermute(values, 'ctx', [(0, 2), (2, 0), (1, 3), (3, 1)])]
    reduce_scatter x6 -> x2, waiting for transfers between devices: 19.6 us -> 0.01 us  [the longest x1 0.01 us: body_four(): lower = lax.psum_scatter(both, 'shard', scatter_dimension=0)]
    ppermute x9 -> x6, starting transfers between devices: 14.8 us -> 11.6 us  [shift(): lax.ppermute(values, 'shard', [(z, (z + step) % 4) for z in range(4)])]
    ppermute x9 -> x6, waiting for transfers between devices: 10.7 us -> 8.44 us  [shift(): lax.ppermute(values, 'shard', [(z, (z + step) % 4) for z in range(4)])]
    ppermute x8 -> x12, starting transfers between devices: 9.1 us -> 10.5 us  [swap_x(): return lax.ppermute(values, 'ctx', [(0, 2), (2, 0), (1, 3), (3, 1)])]
    unnamed x96 -> x112, local copies, waits for them, and re-layouts: 18.1 us -> 19 us
  transfers between devices with their start and end apart: 50 -> 54, of which waited for: 28 -> 30; matrix products, arithmetic and copies ran while one was open for 3% -> 4% of each run, Pallas kernels for 16% -> 18%
where the time goes in v1:
time: 306 us; the launch traced here: 304 us
  waiting for transfers between devices  120 us (39%)
  Pallas kernels  98.8 us (32%)
  starting transfers between devices  37.2 us (12%)
  local copies, waits for them, and re-layouts  29.2 us (10%)
  between operations  16.8 us (5%)
    pallas_call x26, Pallas kernels, run(): return list(call(place, *arrays))  90.7 us
    ppermute x12, waiting for transfers between devices, swap_x(): return lax.ppermute(values, 'ctx', [(0, 2), (2, 0), (1, 3), (3, 1)])  58 us
    ppermute x9, waiting for transfers between devices, swap_tp(): return lax.ppermute(values, 'tp', [(0, 1), (1, 0)])  36.5 us
    unnamed x112, local copies, waits for them, and re-layouts  19 us
    ppermute x6, starting transfers between devices, shift(): lax.ppermute(values, 'shard', [(z, (z + step) % 4) for z in range(4)])  11.6 us
    ppermute x9, starting transfers between devices, swap_tp(): return lax.ppermute(values, 'tp', [(0, 1), (1, 0)])  10.8 us
    ppermute x12, starting transfers between devices, swap_x(): return lax.ppermute(values, 'ctx', [(0, 2), (2, 0), (1, 3), (3, 1)])  10.5 us
    ppermute x23, waiting for transfers between devices, swap_core(): return lax.ppermute(values, 'ctx', [(0, 1), (1, 0), (2, 3), (3, 2)])  8.89 us
  transfers between devices with their start and end apart: 54, of which 30 were waited for; matrix products, arithmetic and copies ran while one was open for 4% of the time, Pallas kernels for 18%

profile of v1, /device:TPU:0, one launch (start us, length us, event | category | flops | bytes accessed | tf_op | source)
XLA Modules:
  0.0 304.4 jit_solution(6228538917375298823)
XLA Ops:
  43.2 12.1 %collective-permute-done.8.refs_4_.refs_12_ = bf16[256,512]{1,0:T(8,128)(2,1)S(1)} collective-permute-done((bf16[256,512]{1,0:T(8,128)(2,1)}, bf16[256,512]{1,0:T(8,128)(2,1)S(1)}, u32[]{:S(2)}, u32[]{:S(2)}) %collective-permute-start.8) | collective-permute-done | bytes 262176 | tf_op jit(solution)/shard_map/ppermute | solution.py:84
  57.5 4.8 %shard_map.180 = (bf16[256,256]{1,0:T(8,128)(2,1)}, f32[256,128]{1,0:T(8,128)}, bf16[256,512]{1,0:T(8,128)(2,1)}, bf16[4,64,512]{2,1,0:T(8,128)(2,1)}) custom-call(s32[3]{0:T(128)} %pad_add_fusion.refs_0_, bf16[256,256]{1,0:T(8,128)(2,1)} %get-tuple-element.104.refs_1_.refs_9_, bf16[256,512]{1,0:T(8,128)(2,1)} %get-tuple-element.105.refs_2_.refs_10_, ...), custom_call_target="tpu_custom_call" | custom-call | flops 1048576 | bytes 1024 | tf_op jit(solution)/shard_map/pallas_call | solution.py:405
  63.8 7.1 %collective-permute-done.10.refs_3_ = bf16[256,512]{1,0:T(8,128)(2,1)S(1)} collective-permute-done((bf16[256,512]{1,0:T(8,128)(2,1)}, bf16[256,512]{1,0:T(8,128)(2,1)S(1)}, u32[]{:S(2)}, u32[]{:S(2)}) %collective-permute-start.10) | collective-permute-done | bytes 262176 | tf_op jit(solution)/shard_map/ppermute | solution.py:76
  70.9 5.8 %all-gather.3.cloned.1.call-done = bf16[20480,128]{1,0:T(8,128)(2,1)} async-done(((bf16[1280,128]{1,0:T(8,128)(2,1)}), bf16[20480,128]{1,0:T(8,128)(2,1)}) %all-gather.3.cloned.1.call-update) | async-done | bytes 5242896 | tf_op jit(solution)/shard_map/all_gather | solution.py:554
  76.7 4.3 %shard_map.182 = (f32[256,512]{1,0:T(8,128)}, bf16[256,512]{1,0:T(8,128)(2,1)}, f32[256,1024]{1,0:T(8,128)}, bf16[256,512]{1,0:T(8,128)(2,1)}) custom-call(s32[3]{0:T(128)} %pad_add_fusion.refs_0_, f32[256,512]{1,0:T(8,128)} %get-tuple-element.103.refs_1_.refs_4_, bf16[256,512]{1,0:T(8,128)(2,1)} %get-tuple-element.106.refs_2_, bf16[256,512]{1,0:T(8,128)(2,1)} %copy-done.37, ...), custom_call_target="tpu_custom_call" | custom-call | flops 1048576 | bytes 1024 | tf_op jit(solution)/shard_map/pallas_call | solution.py:405
  82.4 7.2 %collective-permute-done.11.refs_3_ = bf16[256,512]{1,0:T(8,128)(2,1)S(1)} collective-permute-done((bf16[256,512]{1,0:T(8,128)(2,1)}, bf16[256,512]{1,0:T(8,128)(2,1)S(1)}, u32[]{:S(2)}, u32[]{:S(2)}) %collective-permute-start.11) | collective-permute-done | bytes 262176 | tf_op jit(solution)/shard_map/ppermute | solution.py:76
  90.4 3.2 %shard_map.183 = (f32[256,512]{1,0:T(8,128)}, bf16[256,512]{1,0:T(8,128)(2,1)}, bf16[256,256]{1,0:T(8,128)(2,1)}, bf16[256,512]{1,0:T(8,128)(2,1)}, bf16[4,4,32,768]{3,2,1,0:T(8,128)(2,1)}) custom-call(s32[3]{0:T(128)} %pad_add_fusion.refs_0_, f32[256,512]{1,0:T(8,128)} %get-tuple-element.107.refs_1_.refs_3_, bf16[256,512]{1,0:T(8,128)(2,1)} %get-tuple-element.108.refs_2_, ...), custom_call_target="tpu_custom_call" | custom-call | flops 1048576 | bytes 1024 | tf_op jit(solution)/shard_map/pallas_call | solution.py:405
  94.4 7.1 %collective-permute-done.13.refs_4_.refs_12_ = bf16[256,512]{1,0:T(8,128)(2,1)S(1)} collective-permute-done((bf16[256,512]{1,0:T(8,128)(2,1)}, bf16[256,512]{1,0:T(8,128)(2,1)S(1)}, u32[]{:S(2)}, u32[]{:S(2)}) %collective-permute-start.13) | collective-permute-done | bytes 262176 | tf_op jit(solution)/shard_map/ppermute | solution.py:84
  103.7 4.9 %shard_map.184 = (bf16[256,256]{1,0:T(8,128)(2,1)}, f32[256,128]{1,0:T(8,128)}, bf16[256,512]{1,0:T(8,128)(2,1)}, bf16[4,64,512]{2,1,0:T(8,128)(2,1)}) custom-call(s32[3]{0:T(128)} %pad_add_fusion.refs_0_, bf16[256,256]{1,0:T(8,128)(2,1)} %get-tuple-element.110.refs_1_.refs_9_, bf16[256,512]{1,0:T(8,128)(2,1)} %get-tuple-element.111.refs_2_.refs_10_, ...), custom_call_target="tpu_custom_call" | custom-call | flops 1048576 | bytes 1024 | tf_op jit(solution)/shard_map/pallas_call | solution.py:405
  110.1 7.1 %collective-permute-done.15.refs_3_ = bf16[256,512]{1,0:T(8,128)(2,1)S(1)} collective-permute-done((bf16[256,512]{1,0:T(8,128)(2,1)}, bf16[256,512]{1,0:T(8,128)(2,1)S(1)}, u32[]{:S(2)}, u32[]{:S(2)}) %collective-permute-start.15) | collective-permute-done | bytes 262176 | tf_op jit(solution)/shard_map/ppermute | solution.py:76
  117.9 4.3 %shard_map.185 = (f32[256,512]{1,0:T(8,128)}, bf16[256,512]{1,0:T(8,128)(2,1)}, f32[256,1024]{1,0:T(8,128)}, bf16[256,512]{1,0:T(8,128)(2,1)}) custom-call(s32[3]{0:T(128)} %pad_add_fusion.refs_0_, f32[256,512]{1,0:T(8,128)} %get-tuple-element.109.refs_1_.refs_4_, bf16[256,512]{1,0:T(8,128)(2,1)} %get-tuple-element.112.refs_2_, bf16[256,512]{1,0:T(8,128)(2,1)} %copy-done.38, ...), custom_call_target="tpu_custom_call" | custom-call | flops 1048576 | bytes 1024 | tf_op jit(solution)/shard_map/pallas_call | solution.py:405
  122.2 5.3 %shard_map.186 = (bf16[256,512]{1,0:T(8,128)(2,1)}, f32[1,512]{1,0:T(1,128)}, f32[4,1,256]{2,1,0:T(1,128)}, bf16[2,4,512,128]{3,2,1,0:T(8,128)(2,1)}, bf16[4,512...) custom-call(s32[3]{0:T(128)} %pad_add_fusion.refs_0_, f32[256,512]{1,0:T(8,128)} %get-tuple-element.115.refs_1_.refs_4_, ...), custom_call_target="tpu_custom_call" | custom-call | flops 1048576 | bytes 1024 | tf_op jit(solution)/shard_map/pallas_call | solution.py:405
  129.0 6.3 %collective-permute-done.17.refs_2_ = bf16[256,512]{1,0:T(8,128)(2,1)S(1)} collective-permute-done((bf16[256,512]{1,0:T(8,128)(2,1)}, bf16[256,512]{1,0:T(8,128)(2,1)S(1)}, u32[]{:S(2)}, u32[]{:S(2)}) %collective-permute-start.17) | collective-permute-done | bytes 262176 | tf_op jit(solution)/shard_map/ppermute | solution.py:76
  136.0 9.2 %shard_map.187 = (f32[256,512]{1,0:T(8,128)}, f32[3,512]{1,0:T(4,128)}, bf16[4,64,512]{2,1,0:T(8,128)(2,1)}, bf16[256,256]{1,0:T(8,128)(2,1)}, bf16[2,256,512]{2...) custom-call(s32[3]{0:T(128)} %pad_add_fusion.refs_0_, bf16[256,512]{1,0:T(8,128)(2,1)} %get-tuple-element.118.refs_1_, ...), custom_call_target="tpu_custom_call" | custom-call | flops 1048576 | bytes 1024 | tf_op jit(solution)/shard_map/pallas_call | solution.py:405
  153.4 6.8 %collective-permute-done.19.refs_3_ = bf16[256,512]{1,0:T(8,128)(2,1)S(1)} collective-permute-done((bf16[256,512]{1,0:T(8,128)(2,1)}, bf16[256,512]{1,0:T(8,128)(2,1)S(1)}, u32[]{:S(2)}, u32[]{:S(2)}) %collective-permute-start.19) | collective-permute-done | bytes 262176 | tf_op jit(solution)/shard_map/ppermute | solution.py:84
  166.8 3.3 %shard_map.190 = (bf16[4,768,128]{2,1,0:T(8,128)(2,1)}, bf16[4,768,128]{2,1,0:T(8,128)(2,1)}) custom-call(s32[3]{0:T(128)} %pad_add_fusion.refs_0_, bf16[2,4,512,128]{3,2,1,0:T(8,128)(2,1)} %get-tuple-element.134.refs_1_, bf16[4,512,128]{2,1,0:T(8,128)(2,1)} %copy-done.21, bf16[4,512,128]{2,1,0:T(8,128)(2,1)} %copy-done.22, ...), custom_call_target="tpu_custom_call" | custom-call | flops 1048576 | bytes 1024 | tf_op jit(solution)/shard_map/pallas_call | solution.py:405
  173.7 6.0 %shard_map.191 = (f32[256,512]{1,0:T(8,128)}, f32[2,512]{1,0:T(2,128)}, bf16[256,512]{1,0:T(8,128)(2,1)}, f32[1,512]{1,0:T(1,128)}, f32[4,1,256]{2,1,0:T(1,128)}...) custom-call(s32[3]{0:T(128)} %pad_add_fusion.refs_0_, ...), custom_call_target="tpu_custom_call" | custom-call | flops 1048576 | bytes 1024 | tf_op jit(solution)/shard_map/pallas_call | solution.py:405
  187.5 13.2 %collective-permute-done.26.refs_2_ = bf16[4,768,128]{2,1,0:T(8,128)(2,1)S(1)} collective-permute-done((bf16[4,768,128]{2,1,0:T(8,128)(2,1)S(1)}, bf16[4,768,128]{2,1,0:T(8,128)(2,1)S(1)}, u32[]{:S(2)}, u32[]{:S(2)}) %collective-permute-start.26) | collective-permute-done | bytes 786464 | tf_op jit(solution)/shard_map/ppermute | solution.py:84
  204.7 9.4 %shard_map.194 = (f32[256,512]{1,0:T(8,128)}, f32[3,512]{1,0:T(4,128)}, bf16[4,64,512]{2,1,0:T(8,128)(2,1)}, bf16[256,256]{1,0:T(8,128)(2,1)}, bf16[2,256,512]{2...) custom-call(s32[3]{0:T(128)} %pad_add_fusion.refs_0_, bf16[256,512]{1,0:T(8,128)(2,1)} %get-tuple-element.141.refs_3_.refs_1_, ...), custom_call_target="tpu_custom_call" | custom-call | flops 1048576 | bytes 1024 | tf_op jit(solution)/shard_map/pallas_call | solution.py:405
  223.7 7.8 %collective-permute-done.31.refs_3_ = bf16[256,512]{1,0:T(8,128)(2,1)S(1)} collective-permute-done((bf16[256,512]{1,0:T(8,128)(2,1)}, bf16[256,512]{1,0:T(8,128)(2,1)S(1)}, u32[]{:S(2)}, u32[]{:S(2)}) %collective-permute-start.31) | collective-permute-done | bytes 262176 | tf_op jit(solution)/shard_map/ppermute | solution.py:84
  232.2 3.2 %shard_map.197 = (bf16[256,512]{1,0:T(8,128)(2,1)}, f32[2,256]{1,0:T(2,128)}, bf16[2,4,256,128]{3,2,1,0:T(8,128)(2,1)}, bf16[4,256,128]{2,1,0:T(8,128)(2,1)}, bf16[4,256,128]{2,1,0:T(8,128)(2,1)}) custom-call(s32[3]{0:T(128)} %pad_add_fusion.refs_0_, bf16[256,256]{1,0:T(8,128)(2,1)} %get-tuple-element.152.refs_1_, ...), custom_call_target="tpu_custom_call" | custom-call | flops 1048576 | bytes 1024 | tf_op jit(solution)/shard_map/pallas_call | solution.py:405
  241.0 3.3 %collective-permute-done.32.refs_3_ = bf16[256,512]{1,0:T(8,128)(2,1)S(1)} collective-permute-done((bf16[256,512]{1,0:T(8,128)(2,1)}, bf16[256,512]{1,0:T(8,128)(2,1)S(1)}, u32[]{:S(2)}, u32[]{:S(2)}) %collective-permute-start.32) | collective-permute-done | bytes 262176 | tf_op jit(solution)/shard_map/ppermute | solution.py:76
  263.5 6.2 %collective-permute-done.40.refs_3_ = bf16[304,128]{1,0:T(8,128)(2,1)S(1)} collective-permute-done((bf16[304,128]{1,0:T(8,128)(2,1)}, bf16[304,128]{1,0:T(8,128)(2,1)S(1)}, u32[]{:S(2)}, u32[]{:S(2)}) %collective-permute-start.40) | collective-permute-done | bytes 77856 | tf_op jit(solution)/shard_map/ppermute | solution.py:563
  280.6 3.8 %collective-permute-done.46.refs_3_ = bf16[768,128]{1,0:T(8,128)(2,1)S(1)} collective-permute-done((bf16[768,128]{1,0:T(8,128)(2,1)}, bf16[768,128]{1,0:T(8,128)(2,1)S(1)}, u32[]{:S(2)}, u32[]{:S(2)}) %collective-permute-start.46) | collective-permute-done | bytes 196640 | tf_op jit(solution)/shard_map/ppermute | solution.py:84
  (254 shorter events, 136.0 us)
Async XLA Ops:
  7.2 69.5 %all-gather.3.cloned.1.call-start = ((), (), s32[]{:S(2)}) async-start(), calls=%async_computation.4 | async-start | bytes 5570560 | tf_op jit(solution)/shard_map/all_gather | solution.py:554
  10.0 262.6 %reduce-scatter.5.cloned.1.call-start = ((), (), s32[]{:S(2)}) async-start(), calls=%async_computation.3 | async-start | bytes 655360 | tf_op jit(solution)/shard_map/reduce_scatter | solution.py:1128
  14.6 10.2 %collective-permute-start.1 = (bf16[288,128]{1,0:T(8,128)(2,1)}, bf16[288,128]{1,0:T(8,128)(2,1)S(1)}, u32[]{:S(2)}, u32[]{:S(2)}) collective-permute-start(bf16[288,128]{1,0:T(8,128)(2,1)} %get-tuple-element.102), channel_id=1, source_target_pairs={{0,8},{8,16},{16,24},{24,0},{1,9},{9,17},{17,25},{25,1},{2,10},{10... | collective-permute-start | bytes 221192 | tf_op jit(solution)/shard_map/ppermute | solution.py:563
  42.5 12.8 %collective-permute-start.8 = (bf16[256,512]{1,0:T(8,128)(2,1)}, bf16[256,512]{1,0:T(8,128)(2,1)S(1)}, u32[]{:S(2)}, u32[]{:S(2)}) collective-permute-start(bf16[256,512]{1,0:T(8,128)(2,1)} %get-tuple-element.105.refs_2_.refs_10_), channel_id=1, source_target_pairs={{0,4},{4,0},{2,6},{6,2},{1,5},{5,1},{3,7},{7,3},{8,12},{12,8},{10,... | collective-permute-start | bytes 786440 | tf_op jit(solution)/shard_map/ppermute | solution.py:84
  43.2 12.1 %collective-permute-start.7 = (bf16[256,512]{1,0:T(8,128)(2,1)}, bf16[256,512]{1,0:T(8,128)(2,1)S(1)}, u32[]{:S(2)}, u32[]{:S(2)}) collective-permute-start(bf16[256,512]{1,0:T(8,128)(2,1)} %get-tuple-element.105.refs_2_.refs_10_), channel_id=1, source_target_pairs={{0,2},{2,0},{4,6},{6,4},{1,3},{3,1},{5,7},{7,5},{8,10},{10,8},{12,... | collective-permute-start | bytes 786440 | tf_op jit(solution)/shard_map/ppermute | solution.py:80
  62.3 8.6 %collective-permute-start.10 = (bf16[256,512]{1,0:T(8,128)(2,1)}, bf16[256,512]{1,0:T(8,128)(2,1)S(1)}, u32[]{:S(2)}, u32[]{:S(2)}) collective-permute-start(bf16[256,512]{1,0:T(8,128)(2,1)} %get-tuple-element.106.refs_2_), channel_id=1, source_target_pairs={{0,1},{1,0},{2,3},{3,2},{4,5},{5,4},{6,7},{7,6},{8,9},{9,8},{10,11... | collective-permute-start | bytes 786440 | tf_op jit(solution)/shard_map/ppermute | solution.py:76
  81.0 8.7 %collective-permute-start.11 = (bf16[256,512]{1,0:T(8,128)(2,1)}, bf16[256,512]{1,0:T(8,128)(2,1)S(1)}, u32[]{:S(2)}, u32[]{:S(2)}) collective-permute-start(bf16[256,512]{1,0:T(8,128)(2,1)} %get-tuple-element.108.refs_2_), channel_id=1, source_target_pairs={{0,1},{1,0},{2,3},{3,2},{4,5},{5,4},{6,7},{7,6},{8,9},{9,8},{10,11... | collective-permute-start | bytes 786440 | tf_op jit(solution)/shard_map/ppermute | solution.py:76
  108.6 8.6 %collective-permute-start.15 = (bf16[256,512]{1,0:T(8,128)(2,1)}, bf16[256,512]{1,0:T(8,128)(2,1)S(1)}, u32[]{:S(2)}, u32[]{:S(2)}) collective-permute-start(bf16[256,512]{1,0:T(8,128)(2,1)} %get-tuple-element.112.refs_2_), channel_id=1, source_target_pairs={{0,1},{1,0},{2,3},{3,2},{4,5},{5,4},{6,7},{7,6},{8,9},{9,8},{10,11... | collective-permute-start | bytes 786440 | tf_op jit(solution)/shard_map/ppermute | solution.py:76
  148.1 16.9 %collective-permute-start.21 = (bf16[4,512,128]{2,1,0:T(8,128)(2,1)}, bf16[4,512,128]{2,1,0:T(8,128)(2,1)S(1)}, u32[]{:S(2)}, u32[]{:S(2)}) collective-permute-start(bf16[4,512,128]{2,1,0:T(8,128)(2,1)} %get-tuple-element.135), channel_id=1, source_target_pairs={{0,2},{2,0},{4,6},{6,4},{1,3},{3,1},{5,7},{7,5},{8,10},{10,8},{12,... | collective-permute-start | bytes 1572872 | tf_op jit(solution)/shard_map/ppermute | solution.py:80
  148.4 16.7 %collective-permute-start.22 = (bf16[4,512,128]{2,1,0:T(8,128)(2,1)}, bf16[4,512,128]{2,1,0:T(8,128)(2,1)S(1)}, u32[]{:S(2)}, u32[]{:S(2)}) collective-permute-start(bf16[4,512,128]{2,1,0:T(8,128)(2,1)} %get-tuple-element.136), channel_id=1, source_target_pairs={{0,2},{2,0},{4,6},{6,4},{1,3},{3,1},{5,7},{7,5},{8,10},{10,8},{12,... | collective-permute-start | bytes 1572872 | tf_op jit(solution)/shard_map/ppermute | solution.py:80
  151.6 8.6 %collective-permute-start.19 = (bf16[256,512]{1,0:T(8,128)(2,1)}, bf16[256,512]{1,0:T(8,128)(2,1)S(1)}, u32[]{:S(2)}, u32[]{:S(2)}) collective-permute-start(bf16[256,512]{1,0:T(8,128)(2,1)} %get-tuple-element.127), channel_id=1, source_target_pairs={{0,4},{4,0},{2,6},{6,2},{1,5},{5,1},{3,7},{7,3},{8,12},{12,8},{10,... | collective-permute-start | bytes 786440 | tf_op jit(solution)/shard_map/ppermute | solution.py:84
  164.5 8.4 %collective-permute-start.20 = (bf16[256,512]{1,0:T(8,128)(2,1)}, bf16[256,512]{1,0:T(8,128)(2,1)S(1)}, u32[]{:S(2)}, u32[]{:S(2)}) collective-permute-start(bf16[256,512]{1,0:T(8,128)(2,1)} %get-tuple-element.131.refs_2_), channel_id=1, source_target_pairs={{0,1},{1,0},{2,3},{3,2},{4,5},{5,4},{6,7},{7,6},{8,9},{9,8},{10,11... | collective-permute-start | bytes 786440 | tf_op jit(solution)/shard_map/ppermute | solution.py:76
  180.3 20.4 %collective-permute-start.26 = (bf16[4,768,128]{2,1,0:T(8,128)(2,1)S(1)}, bf16[4,768,128]{2,1,0:T(8,128)(2,1)S(1)}, u32[]{:S(2)}, u32[]{:S(2)}) collective-permute-start(bf16[4,768,128]{2,1,0:T(8,128)(2,1)S(1)} %copy-done.54), channel_id=1, source_target_pairs={{0,4},{4,0},{2,6},{6,2},{1,5},{5,1},{3,7},{7,3},{8,12},{12,8},{10,... | collective-permute-start | bytes 2359304 | tf_op jit(solution)/shard_map/ppermute | solution.py:84
  186.1 28.0 %collective-permute-start.30 = (bf16[4,512,128]{2,1,0:T(8,128)(2,1)}, bf16[4,512,128]{2,1,0:T(8,128)(2,1)S(1)}, u32[]{:S(2)}, u32[]{:S(2)}) collective-permute-start(bf16[4,512,128]{2,1,0:T(8,128)(2,1)} %get-tuple-element.155), channel_id=1, source_target_pairs={{0,4},{4,0},{2,6},{6,2},{1,5},{5,1},{3,7},{7,3},{8,12},{12,8},{10,... | collective-permute-start | bytes 1572872 | tf_op jit(solution)/shard_map/ppermute | solution.py:84
  186.9 17.1 %collective-permute-start.25 = (bf16[256,512]{1,0:T(8,128)(2,1)}, bf16[256,512]{1,0:T(8,128)(2,1)S(1)}, u32[]{:S(2)}, u32[]{:S(2)}) collective-permute-start(bf16[256,512]{1,0:T(8,128)(2,1)} %get-tuple-element.141.refs_3_.refs_1_), channel_id=1, source_target_pairs={{0,1},{1,0},{2,3},{3,2},{4,5},{5,4},{6,7},{7,6},{8,9},{9,8},{10,11... | collective-permute-start | bytes 786440 | tf_op jit(solution)/shard_map/ppermute | solution.py:76
  217.1 58.4 %reduce-scatter.3.cloned.1.call-start = ((), (), s32[]{:S(2)}) async-start(), calls=%async_computation.2 | async-start | bytes 983040 | tf_op jit(solution)/shard_map/reduce_scatter | solution.py:1105
  223.0 8.6 %collective-permute-start.31 = (bf16[256,512]{1,0:T(8,128)(2,1)}, bf16[256,512]{1,0:T(8,128)(2,1)S(1)}, u32[]{:S(2)}, u32[]{:S(2)}) collective-permute-start(bf16[256,512]{1,0:T(8,128)(2,1)} %get-tuple-element.157), channel_id=1, source_target_pairs={{0,4},{4,0},{2,6},{6,2},{1,5},{5,1},{3,7},{7,3},{8,12},{12,8},{10,... | collective-permute-start | bytes 786440 | tf_op jit(solution)/shard_map/ppermute | solution.py:84
  240.3 14.3 %collective-permute-start.35 = (bf16[4,256,128]{2,1,0:T(8,128)(2,1)}, bf16[4,256,128]{2,1,0:T(8,128)(2,1)S(1)}, u32[]{:S(2)}, u32[]{:S(2)}) collective-permute-start(bf16[4,256,128]{2,1,0:T(8,128)(2,1)} %get-tuple-element.176), channel_id=1, source_target_pairs={{0,4},{4,0},{2,6},{6,2},{1,5},{5,1},{3,7},{7,3},{8,12},{12,8},{10,... | collective-permute-start | bytes 786440 | tf_op jit(solution)/shard_map/ppermute | solution.py:84
  258.3 11.3 %collective-permute-start.40 = (bf16[304,128]{1,0:T(8,128)(2,1)}, bf16[304,128]{1,0:T(8,128)(2,1)S(1)}, u32[]{:S(2)}, u32[]{:S(2)}) collective-permute-start(bf16[304,128]{1,0:T(8,128)(2,1)} %get-tuple-element.180), channel_id=1, source_target_pairs={{0,16},{8,24},{16,0},{24,8},{1,17},{9,25},{17,1},{25,9},{2,18},{10... | collective-permute-start | bytes 233480 | tf_op jit(solution)/shard_map/ppermute | solution.py:563
  272.0 14.5 %collective-permute-start.43 = (bf16[256,128]{1,0:T(8,128)(2,1)}, bf16[256,128]{1,0:T(8,128)(2,1)S(1)}, u32[]{:S(2)}, u32[]{:S(2)}) collective-permute-start(bf16[256,128]{1,0:T(8,128)(2,1)} %get-tuple-element.182.refs_5_.refs_1_.refs_2_), channel_id=1, source_target_pairs={{0,4},{4,0},{2,6},{6,2},{1,5},{5,1},{3,7},{7,3},{8,12},{12,8},{10,... | collective-permute-start | bytes 196616 | tf_op jit(solution)/shard_map/ppermute | solution.py:84
  274.1 20.9 %collective-permute-start.48 = (bf16[512,128]{1,0:T(8,128)(2,1)}, bf16[512,128]{1,0:T(8,128)(2,1)S(1)}, u32[]{:S(2)}, u32[]{:S(2)}) collective-permute-start(bf16[512,128]{1,0:T(8,128)(2,1)} %shard_map.204.refs_1_), channel_id=1, source_target_pairs={{0,2},{2,0},{4,6},{6,4},{1,3},{3,1},{5,7},{7,5},{8,10},{10,8},{12,... | collective-permute-start | bytes 393224 | tf_op jit(solution)/shard_map/ppermute | solution.py:80
  275.6 11.5 %collective-permute-start.45 = (bf16[768,128]{1,0:T(8,128)(2,1)}, bf16[768,128]{1,0:T(8,128)(2,1)S(1)}, u32[]{:S(2)}, u32[]{:S(2)}) collective-permute-start(bf16[768,128]{1,0:T(8,128)(2,1)} %bitcast.42), channel_id=1, source_target_pairs={{0,2},{2,0},{4,6},{6,4},{1,3},{3,1},{5,7},{7,5},{8,10},{10,8},{12,... | collective-permute-start | bytes 589832 | tf_op jit(solution)/shard_map/ppermute | solution.py:80
  275.8 8.7 %collective-permute-start.46 = (bf16[768,128]{1,0:T(8,128)(2,1)}, bf16[768,128]{1,0:T(8,128)(2,1)S(1)}, u32[]{:S(2)}, u32[]{:S(2)}) collective-permute-start(bf16[768,128]{1,0:T(8,128)(2,1)} %bitcast.43), channel_id=1, source_target_pairs={{0,4},{4,0},{2,6},{6,2},{1,5},{5,1},{3,7},{7,3},{8,12},{12,8},{10,... | collective-permute-start | bytes 589832 | tf_op jit(solution)/shard_map/ppermute | solution.py:84
  280.6 14.3 %collective-permute-start.50 = (bf16[512,128]{1,0:T(8,128)(2,1)S(1)}, bf16[512,128]{1,0:T(8,128)(2,1)S(1)}, u32[]{:S(2)}, u32[]{:S(2)}) collective-permute-start(bf16[512,128]{1,0:T(8,128)(2,1)S(1)} %collective-permute-done.49.refs_3_), channel_id=1, source_target_pairs={{0,2},{2,0},{4,6},{6,4},{1,3},{3,1},{5,7},{7,5},{8,10},{10,8},{12,... | collective-permute-start | bytes 393224 | tf_op jit(solution)/shard_map/ppermute | solution.py:80
  (85 other events, 313.8 us)
Sparse Core Ops, SparseCore 0:
  10.9 65.7 all-gather.2
  217.2 19.9 reduce-scatter.4
  240.1 21.6 reduce-scatter.2

commit v2 on v1

--- a/solution.py
+++ b/solution.py
@@ -866,18 +866,15 @@
             to[k, 192:256] = gw_ref[p ^ c, :, k * 128 : (k + 1) * 128]
 
 
-def last_quarter_kernel(place, own, got, sums, one, two, three, *outs):
+def last_quarter_kernel(place, own, got, sums, *outs):
     for k in range(4):
         outs[k][:256] = (own[k].astype(f32) + got[k].astype(f32)).astype(bf16)
-        total = (sums[k] + one[k]) + (two[k] + three[k])
-        outs[k][256:] = total.astype(bf16)
-
-
-def last_total_kernel(place, own, one, two, three, out, small_out):
+        outs[k][256:] = sums[k].astype(bf16)
+
+
+def last_total_kernel(place, own, one, two, three, out):
     total = own[...].astype(f32) + one[...].astype(f32)
-    total = total + (two[...].astype(f32) + three[...].astype(f32))
-    out[...] = total[:256].astype(bf16)
-    small_out[...] = total[256:]
+    out[...] = (total + (two[...].astype(f32) + three[...].astype(f32))).astype(bf16)
 
 
 def halve(place, groups, after=()):
@@ -1093,7 +1090,7 @@
                 top_kernel, hidden_outs, place, [grad_state] + tail
             )
         else:
-            own, far = halve(place, [first_grads, grads])
+            own, far = halve(place, [grads])
             grad_state, sums_in, partial, bias_mlp[0], b_first[0], *grads = run(
                 lower_kernel(0),
                 [(square, f32), ((2, 512), f32)] + hidden_outs,
@@ -1102,13 +1099,9 @@
                 after=[own],
             )
             both = quarter(place, own, far, after=[partial])
-            upper = lax.psum_scatter(both, "shard", scatter_dimension=0)
-        behind = []
-        if layer == 1:
-            first_grads = grads
-        else:
-            own, far = halve(place, [grads])
-            behind = [both, own]
+            heads_sum = lax.psum_scatter(both, "shard", scatter_dimension=0)
+        own, far = halve(place, [grads])
+        behind = [own] if layer == 1 else [both, own]
         grad_mid, sums_mid[layer], gw_out, dq, keep, send = run(
             attend_back_kernel(layer),
             [
@@ -1123,10 +1116,9 @@
             [partial, swap_tp(partial), middle, grad_state] + small_parts + [attn, w_out, q] + chunks + [lse],
             after=behind,
         )
-        if layer == 0:
-            both = quarter(place, own, far, after=[keep])
-            lower = lax.psum_scatter(both, "shard", scatter_dimension=0)
-            behind = [both]
+        both = quarter(place, own, far, after=[keep])
+        hidden[layer] = lax.psum_scatter(both, "shard", scatter_dimension=0)
+        behind = [both]
         dkv, chip = run(halve_kernel, [(square, bf16)] * 2, place, [keep, swap_core(send)], after=behind)
         partial, b_query[layer], *grads = run(
             query_back_kernel,
@@ -1156,21 +1148,28 @@
         + b_first,
         after=[own],
     )
-    pieces = run(
-        last_quarter_kernel,
-        [((304, lanes), bf16)] * 4,
+    pieces = run(last_quarter_kernel, [((304, lanes), bf16)] * 4, place, [own, swap_x(far), sums])
+    grad_x = turn(grad_x, z, True)[:, None]
+    outs_heads = heads_out(
+        place, collect(heads_sum), 1, w_qkv.shape, w_proj.shape, [], 0, after=pieces[:1]
+    )
+    outs_hidden = hidden_out(
+        place, collect(hidden[1]), 1, w_fc1.shape, w_fc2.shape, [], 0, after=pieces[:1]
+    )
+    lower = collect(hand_on(place, hidden[0], outs_heads + outs_hidden))
+    got = [shift(pieces[k], 4 - k) for k in (1, 2, 3)]
+    (last,) = run(
+        last_total_kernel,
+        [((304, lanes), bf16)],
         place,
-        [own, swap_x(far), sums, swap_core(sums), swap_x(sums), swap_both(sums)],
-    )
-    grad_x = turn(grad_x, z, True)[:, None]
-    got = [shift(pieces[k], 4 - k) for k in (1, 2, 3)]
-    last, total = run(
-        last_total_kernel, [((256, lanes), bf16), ((48, lanes), f32)], place, [pieces[0]] + got
-    )
-    upper_parts, lower_parts = collect(upper), collect(hand_on(place, lower, [last]))
-    outs_heads = heads_out(place, upper_parts, 1, w_qkv.shape, w_proj.shape, [], 512, after=[last])
-    outs_hidden = hidden_out(place, upper_parts, 1, w_fc1.shape, w_fc2.shape, [], 0, after=[last])
-    grad_fc1, grad_fc2 = hidden_out(place, lower_parts, 0, w_fc1.shape, w_fc2.shape, outs_hidden, 0)
+        [pieces[0]] + got,
+        after=outs_heads + outs_hidden,
+    )
+    last_parts = collect(last)
+    grad_fc1, grad_fc2 = hidden_out(
+        place, lower, 0, w_fc1.shape, w_fc2.shape, outs_hidden, 0, after=[last]
+    )
+    total = sum(part[256:].astype(f32) for part in last_parts)
     grad_gains = total[:4].reshape(gains.shape)
     grad_biases = total[4:12].reshape(biases.shape)
     rest_q = total[12:20].reshape(2, 2, 4, 64)
@@ -1178,7 +1177,7 @@
     grad_b_qv = lax.dynamic_slice_in_dim(rest_q, z * 16, 16, 3)
     grad_b_fc1 = lax.dynamic_slice_in_dim(rest_f, z * 16, 16, 2)
 
-    grad_qkv, grad_proj = heads_out(place, collect(last), 0, w_qkv.shape, w_proj.shape, outs_heads, 0)
+    grad_qkv, grad_proj = heads_out(place, last_parts, 0, w_qkv.shape, w_proj.shape, outs_heads, 0)
     return (
         output, grad_x, grad_qkv, grad_b_qv, grad_proj, grad_fc1, grad_b_fc1, grad_fc2, grad_gains, grad_biases
     )

time: 306 us -> 295 us (0.964)
  waiting for transfers between devices: 120 us -> 104 us
    ppermute x9, waiting for transfers between devices: 36.5 us -> 29.6 us  [swap_tp(): return lax.ppermute(values, 'tp', [(0, 1), (1, 0)])]
    ppermute x6, waiting for transfers between devices: 8.44 us -> 3.46 us  [shift(): lax.ppermute(values, 'shard', [(z, (z + step) % 4) for z in range(4)])]
    ppermute x12 -> x13, starting transfers between devices: 10.5 us -> 14.1 us  [swap_x(): return lax.ppermute(values, 'ctx', [(0, 2), (2, 0), (1, 3), (3, 1)])]
    ppermute x23 -> x24, waiting for transfers between devices: 8.89 us -> 6.04 us  [swap_core(): return lax.ppermute(values, 'ctx', [(0, 1), (1, 0), (2, 3), (3, 2)])]
    pallas_call x26 -> x28, Pallas kernels: 90.7 us -> 93.3 us  [run(): return list(call(place, *arrays))]
    unnamed x112 -> x116, local copies, waits for them, and re-layouts: 19 us -> 20.7 us
    ppermute x12 -> x13, waiting for transfers between devices: 58 us -> 59.3 us  [swap_x(): return lax.ppermute(values, 'ctx', [(0, 2), (2, 0), (1, 3), (3, 1)])]
  transfers between devices with their start and end apart: 54 -> 56, of which waited for: 30 -> 29; matrix products, arithmetic and copies ran while one was open for 4% -> 4% of each run, Pallas kernels for 18% -> 24%
where the time goes in v2:
time: 295 us; the launch traced here: 294 us
  waiting for transfers between devices  104 us (35%)
  Pallas kernels  101 us (34%)
  starting transfers between devices  39.8 us (13%)
  local copies, waits for them, and re-layouts  27.9 us (9%)
  between operations  16.8 us (6%)
  other arithmetic  3.74 us (1%)
    pallas_call x28, Pallas kernels, run(): return list(call(place, *arrays))  93.3 us
    ppermute x13, waiting for transfers between devices, swap_x(): return lax.ppermute(values, 'ctx', [(0, 2), (2, 0), (1, 3), (3, 1)])  59.3 us
    ppermute x9, waiting for transfers between devices, swap_tp(): return lax.ppermute(values, 'tp', [(0, 1), (1, 0)])  29.6 us
    unnamed x116, local copies, waits for them, and re-layouts  20.7 us
    ppermute x13, starting transfers between devices, swap_x(): return lax.ppermute(values, 'ctx', [(0, 2), (2, 0), (1, 3), (3, 1)])  14.1 us
    ppermute x6, starting transfers between devices, shift(): lax.ppermute(values, 'shard', [(z, (z + step) % 4) for z in range(4)])  11.6 us
    ppermute x9, starting transfers between devices, swap_tp(): return lax.ppermute(values, 'tp', [(0, 1), (1, 0)])  10.7 us
    pallas_call x4, Pallas kernels, layer_out(): pl.pallas_call(inner, grid=(1,), out_shape=[jax.ShapeDtypeStruct(shape, f...  8.05 us
  transfers between devices with their start and end apart: 56, of which 29 were waited for; matrix products, arithmetic and copies ran while one was open for 4% of the time, Pallas kernels for 24%

profile of v2, /device:TPU:0, one launch (start us, length us, event | category | flops | bytes accessed | tf_op | source)
XLA Modules:
  0.0 293.9 jit_solution(2775587572696842133)
XLA Ops:
  39.6 3.1 %shard_map.179 = (f32[256,512]{1,0:T(8,128)}, bf16[256,512]{1,0:T(8,128)(2,1)}, bf16[256,256]{1,0:T(8,128)(2,1)}, bf16[256,512]{1,0:T(8,128)(2,1)}, bf16[4,4,32,768]{3,2,1,0:T(8,128)(2,1)}, /*index=5*/f32[256,512]{1,0:T(8,128)}) custom-call(s32[3]{0:T(128)} %pad_add_fusion.refs_0_, bf16[256,512]{1,0:T(8,128)(2,1)} %copy-done.7, bf16[256,512]{1,0:T(8,128)(2,1)} %copy-done.24, ...), custom_call_target="tpu_custom_call" | custom-call | flops 1048576 | bytes 1024 | tf_op jit(solution)/shard_map/pallas_call | solution.py:405
  43.3 12.1 %collective-permute-done.8.refs_4_.refs_12_ = bf16[256,512]{1,0:T(8,128)(2,1)S(1)} collective-permute-done((bf16[256,512]{1,0:T(8,128)(2,1)}, bf16[256,512]{1,0:T(8,128)(2,1)S(1)}, u32[]{:S(2)}, u32[]{:S(2)}) %collective-permute-start.8) | collective-permute-done | bytes 262176 | tf_op jit(solution)/shard_map/ppermute | solution.py:84
  57.6 4.8 %shard_map.180 = (bf16[256,256]{1,0:T(8,128)(2,1)}, f32[256,128]{1,0:T(8,128)}, bf16[256,512]{1,0:T(8,128)(2,1)}, bf16[4,64,512]{2,1,0:T(8,128)(2,1)}) custom-call(s32[3]{0:T(128)} %pad_add_fusion.refs_0_, bf16[256,256]{1,0:T(8,128)(2,1)} %get-tuple-element.104.refs_1_.refs_9_, bf16[256,512]{1,0:T(8,128)(2,1)} %get-tuple-element.105.refs_2_.refs_10_, ...), custom_call_target="tpu_custom_call" | custom-call | flops 1048576 | bytes 1024 | tf_op jit(solution)/shard_map/pallas_call | solution.py:405
  64.1 6.8 %collective-permute-done.10.refs_3_ = bf16[256,512]{1,0:T(8,128)(2,1)S(1)} collective-permute-done((bf16[256,512]{1,0:T(8,128)(2,1)}, bf16[256,512]{1,0:T(8,128)(2,1)S(1)}, u32[]{:S(2)}, u32[]{:S(2)}) %collective-permute-start.10) | collective-permute-done | bytes 262176 | tf_op jit(solution)/shard_map/ppermute | solution.py:76
  71.0 5.8 %all-gather.3.cloned.1.call-done = bf16[20480,128]{1,0:T(8,128)(2,1)} async-done(((bf16[1280,128]{1,0:T(8,128)(2,1)}), bf16[20480,128]{1,0:T(8,128)(2,1)}) %all-gather.3.cloned.1.call-update) | async-done | bytes 5242896 | tf_op jit(solution)/shard_map/all_gather | solution.py:554
  76.7 4.3 %shard_map.182 = (f32[256,512]{1,0:T(8,128)}, bf16[256,512]{1,0:T(8,128)(2,1)}, f32[256,1024]{1,0:T(8,128)}, bf16[256,512]{1,0:T(8,128)(2,1)}) custom-call(s32[3]{0:T(128)} %pad_add_fusion.refs_0_, f32[256,512]{1,0:T(8,128)} %get-tuple-element.103.refs_1_.refs_4_, bf16[256,512]{1,0:T(8,128)(2,1)} %get-tuple-element.106.refs_2_, bf16[256,512]{1,0:T(8,128)(2,1)} %copy-done.36, ...), custom_call_target="tpu_custom_call" | custom-call | flops 1048576 | bytes 1024 | tf_op jit(solution)/shard_map/pallas_call | solution.py:405
  82.5 7.2 %collective-permute-done.11.refs_3_ = bf16[256,512]{1,0:T(8,128)(2,1)S(1)} collective-permute-done((bf16[256,512]{1,0:T(8,128)(2,1)}, bf16[256,512]{1,0:T(8,128)(2,1)S(1)}, u32[]{:S(2)}, u32[]{:S(2)}) %collective-permute-start.11) | collective-permute-done | bytes 262176 | tf_op jit(solution)/shard_map/ppermute | solution.py:76
  90.4 3.3 %shard_map.183 = (f32[256,512]{1,0:T(8,128)}, bf16[256,512]{1,0:T(8,128)(2,1)}, bf16[256,256]{1,0:T(8,128)(2,1)}, bf16[256,512]{1,0:T(8,128)(2,1)}, bf16[4,4,32,768]{3,2,1,0:T(8,128)(2,1)}) custom-call(s32[3]{0:T(128)} %pad_add_fusion.refs_0_, f32[256,512]{1,0:T(8,128)} %get-tuple-element.107.refs_1_.refs_3_, bf16[256,512]{1,0:T(8,128)(2,1)} %get-tuple-element.108.refs_2_, ...), custom_call_target="tpu_custom_call" | custom-call | flops 1048576 | bytes 1024 | tf_op jit(solution)/shard_map/pallas_call | solution.py:405
  94.7 6.9 %collective-permute-done.13.refs_4_.refs_12_ = bf16[256,512]{1,0:T(8,128)(2,1)S(1)} collective-permute-done((bf16[256,512]{1,0:T(8,128)(2,1)}, bf16[256,512]{1,0:T(8,128)(2,1)S(1)}, u32[]{:S(2)}, u32[]{:S(2)}) %collective-permute-start.13) | collective-permute-done | bytes 262176 | tf_op jit(solution)/shard_map/ppermute | solution.py:84
  103.8 4.9 %shard_map.184 = (bf16[256,256]{1,0:T(8,128)(2,1)}, f32[256,128]{1,0:T(8,128)}, bf16[256,512]{1,0:T(8,128)(2,1)}, bf16[4,64,512]{2,1,0:T(8,128)(2,1)}) custom-call(s32[3]{0:T(128)} %pad_add_fusion.refs_0_, bf16[256,256]{1,0:T(8,128)(2,1)} %get-tuple-element.110.refs_1_.refs_9_, bf16[256,512]{1,0:T(8,128)(2,1)} %get-tuple-element.111.refs_2_.refs_10_, ...), custom_call_target="tpu_custom_call" | custom-call | flops 1048576 | bytes 1024 | tf_op jit(solution)/shard_map/pallas_call | solution.py:405
  110.2 7.1 %collective-permute-done.15.refs_3_ = bf16[256,512]{1,0:T(8,128)(2,1)S(1)} collective-permute-done((bf16[256,512]{1,0:T(8,128)(2,1)}, bf16[256,512]{1,0:T(8,128)(2,1)S(1)}, u32[]{:S(2)}, u32[]{:S(2)}) %collective-permute-start.15) | collective-permute-done | bytes 262176 | tf_op jit(solution)/shard_map/ppermute | solution.py:76
  118.0 4.3 %shard_map.185 = (f32[256,512]{1,0:T(8,128)}, bf16[256,512]{1,0:T(8,128)(2,1)}, f32[256,1024]{1,0:T(8,128)}, bf16[256,512]{1,0:T(8,128)(2,1)}) custom-call(s32[3]{0:T(128)} %pad_add_fusion.refs_0_, f32[256,512]{1,0:T(8,128)} %get-tuple-element.109.refs_1_.refs_4_, bf16[256,512]{1,0:T(8,128)(2,1)} %get-tuple-element.112.refs_2_, bf16[256,512]{1,0:T(8,128)(2,1)} %copy-done.37, ...), custom_call_target="tpu_custom_call" | custom-call | flops 1048576 | bytes 1024 | tf_op jit(solution)/shard_map/pallas_call | solution.py:405
  122.3 5.3 %shard_map.186 = (bf16[256,512]{1,0:T(8,128)(2,1)}, f32[1,512]{1,0:T(1,128)}, f32[4,1,256]{2,1,0:T(1,128)}, bf16[2,4,512,128]{3,2,1,0:T(8,128)(2,1)}, bf16[4,512...) custom-call(s32[3]{0:T(128)} %pad_add_fusion.refs_0_, f32[256,512]{1,0:T(8,128)} %get-tuple-element.115.refs_1_.refs_4_, ...), custom_call_target="tpu_custom_call" | custom-call | flops 1048576 | bytes 1024 | tf_op jit(solution)/shard_map/pallas_call | solution.py:405
  137.5 9.2 %shard_map.188 = (f32[256,512]{1,0:T(8,128)}, f32[3,512]{1,0:T(4,128)}, bf16[4,64,512]{2,1,0:T(8,128)(2,1)}, bf16[256,256]{1,0:T(8,128)(2,1)}, bf16[2,256,512]{2...) custom-call(s32[3]{0:T(128)} %pad_add_fusion.refs_0_, bf16[256,512]{1,0:T(8,128)(2,1)} %get-tuple-element.118.refs_1_, ...), custom_call_target="tpu_custom_call" | custom-call | flops 1048576 | bytes 1024 | tf_op jit(solution)/shard_map/pallas_call | solution.py:405
  157.8 6.4 %collective-permute-done.22.refs_3_ = bf16[256,512]{1,0:T(8,128)(2,1)S(1)} collective-permute-done((bf16[256,512]{1,0:T(8,128)(2,1)}, bf16[256,512]{1,0:T(8,128)(2,1)S(1)}, u32[]{:S(2)}, u32[]{:S(2)}) %collective-permute-start.22) | collective-permute-done | bytes 262176 | tf_op jit(solution)/shard_map/ppermute | solution.py:84
  164.9 3.1 %shard_map.191 = (bf16[256,512]{1,0:T(8,128)(2,1)}, f32[2,256]{1,0:T(2,128)}, bf16[2,4,256,128]{3,2,1,0:T(8,128)(2,1)}, bf16[4,256,128]{2,1,0:T(8,128)(2,1)}, bf16[4,256,128]{2,1,0:T(8,128)(2,1)}) custom-call(s32[3]{0:T(128)} %pad_add_fusion.refs_0_, bf16[256,256]{1,0:T(8,128)(2,1)} %get-tuple-element.127.refs_1_, ...), custom_call_target="tpu_custom_call" | custom-call | flops 1048576 | bytes 1024 | tf_op jit(solution)/shard_map/pallas_call | solution.py:405
  172.9 4.0 %collective-permute-done.23.refs_3_ = bf16[256,512]{1,0:T(8,128)(2,1)S(1)} collective-permute-done((bf16[256,512]{1,0:T(8,128)(2,1)}, bf16[256,512]{1,0:T(8,128)(2,1)S(1)}, u32[]{:S(2)}, u32[]{:S(2)}) %collective-permute-start.23) | collective-permute-done | bytes 262176 | tf_op jit(solution)/shard_map/ppermute | solution.py:76
  177.6 6.0 %shard_map.193 = (f32[256,512]{1,0:T(8,128)}, f32[2,512]{1,0:T(2,128)}, bf16[256,512]{1,0:T(8,128)(2,1)}, f32[1,512]{1,0:T(1,128)}, f32[4,1,256]{2,1,0:T(1,128)}...) custom-call(s32[3]{0:T(128)} %pad_add_fusion.refs_0_, ...), custom_call_target="tpu_custom_call" | custom-call | flops 1048576 | bytes 1024 | tf_op jit(solution)/shard_map/pallas_call | solution.py:405
  185.8 6.7 %collective-permute-done.27.refs_2_ = bf16[4,256,128]{2,1,0:T(8,128)(2,1)S(1)} collective-permute-done((bf16[4,256,128]{2,1,0:T(8,128)(2,1)S(1)}, bf16[4,256,128]{2,1,0:T(8,128)(2,1)S(1)}, u32[]{:S(2)}, u32[]{:S(2)}) %collective-permute-start.27) | collective-permute-done | bytes 262176 | tf_op jit(solution)/shard_map/ppermute | solution.py:84
  200.6 9.2 %shard_map.196 = (f32[256,512]{1,0:T(8,128)}, f32[3,512]{1,0:T(4,128)}, bf16[4,64,512]{2,1,0:T(8,128)(2,1)}, bf16[256,256]{1,0:T(8,128)(2,1)}, bf16[2,256,512]{2...) custom-call(s32[3]{0:T(128)} %pad_add_fusion.refs_0_, bf16[256,512]{1,0:T(8,128)(2,1)} %get-tuple-element.143.refs_3_.refs_1_, ...), custom_call_target="tpu_custom_call" | custom-call | flops 1048576 | bytes 1024 | tf_op jit(solution)/shard_map/pallas_call | solution.py:405
  219.0 5.7 %collective-permute-done.32.refs_3_ = bf16[256,512]{1,0:T(8,128)(2,1)S(1)} collective-permute-done((bf16[256,512]{1,0:T(8,128)(2,1)}, bf16[256,512]{1,0:T(8,128)(2,1)S(1)}, u32[]{:S(2)}, u32[]{:S(2)}) %collective-permute-start.32) | collective-permute-done | bytes 262176 | tf_op jit(solution)/shard_map/ppermute | solution.py:84
  236.5 9.7 %collective-permute-done.41.refs_3_ = bf16[256,128]{1,0:T(8,128)(2,1)S(1)} collective-permute-done((bf16[256,128]{1,0:T(8,128)(2,1)}, bf16[256,128]{1,0:T(8,128)(2,1)S(1)}, u32[]{:S(2)}, u32[]{:S(2)}) %collective-permute-start.41) | collective-permute-done | bytes 65568 | tf_op jit(solution)/shard_map/ppermute | solution.py:84
  266.9 3.5 %collective-permute-done.47.refs_3_ = bf16[304,128]{1,0:T(8,128)(2,1)S(1)} collective-permute-done((bf16[304,128]{1,0:T(8,128)(2,1)}, bf16[304,128]{1,0:T(8,128)(2,1)S(1)}, u32[]{:S(2)}, u32[]{:S(2)}) %collective-permute-start.47) | collective-permute-done | bytes 77856 | tf_op jit(solution)/shard_map/ppermute | solution.py:84
  275.7 4.3 %collective-permute-done.50.refs_3_ = bf16[512,128]{1,0:T(8,128)(2,1)S(1)} collective-permute-done((bf16[512,128]{1,0:T(8,128)(2,1)}, bf16[512,128]{1,0:T(8,128)(2,1)S(1)}, u32[]{:S(2)}, u32[]{:S(2)}) %collective-permute-start.50) | collective-permute-done | bytes 131104 | tf_op jit(solution)/shard_map/ppermute | solution.py:84
  (266 shorter events, 133.5 us)
Async XLA Ops:
  7.2 69.6 %all-gather.3.cloned.1.call-start = ((), (), s32[]{:S(2)}) async-start(), calls=%async_computation.6 | async-start | bytes 5570560 | tf_op jit(solution)/shard_map/all_gather | solution.py:554
  10.0 224.4 %reduce-scatter.6.cloned.1.call-start = ((), (), s32[]{:S(2)}) async-start(), calls=%async_computation.4 | async-start | bytes 655360 | tf_op jit(solution)/shard_map/reduce_scatter | solution.py:1120
  14.7 10.2 %collective-permute-start.1 = (bf16[288,128]{1,0:T(8,128)(2,1)}, bf16[288,128]{1,0:T(8,128)(2,1)S(1)}, u32[]{:S(2)}, u32[]{:S(2)}) collective-permute-start(bf16[288,128]{1,0:T(8,128)(2,1)} %get-tuple-element.102), channel_id=1, source_target_pairs={{0,8},{8,16},{16,24},{24,0},{1,9},{9,17},{17,25},{25,1},{2,10},{10... | collective-permute-start | bytes 221192 | tf_op jit(solution)/shard_map/ppermute | solution.py:563
  42.7 12.7 %collective-permute-start.8 = (bf16[256,512]{1,0:T(8,128)(2,1)}, bf16[256,512]{1,0:T(8,128)(2,1)S(1)}, u32[]{:S(2)}, u32[]{:S(2)}) collective-permute-start(bf16[256,512]{1,0:T(8,128)(2,1)} %get-tuple-element.105.refs_2_.refs_10_), channel_id=1, source_target_pairs={{0,4},{4,0},{2,6},{6,2},{1,5},{5,1},{3,7},{7,3},{8,12},{12,8},{10,... | collective-permute-start | bytes 786440 | tf_op jit(solution)/shard_map/ppermute | solution.py:84
  43.3 12.1 %collective-permute-start.7 = (bf16[256,512]{1,0:T(8,128)(2,1)}, bf16[256,512]{1,0:T(8,128)(2,1)S(1)}, u32[]{:S(2)}, u32[]{:S(2)}) collective-permute-start(bf16[256,512]{1,0:T(8,128)(2,1)} %get-tuple-element.105.refs_2_.refs_10_), channel_id=1, source_target_pairs={{0,2},{2,0},{4,6},{6,4},{1,3},{3,1},{5,7},{7,5},{8,10},{10,8},{12,... | collective-permute-start | bytes 786440 | tf_op jit(solution)/shard_map/ppermute | solution.py:80
  81.0 8.7 %collective-permute-start.11 = (bf16[256,512]{1,0:T(8,128)(2,1)}, bf16[256,512]{1,0:T(8,128)(2,1)S(1)}, u32[]{:S(2)}, u32[]{:S(2)}) collective-permute-start(bf16[256,512]{1,0:T(8,128)(2,1)} %get-tuple-element.108.refs_2_), channel_id=1, source_target_pairs={{0,1},{1,0},{2,3},{3,2},{4,5},{5,4},{6,7},{7,6},{8,9},{9,8},{10,11... | collective-permute-start | bytes 786440 | tf_op jit(solution)/shard_map/ppermute | solution.py:76
  134.2 15.5 %collective-permute-start.21 = (bf16[4,512,128]{2,1,0:T(8,128)(2,1)}, bf16[4,512,128]{2,1,0:T(8,128)(2,1)S(1)}, u32[]{:S(2)}, u32[]{:S(2)}) collective-permute-start(bf16[4,512,128]{2,1,0:T(8,128)(2,1)} %get-tuple-element.130), channel_id=1, source_target_pairs={{0,4},{4,0},{2,6},{6,2},{1,5},{5,1},{3,7},{7,3},{8,12},{12,8},{10,... | collective-permute-start | bytes 1572872 | tf_op jit(solution)/shard_map/ppermute | solution.py:84
  146.8 9.9 %collective-permute-start.16 = (bf16[128,512]{1,0:T(8,128)(2,1)S(1)}, bf16[128,512]{1,0:T(8,128)(2,1)S(1)}, u32[]{:S(2)}, u32[]{:S(2)}) collective-permute-start(bf16[128,512]{1,0:T(8,128)(2,1)S(1)} %slice.65), channel_id=1, source_target_pairs={{0,1},{1,0},{2,3},{3,2},{4,5},{5,4},{6,7},{7,6},{8,9},{9,8},{10,11... | collective-permute-start | bytes 393224 | tf_op jit(solution)/shard_map/ppermute | solution.py:76
  169.1 66.3 %reduce-scatter.4.cloned.1.call-start = ((), (), s32[]{:S(2)}) async-start(), calls=%async_computation.3 | async-start | bytes 327680 | tf_op jit(solution)/shard_map/reduce_scatter | solution.py:1102
  183.6 11.4 %collective-permute-start.28 = (bf16[4,512,128]{2,1,0:T(8,128)(2,1)}, bf16[4,512,128]{2,1,0:T(8,128)(2,1)S(1)}, u32[]{:S(2)}, u32[]{:S(2)}) collective-permute-start(bf16[4,512,128]{2,1,0:T(8,128)(2,1)} %get-tuple-element.150), channel_id=1, source_target_pairs={{0,2},{2,0},{4,6},{6,4},{1,3},{3,1},{5,7},{7,5},{8,10},{10,8},{12,... | collective-permute-start | bytes 1572872 | tf_op jit(solution)/shard_map/ppermute | solution.py:80
  183.7 11.3 %collective-permute-start.29 = (bf16[4,512,128]{2,1,0:T(8,128)(2,1)}, bf16[4,512,128]{2,1,0:T(8,128)(2,1)S(1)}, u32[]{:S(2)}, u32[]{:S(2)}) collective-permute-start(bf16[4,512,128]{2,1,0:T(8,128)(2,1)} %get-tuple-element.151), channel_id=1, source_target_pairs={{0,2},{2,0},{4,6},{6,4},{1,3},{3,1},{5,7},{7,5},{8,10},{10,8},{12,... | collective-permute-start | bytes 1572872 | tf_op jit(solution)/shard_map/ppermute | solution.py:80
  185.4 14.5 %collective-permute-start.26 = (bf16[256,512]{1,0:T(8,128)(2,1)}, bf16[256,512]{1,0:T(8,128)(2,1)S(1)}, u32[]{:S(2)}, u32[]{:S(2)}) collective-permute-start(bf16[256,512]{1,0:T(8,128)(2,1)} %get-tuple-element.143.refs_3_.refs_1_), channel_id=1, source_target_pairs={{0,1},{1,0},{2,3},{3,2},{4,5},{5,4},{6,7},{7,6},{8,9},{9,8},{10,11... | collective-permute-start | bytes 786440 | tf_op jit(solution)/shard_map/ppermute | solution.py:76
  198.7 13.3 %collective-permute-start.31 = (bf16[4,512,128]{2,1,0:T(8,128)(2,1)}, bf16[4,512,128]{2,1,0:T(8,128)(2,1)S(1)}, u32[]{:S(2)}, u32[]{:S(2)}) collective-permute-start(bf16[4,512,128]{2,1,0:T(8,128)(2,1)} %get-tuple-element.157), channel_id=1, source_target_pairs={{0,4},{4,0},{2,6},{6,2},{1,5},{5,1},{3,7},{7,3},{8,12},{12,8},{10,... | collective-permute-start | bytes 1572872 | tf_op jit(solution)/shard_map/ppermute | solution.py:84
  209.8 62.7 %reduce-scatter.8.cloned.1.call-start = ((), (), s32[]{:S(2)}) async-start(), calls=%async_computation.5 | async-start | bytes 655360 | tf_op jit(solution)/shard_map/reduce_scatter | solution.py:1120
  229.0 17.6 %collective-permute-start.33 = (bf16[256,512]{1,0:T(8,128)(2,1)}, bf16[256,512]{1,0:T(8,128)(2,1)S(1)}, u32[]{:S(2)}, u32[]{:S(2)}) collective-permute-start(bf16[256,512]{1,0:T(8,128)(2,1)} %get-tuple-element.163.refs_2_), channel_id=1, source_target_pairs={{0,1},{1,0},{2,3},{3,2},{4,5},{5,4},{6,7},{7,6},{8,9},{9,8},{10,11... | collective-permute-start | bytes 786440 | tf_op jit(solution)/shard_map/ppermute | solution.py:76
  233.3 16.5 %collective-permute-start.36 = (bf16[4,256,128]{2,1,0:T(8,128)(2,1)}, bf16[4,256,128]{2,1,0:T(8,128)(2,1)S(1)}, u32[]{:S(2)}, u32[]{:S(2)}) collective-permute-start(bf16[4,256,128]{2,1,0:T(8,128)(2,1)} %get-tuple-element.178), channel_id=1, source_target_pairs={{0,4},{4,0},{2,6},{6,2},{1,5},{5,1},{3,7},{7,3},{8,12},{12,8},{10,... | collective-permute-start | bytes 786440 | tf_op jit(solution)/shard_map/ppermute | solution.py:84
  234.4 11.7 %collective-permute-start.44 = (bf16[512,128]{1,0:T(8,128)(2,1)}, bf16[512,128]{1,0:T(8,128)(2,1)S(1)}, u32[]{:S(2)}, u32[]{:S(2)}) collective-permute-start(bf16[512,128]{1,0:T(8,128)(2,1)} %bitcast.46), channel_id=1, source_target_pairs={{0,4},{4,0},{2,6},{6,2},{1,5},{5,1},{3,7},{7,3},{8,12},{12,8},{10,... | collective-permute-start | bytes 393224 | tf_op jit(solution)/shard_map/ppermute | solution.py:84
  235.4 10.7 %collective-permute-start.41 = (bf16[256,128]{1,0:T(8,128)(2,1)}, bf16[256,128]{1,0:T(8,128)(2,1)S(1)}, u32[]{:S(2)}, u32[]{:S(2)}) collective-permute-start(bf16[256,128]{1,0:T(8,128)(2,1)} %bitcast.49), channel_id=1, source_target_pairs={{0,4},{4,0},{2,6},{6,2},{1,5},{5,1},{3,7},{7,3},{8,12},{12,8},{10,... | collective-permute-start | bytes 196616 | tf_op jit(solution)/shard_map/ppermute | solution.py:84
  236.4 17.2 %collective-permute-start.40 = (bf16[256,128]{1,0:T(8,128)(2,1)}, bf16[256,128]{1,0:T(8,128)(2,1)S(1)}, u32[]{:S(2)}, u32[]{:S(2)}) collective-permute-start(bf16[256,128]{1,0:T(8,128)(2,1)} %bitcast.50), channel_id=1, source_target_pairs={{0,2},{2,0},{4,6},{6,4},{1,3},{3,1},{5,7},{7,5},{8,10},{10,8},{12,... | collective-permute-start | bytes 196616 | tf_op jit(solution)/shard_map/ppermute | solution.py:80
  246.1 9.9 %collective-permute-start.42 = (bf16[256,128]{1,0:T(8,128)(2,1)S(1)}, bf16[256,128]{1,0:T(8,128)(2,1)S(1)}, u32[]{:S(2)}, u32[]{:S(2)}) collective-permute-start(bf16[256,128]{1,0:T(8,128)(2,1)S(1)} %collective-permute-done.41.refs_3_), channel_id=1, source_target_pairs={{0,2},{2,0},{4,6},{6,4},{1,3},{3,1},{5,7},{7,5},{8,10},{10,8},{12,... | collective-permute-start | bytes 196616 | tf_op jit(solution)/shard_map/ppermute | solution.py:80
  246.1 12.7 %collective-permute-start.43 = (bf16[512,128]{1,0:T(8,128)(2,1)}, bf16[512,128]{1,0:T(8,128)(2,1)S(1)}, u32[]{:S(2)}, u32[]{:S(2)}) collective-permute-start(bf16[512,128]{1,0:T(8,128)(2,1)} %bitcast.47), channel_id=1, source_target_pairs={{0,2},{2,0},{4,6},{6,4},{1,3},{3,1},{5,7},{7,5},{8,10},{10,8},{12,... | collective-permute-start | bytes 393224 | tf_op jit(solution)/shard_map/ppermute | solution.py:80
  246.6 12.2 %collective-permute-start.45 = (bf16[512,128]{1,0:T(8,128)(2,1)S(1)}, bf16[512,128]{1,0:T(8,128)(2,1)S(1)}, u32[]{:S(2)}, u32[]{:S(2)}) collective-permute-start(bf16[512,128]{1,0:T(8,128)(2,1)S(1)} %collective-permute-done.44.refs_3_), channel_id=1, source_target_pairs={{0,2},{2,0},{4,6},{6,4},{1,3},{3,1},{5,7},{7,5},{8,10},{10,8},{12,... | collective-permute-start | bytes 393224 | tf_op jit(solution)/shard_map/ppermute | solution.py:80
  252.4 9.9 %collective-permute-start.37 = (bf16[304,128]{1,0:T(8,128)(2,1)}, bf16[304,128]{1,0:T(8,128)(2,1)S(1)}, u32[]{:S(2)}, u32[]{:S(2)}) collective-permute-start(bf16[304,128]{1,0:T(8,128)(2,1)} %get-tuple-element.181), channel_id=1, source_target_pairs={{0,24},{8,0},{16,8},{24,16},{1,25},{9,1},{17,9},{25,17},{2,26},{10... | collective-permute-start | bytes 233480 | tf_op jit(solution)/shard_map/ppermute | solution.py:563
  253.7 9.8 %collective-permute-start.38 = (bf16[304,128]{1,0:T(8,128)(2,1)}, bf16[304,128]{1,0:T(8,128)(2,1)S(1)}, u32[]{:S(2)}, u32[]{:S(2)}) collective-permute-start(bf16[304,128]{1,0:T(8,128)(2,1)} %get-tuple-element.182), channel_id=1, source_target_pairs={{0,16},{8,24},{16,0},{24,8},{1,17},{9,25},{17,1},{25,9},{2,18},{10... | collective-permute-start | bytes 233480 | tf_op jit(solution)/shard_map/ppermute | solution.py:563
  (89 other events, 384.8 us)
Sparse Core Ops, SparseCore 0:
  10.9 65.8 all-gather.2
  169.2 20.8 reduce-scatter.5
  209.9 18.3 reduce-scatter.3
  230.5 19.9 reduce-scatter.7

commit v3 on v2

--- a/solution.py
+++ b/solution.py
@@ -890,12 +890,8 @@
     return both
 
 
-def copy_kernel(place, source, out):
-    out[...] = source[...]
-
-
-def hand_on(place, array, after):
-    return run(copy_kernel, [(array.shape, bf16)], place, [array], after=after)[0]
+def join_kernel(place, one, two, three, out):
+    out[:512], out[512:1024], out[1024:] = one[...], two[...], three[...]
 
 
 def collect(total):
@@ -1150,24 +1146,23 @@
     )
     pieces = run(last_quarter_kernel, [((304, lanes), bf16)] * 4, place, [own, swap_x(far), sums])
     grad_x = turn(grad_x, z, True)[:, None]
-    outs_heads = heads_out(
-        place, collect(heads_sum), 1, w_qkv.shape, w_proj.shape, [], 0, after=pieces[:1]
-    )
-    outs_hidden = hidden_out(
-        place, collect(hidden[1]), 1, w_fc1.shape, w_fc2.shape, [], 0, after=pieces[:1]
-    )
-    lower = collect(hand_on(place, hidden[0], outs_heads + outs_hidden))
+    (joined,) = run(
+        join_kernel, [((1280, lanes), bf16)], place, [hidden[1], hidden[0], heads_sum], after=pieces[:1]
+    )
+    upper = collect(joined)
     got = [shift(pieces[k], 4 - k) for k in (1, 2, 3)]
     (last,) = run(
         last_total_kernel,
         [((304, lanes), bf16)],
         place,
         [pieces[0]] + got,
-        after=outs_heads + outs_hidden,
+        after=upper[1:],
     )
     last_parts = collect(last)
+    outs_heads = heads_out(place, upper, 1, w_qkv.shape, w_proj.shape, [], 1024, after=[last])
+    outs_hidden = hidden_out(place, upper, 1, w_fc1.shape, w_fc2.shape, [], 0, after=[last])
     grad_fc1, grad_fc2 = hidden_out(
-        place, lower, 0, w_fc1.shape, w_fc2.shape, outs_hidden, 0, after=[last]
+        place, upper, 0, w_fc1.shape, w_fc2.shape, outs_hidden, 512, after=[last]
     )
     total = sum(part[256:].astype(f32) for part in last_parts)
     grad_gains = total[:4].reshape(gains.shape)

time: 295 us -> 290 us (0.983)
  starting transfers between devices: 39.8 us -> 35.6 us
    ppermute x13 -> x11, waiting for transfers between devices: 59.3 us -> 49.6 us  [swap_x(): return lax.ppermute(values, 'ctx', [(0, 2), (2, 0), (1, 3), (3, 1)])]
    ppermute x6, waiting for transfers between devices: 3.46 us -> 9.24 us  [shift(): lax.ppermute(values, 'shard', [(z, (z + step) % 4) for z in range(4)])]
    ppermute x13 -> x11, starting transfers between devices: 14.1 us -> 10.6 us  [swap_x(): return lax.ppermute(values, 'ctx', [(0, 2), (2, 0), (1, 3), (3, 1)])]
    ppermute x9, waiting for transfers between devices: 29.6 us -> 32.9 us  [swap_tp(): return lax.ppermute(values, 'tp', [(0, 1), (1, 0)])]
    unnamed x116 -> x102, local copies, waits for them, and re-layouts: 20.7 us -> 18.6 us
    ppermute x24 -> x20, waiting for transfers between devices: 6.04 us -> 7.06 us  [swap_core(): return lax.ppermute(values, 'ctx', [(0, 1), (1, 0), (2, 3), (3, 2)])]
  transfers between devices with their start and end apart: 56 -> 50, of which waited for: 29 -> 31; matrix products, arithmetic and copies ran while one was open for 4% -> 3% of each run, Pallas kernels for 24% -> 25%
where the time goes in v3:
time: 290 us; the launch traced here: 289 us
  waiting for transfers between devices  105 us (36%)
  Pallas kernels  101 us (35%)
  starting transfers between devices  35.6 us (12%)
  local copies, waits for them, and re-layouts  26.7 us (9%)
  between operations  16.8 us (6%)
  other arithmetic  3.77 us (1%)
    pallas_call x28, Pallas kernels, run(): return list(call(place, *arrays))  93.4 us
    ppermute x11, waiting for transfers between devices, swap_x(): return lax.ppermute(values, 'ctx', [(0, 2), (2, 0), (1, 3), (3, 1)])  49.6 us
    ppermute x9, waiting for transfers between devices, swap_tp(): return lax.ppermute(values, 'tp', [(0, 1), (1, 0)])  32.9 us
    unnamed x102, local copies, waits for them, and re-layouts  18.6 us
    ppermute x6, starting transfers between devices, shift(): lax.ppermute(values, 'shard', [(z, (z + step) % 4) for z in range(4)])  11.6 us
    ppermute x9, starting transfers between devices, swap_tp(): return lax.ppermute(values, 'tp', [(0, 1), (1, 0)])  10.7 us
    ppermute x11, starting transfers between devices, swap_x(): return lax.ppermute(values, 'ctx', [(0, 2), (2, 0), (1, 3), (3, 1)])  10.6 us
    ppermute x6, waiting for transfers between devices, shift(): lax.ppermute(values, 'shard', [(z, (z + step) % 4) for z in range(4)])  9.24 us
  transfers between devices with their start and end apart: 50, of which 31 were waited for; matrix products, arithmetic and copies ran while one was open for 3% of the time, Pallas kernels for 25%

profile of v3, /device:TPU:0, one launch (start us, length us, event | category | flops | bytes accessed | tf_op | source)
XLA Modules:
  0.0 289.0 jit_solution(16495466587448942313)
XLA Ops:
  39.5 3.1 %shard_map.179 = (f32[256,512]{1,0:T(8,128)}, bf16[256,512]{1,0:T(8,128)(2,1)}, bf16[256,256]{1,0:T(8,128)(2,1)}, bf16[256,512]{1,0:T(8,128)(2,1)}, bf16[4,4,32,768]{3,2,1,0:T(8,128)(2,1)}, /*index=5*/f32[256,512]{1,0:T(8,128)}) custom-call(s32[3]{0:T(128)} %pad_add_fusion.refs_0_, bf16[256,512]{1,0:T(8,128)(2,1)} %copy-done.10, ...), custom_call_target="tpu_custom_call" | custom-call | flops 1048576 | bytes 1024 | tf_op jit(solution)/shard_map/pallas_call | solution.py:405
  43.3 12.1 %collective-permute-done.8.refs_4_.refs_12_ = bf16[256,512]{1,0:T(8,128)(2,1)S(1)} collective-permute-done((bf16[256,512]{1,0:T(8,128)(2,1)}, bf16[256,512]{1,0:T(8,128)(2,1)S(1)}, u32[]{:S(2)}, u32[]{:S(2)}) %collective-permute-start.8) | collective-permute-done | bytes 262176 | tf_op jit(solution)/shard_map/ppermute | solution.py:84
  57.6 4.8 %shard_map.180 = (bf16[256,256]{1,0:T(8,128)(2,1)}, f32[256,128]{1,0:T(8,128)}, bf16[256,512]{1,0:T(8,128)(2,1)}, bf16[4,64,512]{2,1,0:T(8,128)(2,1)}) custom-call(s32[3]{0:T(128)} %pad_add_fusion.refs_0_, bf16[256,256]{1,0:T(8,128)(2,1)} %get-tuple-element.104.refs_1_.refs_9_, bf16[256,512]{1,0:T(8,128)(2,1)} %get-tuple-element.105.refs_2_.refs_10_, ...), custom_call_target="tpu_custom_call" | custom-call | flops 1048576 | bytes 1024 | tf_op jit(solution)/shard_map/pallas_call | solution.py:405
  63.9 6.9 %collective-permute-done.10.refs_3_ = bf16[256,512]{1,0:T(8,128)(2,1)S(1)} collective-permute-done((bf16[256,512]{1,0:T(8,128)(2,1)}, bf16[256,512]{1,0:T(8,128)(2,1)S(1)}, u32[]{:S(2)}, u32[]{:S(2)}) %collective-permute-start.10) | collective-permute-done | bytes 262176 | tf_op jit(solution)/shard_map/ppermute | solution.py:76
  70.9 5.9 %all-gather.3.cloned.1.call-done = bf16[20480,128]{1,0:T(8,128)(2,1)} async-done(((bf16[1280,128]{1,0:T(8,128)(2,1)}), bf16[20480,128]{1,0:T(8,128)(2,1)}) %all-gather.3.cloned.1.call-update) | async-done | bytes 5242896 | tf_op jit(solution)/shard_map/all_gather | solution.py:554
  76.8 4.3 %shard_map.182 = (f32[256,512]{1,0:T(8,128)}, bf16[256,512]{1,0:T(8,128)(2,1)}, f32[256,1024]{1,0:T(8,128)}, bf16[256,512]{1,0:T(8,128)(2,1)}) custom-call(s32[3]{0:T(128)} %pad_add_fusion.refs_0_, f32[256,512]{1,0:T(8,128)} %get-tuple-element.103.refs_1_.refs_4_, bf16[256,512]{1,0:T(8,128)(2,1)} %get-tuple-element.106.refs_2_, bf16[256,512]{1,0:T(8,128)(2,1)} %copy-done.38, ...), custom_call_target="tpu_custom_call" | custom-call | flops 1048576 | bytes 1024 | tf_op jit(solution)/shard_map/pallas_call | solution.py:405
  82.5 7.2 %collective-permute-done.11.refs_3_ = bf16[256,512]{1,0:T(8,128)(2,1)S(1)} collective-permute-done((bf16[256,512]{1,0:T(8,128)(2,1)}, bf16[256,512]{1,0:T(8,128)(2,1)S(1)}, u32[]{:S(2)}, u32[]{:S(2)}) %collective-permute-start.11) | collective-permute-done | bytes 262176 | tf_op jit(solution)/shard_map/ppermute | solution.py:76
  90.4 3.2 %shard_map.183 = (f32[256,512]{1,0:T(8,128)}, bf16[256,512]{1,0:T(8,128)(2,1)}, bf16[256,256]{1,0:T(8,128)(2,1)}, bf16[256,512]{1,0:T(8,128)(2,1)}, bf16[4,4,32,768]{3,2,1,0:T(8,128)(2,1)}) custom-call(s32[3]{0:T(128)} %pad_add_fusion.refs_0_, f32[256,512]{1,0:T(8,128)} %get-tuple-element.107.refs_1_.refs_3_, bf16[256,512]{1,0:T(8,128)(2,1)} %get-tuple-element.108.refs_2_, ...), custom_call_target="tpu_custom_call" | custom-call | flops 1048576 | bytes 1024 | tf_op jit(solution)/shard_map/pallas_call | solution.py:405
  94.5 7.1 %collective-permute-done.13.refs_4_.refs_12_ = bf16[256,512]{1,0:T(8,128)(2,1)S(1)} collective-permute-done((bf16[256,512]{1,0:T(8,128)(2,1)}, bf16[256,512]{1,0:T(8,128)(2,1)S(1)}, u32[]{:S(2)}, u32[]{:S(2)}) %collective-permute-start.13) | collective-permute-done | bytes 262176 | tf_op jit(solution)/shard_map/ppermute | solution.py:84
  103.7 4.9 %shard_map.184 = (bf16[256,256]{1,0:T(8,128)(2,1)}, f32[256,128]{1,0:T(8,128)}, bf16[256,512]{1,0:T(8,128)(2,1)}, bf16[4,64,512]{2,1,0:T(8,128)(2,1)}) custom-call(s32[3]{0:T(128)} %pad_add_fusion.refs_0_, bf16[256,256]{1,0:T(8,128)(2,1)} %get-tuple-element.110.refs_1_.refs_9_, bf16[256,512]{1,0:T(8,128)(2,1)} %get-tuple-element.111.refs_2_.refs_10_, ...), custom_call_target="tpu_custom_call" | custom-call | flops 1048576 | bytes 1024 | tf_op jit(solution)/shard_map/pallas_call | solution.py:405
  110.2 7.1 %collective-permute-done.15.refs_3_ = bf16[256,512]{1,0:T(8,128)(2,1)S(1)} collective-permute-done((bf16[256,512]{1,0:T(8,128)(2,1)}, bf16[256,512]{1,0:T(8,128)(2,1)S(1)}, u32[]{:S(2)}, u32[]{:S(2)}) %collective-permute-start.15) | collective-permute-done | bytes 262176 | tf_op jit(solution)/shard_map/ppermute | solution.py:76
  117.9 4.3 %shard_map.185 = (f32[256,512]{1,0:T(8,128)}, bf16[256,512]{1,0:T(8,128)(2,1)}, f32[256,1024]{1,0:T(8,128)}, bf16[256,512]{1,0:T(8,128)(2,1)}) custom-call(s32[3]{0:T(128)} %pad_add_fusion.refs_0_, f32[256,512]{1,0:T(8,128)} %get-tuple-element.109.refs_1_.refs_4_, bf16[256,512]{1,0:T(8,128)(2,1)} %get-tuple-element.112.refs_2_, bf16[256,512]{1,0:T(8,128)(2,1)} %copy-done.39, ...), custom_call_target="tpu_custom_call" | custom-call | flops 1048576 | bytes 1024 | tf_op jit(solution)/shard_map/pallas_call | solution.py:405
  122.2 5.3 %shard_map.186 = (bf16[256,512]{1,0:T(8,128)(2,1)}, f32[1,512]{1,0:T(1,128)}, f32[4,1,256]{2,1,0:T(1,128)}, bf16[2,4,512,128]{3,2,1,0:T(8,128)(2,1)}, bf16[4,512...) custom-call(s32[3]{0:T(128)} %pad_add_fusion.refs_0_, f32[256,512]{1,0:T(8,128)} %get-tuple-element.115.refs_1_.refs_4_, ...), custom_call_target="tpu_custom_call" | custom-call | flops 1048576 | bytes 1024 | tf_op jit(solution)/shard_map/pallas_call | solution.py:405
  137.3 9.2 %shard_map.188 = (f32[256,512]{1,0:T(8,128)}, f32[3,512]{1,0:T(4,128)}, bf16[4,64,512]{2,1,0:T(8,128)(2,1)}, bf16[256,256]{1,0:T(8,128)(2,1)}, bf16[2,256,512]{2...) custom-call(s32[3]{0:T(128)} %pad_add_fusion.refs_0_, bf16[256,512]{1,0:T(8,128)(2,1)} %get-tuple-element.118.refs_1_, ...), custom_call_target="tpu_custom_call" | custom-call | flops 1048576 | bytes 1024 | tf_op jit(solution)/shard_map/pallas_call | solution.py:405
  157.4 6.6 %collective-permute-done.22.refs_3_ = bf16[256,512]{1,0:T(8,128)(2,1)S(1)} collective-permute-done((bf16[256,512]{1,0:T(8,128)(2,1)}, bf16[256,512]{1,0:T(8,128)(2,1)S(1)}, u32[]{:S(2)}, u32[]{:S(2)}) %collective-permute-start.22) | collective-permute-done | bytes 262176 | tf_op jit(solution)/shard_map/ppermute | solution.py:84
  164.6 3.1 %shard_map.191 = (bf16[256,512]{1,0:T(8,128)(2,1)}, f32[2,256]{1,0:T(2,128)}, bf16[2,4,256,128]{3,2,1,0:T(8,128)(2,1)}, bf16[4,256,128]{2,1,0:T(8,128)(2,1)}, bf16[4,256,128]{2,1,0:T(8,128)(2,1)}) custom-call(s32[3]{0:T(128)} %pad_add_fusion.refs_0_, bf16[256,256]{1,0:T(8,128)(2,1)} %get-tuple-element.127.refs_1_, ...), custom_call_target="tpu_custom_call" | custom-call | flops 1048576 | bytes 1024 | tf_op jit(solution)/shard_map/pallas_call | solution.py:405
  172.7 4.0 %collective-permute-done.23.refs_3_ = bf16[256,512]{1,0:T(8,128)(2,1)S(1)} collective-permute-done((bf16[256,512]{1,0:T(8,128)(2,1)}, bf16[256,512]{1,0:T(8,128)(2,1)S(1)}, u32[]{:S(2)}, u32[]{:S(2)}) %collective-permute-start.23) | collective-permute-done | bytes 262176 | tf_op jit(solution)/shard_map/ppermute | solution.py:76
  177.4 6.0 %shard_map.193 = (f32[256,512]{1,0:T(8,128)}, f32[2,512]{1,0:T(2,128)}, bf16[256,512]{1,0:T(8,128)(2,1)}, f32[1,512]{1,0:T(1,128)}, f32[4,1,256]{2,1,0:T(1,128)}...) custom-call(s32[3]{0:T(128)} %pad_add_fusion.refs_0_, ...), custom_call_target="tpu_custom_call" | custom-call | flops 1048576 | bytes 1024 | tf_op jit(solution)/shard_map/pallas_call | solution.py:405
  195.8 9.2 %shard_map.196 = (f32[256,512]{1,0:T(8,128)}, f32[3,512]{1,0:T(4,128)}, bf16[4,64,512]{2,1,0:T(8,128)(2,1)}, bf16[256,256]{1,0:T(8,128)(2,1)}, bf16[2,256,512]{2...) custom-call(s32[3]{0:T(128)} %pad_add_fusion.refs_0_, bf16[256,512]{1,0:T(8,128)(2,1)} %get-tuple-element.143.refs_3_.refs_1_, ...), custom_call_target="tpu_custom_call" | custom-call | flops 1048576 | bytes 1024 | tf_op jit(solution)/shard_map/pallas_call | solution.py:405
  211.9 7.9 %collective-permute-done.32.refs_3_ = bf16[256,512]{1,0:T(8,128)(2,1)S(1)} collective-permute-done((bf16[256,512]{1,0:T(8,128)(2,1)}, bf16[256,512]{1,0:T(8,128)(2,1)S(1)}, u32[]{:S(2)}, u32[]{:S(2)}) %collective-permute-start.32) | collective-permute-done | bytes 262176 | tf_op jit(solution)/shard_map/ppermute | solution.py:84
  220.6 3.1 %shard_map.199 = (bf16[256,512]{1,0:T(8,128)(2,1)}, f32[2,256]{1,0:T(2,128)}, bf16[2,4,256,128]{3,2,1,0:T(8,128)(2,1)}, bf16[4,256,128]{2,1,0:T(8,128)(2,1)}, bf16[4,256,128]{2,1,0:T(8,128)(2,1)}) custom-call(s32[3]{0:T(128)} %pad_add_fusion.refs_0_, bf16[256,256]{1,0:T(8,128)(2,1)} %get-tuple-element.154.refs_1_, ...), custom_call_target="tpu_custom_call" | custom-call | flops 1048576 | bytes 1024 | tf_op jit(solution)/shard_map/pallas_call | solution.py:405
  229.5 3.1 %collective-permute-done.33.refs_3_ = bf16[256,512]{1,0:T(8,128)(2,1)S(1)} collective-permute-done((bf16[256,512]{1,0:T(8,128)(2,1)}, bf16[256,512]{1,0:T(8,128)(2,1)S(1)}, u32[]{:S(2)}, u32[]{:S(2)}) %collective-permute-start.33) | collective-permute-done | bytes 262176 | tf_op jit(solution)/shard_map/ppermute | solution.py:76
  242.3 8.2 %collective-permute-done.41.refs_6_.refs_3_ = bf16[1280,128]{1,0:T(8,128)(2,1)S(1)} collective-permute-done((bf16[1280,128]{1,0:T(8,128)(2,1)}, bf16[1280,128]{1,0:T(8,128)(2,1)S(1)}, u32[]{:S(2)}, u32[]{:S(2)}) %collective-permute-start.41) | collective-permute-done | bytes 327712 | tf_op jit(solution)/shard_map/ppermute | solution.py:84
  255.9 6.2 %collective-permute-done.38.refs_3_ = bf16[304,128]{1,0:T(8,128)(2,1)S(1)} collective-permute-done((bf16[304,128]{1,0:T(8,128)(2,1)}, bf16[304,128]{1,0:T(8,128)(2,1)S(1)}, u32[]{:S(2)}, u32[]{:S(2)}) %collective-permute-start.38) | collective-permute-done | bytes 77856 | tf_op jit(solution)/shard_map/ppermute | solution.py:563
  (240 shorter events, 129.6 us)
Async XLA Ops:
  7.2 69.6 %all-gather.3.cloned.1.call-start = ((), (), s32[]{:S(2)}) async-start(), calls=%async_computation.6 | async-start | bytes 5570560 | tf_op jit(solution)/shard_map/all_gather | solution.py:554
  10.0 229.6 %reduce-scatter.4.cloned.1.call-start = ((), (), s32[]{:S(2)}) async-start(), calls=%async_computation.3 | async-start | bytes 655360 | tf_op jit(solution)/shard_map/reduce_scatter | solution.py:1116
  14.7 10.2 %collective-permute-start.1 = (bf16[288,128]{1,0:T(8,128)(2,1)}, bf16[288,128]{1,0:T(8,128)(2,1)S(1)}, u32[]{:S(2)}, u32[]{:S(2)}) collective-permute-start(bf16[288,128]{1,0:T(8,128)(2,1)} %get-tuple-element.102), channel_id=1, source_target_pairs={{0,8},{8,16},{16,24},{24,0},{1,9},{9,17},{17,25},{25,1},{2,10},{10... | collective-permute-start | bytes 221192 | tf_op jit(solution)/shard_map/ppermute | solution.py:563
  42.6 12.7 %collective-permute-start.8 = (bf16[256,512]{1,0:T(8,128)(2,1)}, bf16[256,512]{1,0:T(8,128)(2,1)S(1)}, u32[]{:S(2)}, u32[]{:S(2)}) collective-permute-start(bf16[256,512]{1,0:T(8,128)(2,1)} %get-tuple-element.105.refs_2_.refs_10_), channel_id=1, source_target_pairs={{0,4},{4,0},{2,6},{6,2},{1,5},{5,1},{3,7},{7,3},{8,12},{12,8},{10,... | collective-permute-start | bytes 786440 | tf_op jit(solution)/shard_map/ppermute | solution.py:84
  43.3 12.1 %collective-permute-start.7 = (bf16[256,512]{1,0:T(8,128)(2,1)}, bf16[256,512]{1,0:T(8,128)(2,1)S(1)}, u32[]{:S(2)}, u32[]{:S(2)}) collective-permute-start(bf16[256,512]{1,0:T(8,128)(2,1)} %get-tuple-element.105.refs_2_.refs_10_), channel_id=1, source_target_pairs={{0,2},{2,0},{4,6},{6,4},{1,3},{3,1},{5,7},{7,5},{8,10},{10,8},{12,... | collective-permute-start | bytes 786440 | tf_op jit(solution)/shard_map/ppermute | solution.py:80
  62.3 8.6 %collective-permute-start.10 = (bf16[256,512]{1,0:T(8,128)(2,1)}, bf16[256,512]{1,0:T(8,128)(2,1)S(1)}, u32[]{:S(2)}, u32[]{:S(2)}) collective-permute-start(bf16[256,512]{1,0:T(8,128)(2,1)} %get-tuple-element.106.refs_2_), channel_id=1, source_target_pairs={{0,1},{1,0},{2,3},{3,2},{4,5},{5,4},{6,7},{7,6},{8,9},{9,8},{10,11... | collective-permute-start | bytes 786440 | tf_op jit(solution)/shard_map/ppermute | solution.py:76
  81.0 8.7 %collective-permute-start.11 = (bf16[256,512]{1,0:T(8,128)(2,1)}, bf16[256,512]{1,0:T(8,128)(2,1)S(1)}, u32[]{:S(2)}, u32[]{:S(2)}) collective-permute-start(bf16[256,512]{1,0:T(8,128)(2,1)} %get-tuple-element.108.refs_2_), channel_id=1, source_target_pairs={{0,1},{1,0},{2,3},{3,2},{4,5},{5,4},{6,7},{7,6},{8,9},{9,8},{10,11... | collective-permute-start | bytes 786440 | tf_op jit(solution)/shard_map/ppermute | solution.py:76
  108.7 8.6 %collective-permute-start.15 = (bf16[256,512]{1,0:T(8,128)(2,1)}, bf16[256,512]{1,0:T(8,128)(2,1)S(1)}, u32[]{:S(2)}, u32[]{:S(2)}) collective-permute-start(bf16[256,512]{1,0:T(8,128)(2,1)} %get-tuple-element.112.refs_2_), channel_id=1, source_target_pairs={{0,1},{1,0},{2,3},{3,2},{4,5},{5,4},{6,7},{7,6},{8,9},{9,8},{10,11... | collective-permute-start | bytes 786440 | tf_op jit(solution)/shard_map/ppermute | solution.py:76
  128.1 8.5 %collective-permute-start.17 = (bf16[256,512]{1,0:T(8,128)(2,1)}, bf16[256,512]{1,0:T(8,128)(2,1)S(1)}, u32[]{:S(2)}, u32[]{:S(2)}) collective-permute-start(bf16[256,512]{1,0:T(8,128)(2,1)} %get-tuple-element.118.refs_1_), channel_id=1, source_target_pairs={{0,1},{1,0},{2,3},{3,2},{4,5},{5,4},{6,7},{7,6},{8,9},{9,8},{10,11... | collective-permute-start | bytes 786440 | tf_op jit(solution)/shard_map/ppermute | solution.py:76
  134.0 15.4 %collective-permute-start.21 = (bf16[4,512,128]{2,1,0:T(8,128)(2,1)}, bf16[4,512,128]{2,1,0:T(8,128)(2,1)S(1)}, u32[]{:S(2)}, u32[]{:S(2)}) collective-permute-start(bf16[4,512,128]{2,1,0:T(8,128)(2,1)} %get-tuple-element.130), channel_id=1, source_target_pairs={{0,4},{4,0},{2,6},{6,2},{1,5},{5,1},{3,7},{7,3},{8,12},{12,8},{10,... | collective-permute-start | bytes 1572872 | tf_op jit(solution)/shard_map/ppermute | solution.py:84
  146.5 9.8 %collective-permute-start.16 = (bf16[128,512]{1,0:T(8,128)(2,1)S(1)}, bf16[128,512]{1,0:T(8,128)(2,1)S(1)}, u32[]{:S(2)}, u32[]{:S(2)}) collective-permute-start(bf16[128,512]{1,0:T(8,128)(2,1)S(1)} %slice.65), channel_id=1, source_target_pairs={{0,1},{1,0},{2,3},{3,2},{4,5},{5,4},{6,7},{7,6},{8,9},{9,8},{10,11... | collective-permute-start | bytes 393224 | tf_op jit(solution)/shard_map/ppermute | solution.py:76
  152.4 87.2 %reduce-scatter.8.cloned.1.call-start = ((), (), s32[]{:S(2)}) async-start(), calls=%async_computation.5 | async-start | bytes 327680 | tf_op jit(solution)/shard_map/reduce_scatter | solution.py:1098
  155.3 8.6 %collective-permute-start.22 = (bf16[256,512]{1,0:T(8,128)(2,1)}, bf16[256,512]{1,0:T(8,128)(2,1)S(1)}, u32[]{:S(2)}, u32[]{:S(2)}) collective-permute-start(bf16[256,512]{1,0:T(8,128)(2,1)} %get-tuple-element.132), channel_id=1, source_target_pairs={{0,4},{4,0},{2,6},{6,2},{1,5},{5,1},{3,7},{7,3},{8,12},{12,8},{10,... | collective-permute-start | bytes 786440 | tf_op jit(solution)/shard_map/ppermute | solution.py:84
  185.0 10.1 %collective-permute-start.26 = (bf16[256,512]{1,0:T(8,128)(2,1)}, bf16[256,512]{1,0:T(8,128)(2,1)S(1)}, u32[]{:S(2)}, u32[]{:S(2)}) collective-permute-start(bf16[256,512]{1,0:T(8,128)(2,1)} %get-tuple-element.143.refs_3_.refs_1_), channel_id=1, source_target_pairs={{0,1},{1,0},{2,3},{3,2},{4,5},{5,4},{6,7},{7,6},{8,9},{9,8},{10,11... | collective-permute-start | bytes 786440 | tf_op jit(solution)/shard_map/ppermute | solution.py:76
  189.8 15.2 %collective-permute-start.31 = (bf16[4,512,128]{2,1,0:T(8,128)(2,1)}, bf16[4,512,128]{2,1,0:T(8,128)(2,1)S(1)}, u32[]{:S(2)}, u32[]{:S(2)}) collective-permute-start(bf16[4,512,128]{2,1,0:T(8,128)(2,1)} %get-tuple-element.157), channel_id=1, source_target_pairs={{0,4},{4,0},{2,6},{6,2},{1,5},{5,1},{3,7},{7,3},{8,12},{12,8},{10,... | collective-permute-start | bytes 1572872 | tf_op jit(solution)/shard_map/ppermute | solution.py:84
  194.8 44.8 %reduce-scatter.6.cloned.1.call-start = ((), (), s32[]{:S(2)}) async-start(), calls=%async_computation.4 | async-start | bytes 655360 | tf_op jit(solution)/shard_map/reduce_scatter | solution.py:1116
  210.9 8.9 %collective-permute-start.32 = (bf16[256,512]{1,0:T(8,128)(2,1)}, bf16[256,512]{1,0:T(8,128)(2,1)S(1)}, u32[]{:S(2)}, u32[]{:S(2)}) collective-permute-start(bf16[256,512]{1,0:T(8,128)(2,1)} %get-tuple-element.159), channel_id=1, source_target_pairs={{0,4},{4,0},{2,6},{6,2},{1,5},{5,1},{3,7},{7,3},{8,12},{12,8},{10,... | collective-permute-start | bytes 786440 | tf_op jit(solution)/shard_map/ppermute | solution.py:84
  224.2 8.4 %collective-permute-start.33 = (bf16[256,512]{1,0:T(8,128)(2,1)}, bf16[256,512]{1,0:T(8,128)(2,1)S(1)}, u32[]{:S(2)}, u32[]{:S(2)}) collective-permute-start(bf16[256,512]{1,0:T(8,128)(2,1)} %get-tuple-element.163.refs_2_), channel_id=1, source_target_pairs={{0,1},{1,0},{2,3},{3,2},{4,5},{5,4},{6,7},{7,6},{8,9},{9,8},{10,11... | collective-permute-start | bytes 786440 | tf_op jit(solution)/shard_map/ppermute | solution.py:76
  228.5 8.6 %collective-permute-start.36 = (bf16[4,256,128]{2,1,0:T(8,128)(2,1)}, bf16[4,256,128]{2,1,0:T(8,128)(2,1)S(1)}, u32[]{:S(2)}, u32[]{:S(2)}) collective-permute-start(bf16[4,256,128]{2,1,0:T(8,128)(2,1)} %get-tuple-element.178), channel_id=1, source_target_pairs={{0,4},{4,0},{2,6},{6,2},{1,5},{5,1},{3,7},{7,3},{8,12},{12,8},{10,... | collective-permute-start | bytes 786440 | tf_op jit(solution)/shard_map/ppermute | solution.py:84
  241.4 9.1 %collective-permute-start.41 = (bf16[1280,128]{1,0:T(8,128)(2,1)}, bf16[1280,128]{1,0:T(8,128)(2,1)S(1)}, u32[]{:S(2)}, u32[]{:S(2)}) collective-permute-start(bf16[1280,128]{1,0:T(8,128)(2,1)} %shard_map.203.refs_1_), channel_id=1, source_target_pairs={{0,4},{4,0},{2,6},{6,2},{1,5},{5,1},{3,7},{7,3},{8,12},{12,8},{10,... | collective-permute-start | bytes 983048 | tf_op jit(solution)/shard_map/ppermute | solution.py:84
  242.3 19.8 %collective-permute-start.40 = (bf16[1280,128]{1,0:T(8,128)(2,1)}, bf16[1280,128]{1,0:T(8,128)(2,1)S(1)}, u32[]{:S(2)}, u32[]{:S(2)}) collective-permute-start(bf16[1280,128]{1,0:T(8,128)(2,1)} %shard_map.203.refs_1_), channel_id=1, source_target_pairs={{0,2},{2,0},{4,6},{6,4},{1,3},{3,1},{5,7},{7,5},{8,10},{10,8},{12,... | collective-permute-start | bytes 983048 | tf_op jit(solution)/shard_map/ppermute | solution.py:80
  250.5 11.7 %collective-permute-start.42 = (bf16[1280,128]{1,0:T(8,128)(2,1)S(1)}, bf16[1280,128]{1,0:T(8,128)(2,1)S(1)}, u32[]{:S(2)}, u32[]{:S(2)}) collective-permute-start(bf16[1280,128]{1,0:T(8,128)(2,1)S(1)} %collective-permute-done.41.refs_6_.refs_3_), channel_id=1, source_target_pairs={{0,2},{2,0},{4,6},{6,4},{1,3},{3,1},{5,7},{7,5},{8,10},{10,8},{12,... | collective-permute-start | bytes 983048 | tf_op jit(solution)/shard_map/ppermute | solution.py:80
  251.1 11.0 %collective-permute-start.38 = (bf16[304,128]{1,0:T(8,128)(2,1)}, bf16[304,128]{1,0:T(8,128)(2,1)S(1)}, u32[]{:S(2)}, u32[]{:S(2)}) collective-permute-start(bf16[304,128]{1,0:T(8,128)(2,1)} %get-tuple-element.182), channel_id=1, source_target_pairs={{0,16},{8,24},{16,0},{24,8},{1,17},{9,25},{17,1},{25,9},{2,18},{10... | collective-permute-start | bytes 233480 | tf_op jit(solution)/shard_map/ppermute | solution.py:563
  266.9 10.3 %collective-permute-start.43 = (bf16[304,128]{1,0:T(8,128)(2,1)}, bf16[304,128]{1,0:T(8,128)(2,1)S(1)}, u32[]{:S(2)}, u32[]{:S(2)}) collective-permute-start(bf16[304,128]{1,0:T(8,128)(2,1)} %shard_map.204.refs_5_.refs_1_.refs_7_), channel_id=1, source_target_pairs={{0,2},{2,0},{4,6},{6,4},{1,3},{3,1},{5,7},{7,5},{8,10},{10,8},{12,... | collective-permute-start | bytes 233480 | tf_op jit(solution)/shard_map/ppermute | solution.py:80
  (76 other events, 283.6 us)
Sparse Core Ops, SparseCore 0:
  10.9 65.8 all-gather.2
  152.5 19.9 reduce-scatter.3
  194.9 17.9 reduce-scatter.7
  215.1 19.9 reduce-scatter.5

commit v4 on v3

--- a/solution.py
+++ b/solution.py
@@ -1086,18 +1086,20 @@
                 top_kernel, hidden_outs, place, [grad_state] + tail
             )
         else:
-            own, far = halve(place, [grads])
+            head_own, head_far = halve(place, [grads])
             grad_state, sums_in, partial, bias_mlp[0], b_first[0], *grads = run(
                 lower_kernel(0),
                 [(square, f32), ((2, 512), f32)] + hidden_outs,
                 place,
                 [grad_mid, partial, swap_tp(partial), saved[1][0]] + small_parts + tail,
-                after=[own],
+                after=[head_own],
             )
-            both = quarter(place, own, far, after=[partial])
+        own, far = halve(place, [grads])
+        behind = [own]
+        if layer == 0:
+            both = quarter(place, head_own, head_far, after=[own])
             heads_sum = lax.psum_scatter(both, "shard", scatter_dimension=0)
-        own, far = halve(place, [grads])
-        behind = [own] if layer == 1 else [both, own]
+            behind = [both]
         grad_mid, sums_mid[layer], gw_out, dq, keep, send = run(
             attend_back_kernel(layer),
             [
@@ -1156,7 +1158,7 @@
         [((304, lanes), bf16)],
         place,
         [pieces[0]] + got,
-        after=upper[1:],
+        after=upper[1:3],
     )
     last_parts = collect(last)
     outs_heads = heads_out(place, upper, 1, w_qkv.shape, w_proj.shape, [], 1024, after=[last])

time: 290 us -> 283 us (0.976)
  waiting for transfers between devices: 105 us -> 95.3 us
    ppermute x11, waiting for transfers between devices: 49.6 us -> 40.5 us  [swap_x(): return lax.ppermute(values, 'ctx', [(0, 2), (2, 0), (1, 3), (3, 1)])]
  transfers between devices with their start and end apart: 50 -> 50, of which waited for: 31 -> 30; matrix products, arithmetic and copies ran while one was open for 3% -> 4% of each run, Pallas kernels for 25% -> 23%
where the time goes in v4:
time: 283 us; the launch traced here: 281 us
  Pallas kernels  101 us (36%)
  waiting for transfers between devices  95.3 us (34%)
  starting transfers between devices  36.6 us (13%)
  local copies, waits for them, and re-layouts  27.5 us (10%)
  between operations  16.8 us (6%)
  other arithmetic  3.77 us (1%)
    pallas_call x28, Pallas kernels, run(): return list(call(place, *arrays))  93.4 us
    ppermute x11, waiting for transfers between devices, swap_x(): return lax.ppermute(values, 'ctx', [(0, 2), (2, 0), (1, 3), (3, 1)])  40.5 us
    ppermute x9, waiting for transfers between devices, swap_tp(): return lax.ppermute(values, 'tp', [(0, 1), (1, 0)])  32.9 us
    unnamed x102, local copies, waits for them, and re-layouts  19.3 us
    ppermute x11, starting transfers between devices, swap_x(): return lax.ppermute(values, 'ctx', [(0, 2), (2, 0), (1, 3), (3, 1)])  11.5 us
    ppermute x6, starting transfers between devices, shift(): lax.ppermute(values, 'shard', [(z, (z + step) % 4) for z in range(4)])  11.2 us
    ppermute x9, starting transfers between devices, swap_tp(): return lax.ppermute(values, 'tp', [(0, 1), (1, 0)])  10.7 us
    ppermute x6, waiting for transfers between devices, shift(): lax.ppermute(values, 'shard', [(z, (z + step) % 4) for z in range(4)])  8.94 us
  transfers between devices with their start and end apart: 50, of which 30 were waited for; matrix products, arithmetic and copies ran while one was open for 4% of the time, Pallas kernels for 23%

profile of v4, /device:TPU:0, one launch (start us, length us, event | category | flops | bytes accessed | tf_op | source)
XLA Modules:
  0.0 281.4 jit_solution(15140597976583785741)
XLA Ops:
  14.7 3.0 %collective-permute-start.1 = (bf16[288,128]{1,0:T(8,128)(2,1)}, bf16[288,128]{1,0:T(8,128)(2,1)S(1)}, u32[]{:S(2)}, u32[]{:S(2)}) collective-permute-start(bf16[288,128]{1,0:T(8,128)(2,1)} %get-tuple-element.102), channel_id=1, source_target_pairs={{0,8},{8,16},{16,24},{24,0},{1,9},{9,17},{17,25},{25,1},{2,10},{10... | collective-permute-start | bytes 221192 | tf_op jit(solution)/shard_map/ppermute | solution.py:563
  39.5 3.1 %shard_map.179 = (f32[256,512]{1,0:T(8,128)}, bf16[256,512]{1,0:T(8,128)(2,1)}, bf16[256,256]{1,0:T(8,128)(2,1)}, bf16[256,512]{1,0:T(8,128)(2,1)}, bf16[4,4,32,768]{3,2,1,0:T(8,128)(2,1)}, /*index=5*/f32[256,512]{1,0:T(8,128)}) custom-call(s32[3]{0:T(128)} %pad_add_fusion.refs_0_, bf16[256,512]{1,0:T(8,128)(2,1)} %copy-done.10, ...), custom_call_target="tpu_custom_call" | custom-call | flops 1048576 | bytes 1024 | tf_op jit(solution)/shard_map/pallas_call | solution.py:405
  43.3 12.1 %collective-permute-done.8.refs_4_.refs_12_ = bf16[256,512]{1,0:T(8,128)(2,1)S(1)} collective-permute-done((bf16[256,512]{1,0:T(8,128)(2,1)}, bf16[256,512]{1,0:T(8,128)(2,1)S(1)}, u32[]{:S(2)}, u32[]{:S(2)}) %collective-permute-start.8) | collective-permute-done | bytes 262176 | tf_op jit(solution)/shard_map/ppermute | solution.py:84
  57.6 4.8 %shard_map.180 = (bf16[256,256]{1,0:T(8,128)(2,1)}, f32[256,128]{1,0:T(8,128)}, bf16[256,512]{1,0:T(8,128)(2,1)}, bf16[4,64,512]{2,1,0:T(8,128)(2,1)}) custom-call(s32[3]{0:T(128)} %pad_add_fusion.refs_0_, bf16[256,256]{1,0:T(8,128)(2,1)} %get-tuple-element.104.refs_1_.refs_9_, bf16[256,512]{1,0:T(8,128)(2,1)} %get-tuple-element.105.refs_2_.refs_10_, ...), custom_call_target="tpu_custom_call" | custom-call | flops 1048576 | bytes 1024 | tf_op jit(solution)/shard_map/pallas_call | solution.py:405
  63.9 6.9 %collective-permute-done.10.refs_3_ = bf16[256,512]{1,0:T(8,128)(2,1)S(1)} collective-permute-done((bf16[256,512]{1,0:T(8,128)(2,1)}, bf16[256,512]{1,0:T(8,128)(2,1)S(1)}, u32[]{:S(2)}, u32[]{:S(2)}) %collective-permute-start.10) | collective-permute-done | bytes 262176 | tf_op jit(solution)/shard_map/ppermute | solution.py:76
  70.9 5.9 %all-gather.3.cloned.1.call-done = bf16[20480,128]{1,0:T(8,128)(2,1)} async-done(((bf16[1280,128]{1,0:T(8,128)(2,1)}), bf16[20480,128]{1,0:T(8,128)(2,1)}) %all-gather.3.cloned.1.call-update) | async-done | bytes 5242896 | tf_op jit(solution)/shard_map/all_gather | solution.py:554
  76.8 4.3 %shard_map.182 = (f32[256,512]{1,0:T(8,128)}, bf16[256,512]{1,0:T(8,128)(2,1)}, f32[256,1024]{1,0:T(8,128)}, bf16[256,512]{1,0:T(8,128)(2,1)}) custom-call(s32[3]{0:T(128)} %pad_add_fusion.refs_0_, f32[256,512]{1,0:T(8,128)} %get-tuple-element.103.refs_1_.refs_4_, bf16[256,512]{1,0:T(8,128)(2,1)} %get-tuple-element.106.refs_2_, bf16[256,512]{1,0:T(8,128)(2,1)} %copy-done.38, ...), custom_call_target="tpu_custom_call" | custom-call | flops 1048576 | bytes 1024 | tf_op jit(solution)/shard_map/pallas_call | solution.py:405
  82.5 7.2 %collective-permute-done.11.refs_3_ = bf16[256,512]{1,0:T(8,128)(2,1)S(1)} collective-permute-done((bf16[256,512]{1,0:T(8,128)(2,1)}, bf16[256,512]{1,0:T(8,128)(2,1)S(1)}, u32[]{:S(2)}, u32[]{:S(2)}) %collective-permute-start.11) | collective-permute-done | bytes 262176 | tf_op jit(solution)/shard_map/ppermute | solution.py:76
  90.4 3.2 %shard_map.183 = (f32[256,512]{1,0:T(8,128)}, bf16[256,512]{1,0:T(8,128)(2,1)}, bf16[256,256]{1,0:T(8,128)(2,1)}, bf16[256,512]{1,0:T(8,128)(2,1)}, bf16[4,4,32,768]{3,2,1,0:T(8,128)(2,1)}) custom-call(s32[3]{0:T(128)} %pad_add_fusion.refs_0_, f32[256,512]{1,0:T(8,128)} %get-tuple-element.107.refs_1_.refs_3_, bf16[256,512]{1,0:T(8,128)(2,1)} %get-tuple-element.108.refs_2_, ...), custom_call_target="tpu_custom_call" | custom-call | flops 1048576 | bytes 1024 | tf_op jit(solution)/shard_map/pallas_call | solution.py:405
  94.5 7.1 %collective-permute-done.13.refs_4_.refs_12_ = bf16[256,512]{1,0:T(8,128)(2,1)S(1)} collective-permute-done((bf16[256,512]{1,0:T(8,128)(2,1)}, bf16[256,512]{1,0:T(8,128)(2,1)S(1)}, u32[]{:S(2)}, u32[]{:S(2)}) %collective-permute-start.13) | collective-permute-done | bytes 262176 | tf_op jit(solution)/shard_map/ppermute | solution.py:84
  103.7 4.9 %shard_map.184 = (bf16[256,256]{1,0:T(8,128)(2,1)}, f32[256,128]{1,0:T(8,128)}, bf16[256,512]{1,0:T(8,128)(2,1)}, bf16[4,64,512]{2,1,0:T(8,128)(2,1)}) custom-call(s32[3]{0:T(128)} %pad_add_fusion.refs_0_, bf16[256,256]{1,0:T(8,128)(2,1)} %get-tuple-element.110.refs_1_.refs_9_, bf16[256,512]{1,0:T(8,128)(2,1)} %get-tuple-element.111.refs_2_.refs_10_, ...), custom_call_target="tpu_custom_call" | custom-call | flops 1048576 | bytes 1024 | tf_op jit(solution)/shard_map/pallas_call | solution.py:405
  110.2 7.1 %collective-permute-done.15.refs_3_ = bf16[256,512]{1,0:T(8,128)(2,1)S(1)} collective-permute-done((bf16[256,512]{1,0:T(8,128)(2,1)}, bf16[256,512]{1,0:T(8,128)(2,1)S(1)}, u32[]{:S(2)}, u32[]{:S(2)}) %collective-permute-start.15) | collective-permute-done | bytes 262176 | tf_op jit(solution)/shard_map/ppermute | solution.py:76
  117.9 4.3 %shard_map.185 = (f32[256,512]{1,0:T(8,128)}, bf16[256,512]{1,0:T(8,128)(2,1)}, f32[256,1024]{1,0:T(8,128)}, bf16[256,512]{1,0:T(8,128)(2,1)}) custom-call(s32[3]{0:T(128)} %pad_add_fusion.refs_0_, f32[256,512]{1,0:T(8,128)} %get-tuple-element.109.refs_1_.refs_4_, bf16[256,512]{1,0:T(8,128)(2,1)} %get-tuple-element.112.refs_2_, bf16[256,512]{1,0:T(8,128)(2,1)} %copy-done.39, ...), custom_call_target="tpu_custom_call" | custom-call | flops 1048576 | bytes 1024 | tf_op jit(solution)/shard_map/pallas_call | solution.py:405
  122.2 5.3 %shard_map.186 = (bf16[256,512]{1,0:T(8,128)(2,1)}, f32[1,512]{1,0:T(1,128)}, f32[4,1,256]{2,1,0:T(1,128)}, bf16[2,4,512,128]{3,2,1,0:T(8,128)(2,1)}, bf16[4,512...) custom-call(s32[3]{0:T(128)} %pad_add_fusion.refs_0_, f32[256,512]{1,0:T(8,128)} %get-tuple-element.115.refs_1_.refs_4_, ...), custom_call_target="tpu_custom_call" | custom-call | flops 1048576 | bytes 1024 | tf_op jit(solution)/shard_map/pallas_call | solution.py:405
  137.3 9.2 %shard_map.188 = (f32[256,512]{1,0:T(8,128)}, f32[3,512]{1,0:T(4,128)}, bf16[4,64,512]{2,1,0:T(8,128)(2,1)}, bf16[256,256]{1,0:T(8,128)(2,1)}, bf16[2,256,512]{2...) custom-call(s32[3]{0:T(128)} %pad_add_fusion.refs_0_, bf16[256,512]{1,0:T(8,128)(2,1)} %get-tuple-element.118.refs_1_, ...), custom_call_target="tpu_custom_call" | custom-call | flops 1048576 | bytes 1024 | tf_op jit(solution)/shard_map/pallas_call | solution.py:405
  157.4 6.6 %collective-permute-done.22.refs_3_ = bf16[256,512]{1,0:T(8,128)(2,1)S(1)} collective-permute-done((bf16[256,512]{1,0:T(8,128)(2,1)}, bf16[256,512]{1,0:T(8,128)(2,1)S(1)}, u32[]{:S(2)}, u32[]{:S(2)}) %collective-permute-start.22) | collective-permute-done | bytes 262176 | tf_op jit(solution)/shard_map/ppermute | solution.py:84
  164.6 3.1 %shard_map.191 = (bf16[256,512]{1,0:T(8,128)(2,1)}, f32[2,256]{1,0:T(2,128)}, bf16[2,4,256,128]{3,2,1,0:T(8,128)(2,1)}, bf16[4,256,128]{2,1,0:T(8,128)(2,1)}, bf16[4,256,128]{2,1,0:T(8,128)(2,1)}) custom-call(s32[3]{0:T(128)} %pad_add_fusion.refs_0_, bf16[256,256]{1,0:T(8,128)(2,1)} %get-tuple-element.127.refs_1_, ...), custom_call_target="tpu_custom_call" | custom-call | flops 1048576 | bytes 1024 | tf_op jit(solution)/shard_map/pallas_call | solution.py:405
  172.7 4.0 %collective-permute-done.23.refs_3_ = bf16[256,512]{1,0:T(8,128)(2,1)S(1)} collective-permute-done((bf16[256,512]{1,0:T(8,128)(2,1)}, bf16[256,512]{1,0:T(8,128)(2,1)S(1)}, u32[]{:S(2)}, u32[]{:S(2)}) %collective-permute-start.23) | collective-permute-done | bytes 262176 | tf_op jit(solution)/shard_map/ppermute | solution.py:76
  177.4 6.0 %shard_map.193 = (f32[256,512]{1,0:T(8,128)}, f32[2,512]{1,0:T(2,128)}, bf16[256,512]{1,0:T(8,128)(2,1)}, f32[1,512]{1,0:T(1,128)}, f32[4,1,256]{2,1,0:T(1,128)}...) custom-call(s32[3]{0:T(128)} %pad_add_fusion.refs_0_, ...), custom_call_target="tpu_custom_call" | custom-call | flops 1048576 | bytes 1024 | tf_op jit(solution)/shard_map/pallas_call | solution.py:405
  195.8 9.2 %shard_map.196 = (f32[256,512]{1,0:T(8,128)}, f32[3,512]{1,0:T(4,128)}, bf16[4,64,512]{2,1,0:T(8,128)(2,1)}, bf16[256,256]{1,0:T(8,128)(2,1)}, bf16[2,256,512]{2...) custom-call(s32[3]{0:T(128)} %pad_add_fusion.refs_0_, bf16[256,512]{1,0:T(8,128)(2,1)} %get-tuple-element.143.refs_1_, ...), custom_call_target="tpu_custom_call" | custom-call | flops 1048576 | bytes 1024 | tf_op jit(solution)/shard_map/pallas_call | solution.py:405
  211.9 7.9 %collective-permute-done.32.refs_3_ = bf16[256,512]{1,0:T(8,128)(2,1)S(1)} collective-permute-done((bf16[256,512]{1,0:T(8,128)(2,1)}, bf16[256,512]{1,0:T(8,128)(2,1)S(1)}, u32[]{:S(2)}, u32[]{:S(2)}) %collective-permute-start.32) | collective-permute-done | bytes 262176 | tf_op jit(solution)/shard_map/ppermute | solution.py:84
  220.6 3.1 %shard_map.199 = (bf16[256,512]{1,0:T(8,128)(2,1)}, f32[2,256]{1,0:T(2,128)}, bf16[2,4,256,128]{3,2,1,0:T(8,128)(2,1)}, bf16[4,256,128]{2,1,0:T(8,128)(2,1)}, bf16[4,256,128]{2,1,0:T(8,128)(2,1)}) custom-call(s32[3]{0:T(128)} %pad_add_fusion.refs_0_, bf16[256,256]{1,0:T(8,128)(2,1)} %get-tuple-element.154.refs_1_, ...), custom_call_target="tpu_custom_call" | custom-call | flops 1048576 | bytes 1024 | tf_op jit(solution)/shard_map/pallas_call | solution.py:405
  229.5 3.1 %collective-permute-done.33.refs_3_ = bf16[256,512]{1,0:T(8,128)(2,1)S(1)} collective-permute-done((bf16[256,512]{1,0:T(8,128)(2,1)}, bf16[256,512]{1,0:T(8,128)(2,1)S(1)}, u32[]{:S(2)}, u32[]{:S(2)}) %collective-permute-start.33) | collective-permute-done | bytes 262176 | tf_op jit(solution)/shard_map/ppermute | solution.py:76
  247.1 6.2 %collective-permute-done.38.refs_3_ = bf16[304,128]{1,0:T(8,128)(2,1)S(1)} collective-permute-done((bf16[304,128]{1,0:T(8,128)(2,1)}, bf16[304,128]{1,0:T(8,128)(2,1)S(1)}, u32[]{:S(2)}, u32[]{:S(2)}) %collective-permute-start.38) | collective-permute-done | bytes 77856 | tf_op jit(solution)/shard_map/ppermute | solution.py:563
  (240 shorter events, 127.2 us)
Async XLA Ops:
  7.2 69.6 %all-gather.3.cloned.1.call-start = ((), (), s32[]{:S(2)}) async-start(), calls=%async_computation.6 | async-start | bytes 5570560 | tf_op jit(solution)/shard_map/all_gather | solution.py:554
  10.0 229.6 %reduce-scatter.4.cloned.1.call-start = ((), (), s32[]{:S(2)}) async-start(), calls=%async_computation.3 | async-start | bytes 655360 | tf_op jit(solution)/shard_map/reduce_scatter | solution.py:1118
  14.7 10.2 %collective-permute-start.1 = (bf16[288,128]{1,0:T(8,128)(2,1)}, bf16[288,128]{1,0:T(8,128)(2,1)S(1)}, u32[]{:S(2)}, u32[]{:S(2)}) collective-permute-start(bf16[288,128]{1,0:T(8,128)(2,1)} %get-tuple-element.102), channel_id=1, source_target_pairs={{0,8},{8,16},{16,24},{24,0},{1,9},{9,17},{17,25},{25,1},{2,10},{10... | collective-permute-start | bytes 221192 | tf_op jit(solution)/shard_map/ppermute | solution.py:563
  42.6 12.7 %collective-permute-start.8 = (bf16[256,512]{1,0:T(8,128)(2,1)}, bf16[256,512]{1,0:T(8,128)(2,1)S(1)}, u32[]{:S(2)}, u32[]{:S(2)}) collective-permute-start(bf16[256,512]{1,0:T(8,128)(2,1)} %get-tuple-element.105.refs_2_.refs_10_), channel_id=1, source_target_pairs={{0,4},{4,0},{2,6},{6,2},{1,5},{5,1},{3,7},{7,3},{8,12},{12,8},{10,... | collective-permute-start | bytes 786440 | tf_op jit(solution)/shard_map/ppermute | solution.py:84
  43.3 12.1 %collective-permute-start.7 = (bf16[256,512]{1,0:T(8,128)(2,1)}, bf16[256,512]{1,0:T(8,128)(2,1)S(1)}, u32[]{:S(2)}, u32[]{:S(2)}) collective-permute-start(bf16[256,512]{1,0:T(8,128)(2,1)} %get-tuple-element.105.refs_2_.refs_10_), channel_id=1, source_target_pairs={{0,2},{2,0},{4,6},{6,4},{1,3},{3,1},{5,7},{7,5},{8,10},{10,8},{12,... | collective-permute-start | bytes 786440 | tf_op jit(solution)/shard_map/ppermute | solution.py:80
  62.3 8.6 %collective-permute-start.10 = (bf16[256,512]{1,0:T(8,128)(2,1)}, bf16[256,512]{1,0:T(8,128)(2,1)S(1)}, u32[]{:S(2)}, u32[]{:S(2)}) collective-permute-start(bf16[256,512]{1,0:T(8,128)(2,1)} %get-tuple-element.106.refs_2_), channel_id=1, source_target_pairs={{0,1},{1,0},{2,3},{3,2},{4,5},{5,4},{6,7},{7,6},{8,9},{9,8},{10,11... | collective-permute-start | bytes 786440 | tf_op jit(solution)/shard_map/ppermute | solution.py:76
  81.0 8.7 %collective-permute-start.11 = (bf16[256,512]{1,0:T(8,128)(2,1)}, bf16[256,512]{1,0:T(8,128)(2,1)S(1)}, u32[]{:S(2)}, u32[]{:S(2)}) collective-permute-start(bf16[256,512]{1,0:T(8,128)(2,1)} %get-tuple-element.108.refs_2_), channel_id=1, source_target_pairs={{0,1},{1,0},{2,3},{3,2},{4,5},{5,4},{6,7},{7,6},{8,9},{9,8},{10,11... | collective-permute-start | bytes 786440 | tf_op jit(solution)/shard_map/ppermute | solution.py:76
  108.7 8.6 %collective-permute-start.15 = (bf16[256,512]{1,0:T(8,128)(2,1)}, bf16[256,512]{1,0:T(8,128)(2,1)S(1)}, u32[]{:S(2)}, u32[]{:S(2)}) collective-permute-start(bf16[256,512]{1,0:T(8,128)(2,1)} %get-tuple-element.112.refs_2_), channel_id=1, source_target_pairs={{0,1},{1,0},{2,3},{3,2},{4,5},{5,4},{6,7},{7,6},{8,9},{9,8},{10,11... | collective-permute-start | bytes 786440 | tf_op jit(solution)/shard_map/ppermute | solution.py:76
  128.1 8.5 %collective-permute-start.17 = (bf16[256,512]{1,0:T(8,128)(2,1)}, bf16[256,512]{1,0:T(8,128)(2,1)S(1)}, u32[]{:S(2)}, u32[]{:S(2)}) collective-permute-start(bf16[256,512]{1,0:T(8,128)(2,1)} %get-tuple-element.118.refs_1_), channel_id=1, source_target_pairs={{0,1},{1,0},{2,3},{3,2},{4,5},{5,4},{6,7},{7,6},{8,9},{9,8},{10,11... | collective-permute-start | bytes 786440 | tf_op jit(solution)/shard_map/ppermute | solution.py:76
  134.0 15.4 %collective-permute-start.21 = (bf16[4,512,128]{2,1,0:T(8,128)(2,1)}, bf16[4,512,128]{2,1,0:T(8,128)(2,1)S(1)}, u32[]{:S(2)}, u32[]{:S(2)}) collective-permute-start(bf16[4,512,128]{2,1,0:T(8,128)(2,1)} %get-tuple-element.130), channel_id=1, source_target_pairs={{0,4},{4,0},{2,6},{6,2},{1,5},{5,1},{3,7},{7,3},{8,12},{12,8},{10,... | collective-permute-start | bytes 1572872 | tf_op jit(solution)/shard_map/ppermute | solution.py:84
  146.5 9.8 %collective-permute-start.16 = (bf16[128,512]{1,0:T(8,128)(2,1)S(1)}, bf16[128,512]{1,0:T(8,128)(2,1)S(1)}, u32[]{:S(2)}, u32[]{:S(2)}) collective-permute-start(bf16[128,512]{1,0:T(8,128)(2,1)S(1)} %slice.65), channel_id=1, source_target_pairs={{0,1},{1,0},{2,3},{3,2},{4,5},{5,4},{6,7},{7,6},{8,9},{9,8},{10,11... | collective-permute-start | bytes 393224 | tf_op jit(solution)/shard_map/ppermute | solution.py:76
  152.4 87.2 %reduce-scatter.8.cloned.1.call-start = ((), (), s32[]{:S(2)}) async-start(), calls=%async_computation.5 | async-start | bytes 327680 | tf_op jit(solution)/shard_map/reduce_scatter | solution.py:1101
  155.3 8.6 %collective-permute-start.22 = (bf16[256,512]{1,0:T(8,128)(2,1)}, bf16[256,512]{1,0:T(8,128)(2,1)S(1)}, u32[]{:S(2)}, u32[]{:S(2)}) collective-permute-start(bf16[256,512]{1,0:T(8,128)(2,1)} %get-tuple-element.132), channel_id=1, source_target_pairs={{0,4},{4,0},{2,6},{6,2},{1,5},{5,1},{3,7},{7,3},{8,12},{12,8},{10,... | collective-permute-start | bytes 786440 | tf_op jit(solution)/shard_map/ppermute | solution.py:84
  168.3 8.4 %collective-permute-start.23 = (bf16[256,512]{1,0:T(8,128)(2,1)}, bf16[256,512]{1,0:T(8,128)(2,1)S(1)}, u32[]{:S(2)}, u32[]{:S(2)}) collective-permute-start(bf16[256,512]{1,0:T(8,128)(2,1)} %get-tuple-element.136.refs_2_), channel_id=1, source_target_pairs={{0,1},{1,0},{2,3},{3,2},{4,5},{5,4},{6,7},{7,6},{8,9},{9,8},{10,11... | collective-permute-start | bytes 786440 | tf_op jit(solution)/shard_map/ppermute | solution.py:76
  184.0 8.3 %collective-permute-start.27 = (bf16[4,256,128]{2,1,0:T(8,128)(2,1)S(1)}, bf16[4,256,128]{2,1,0:T(8,128)(2,1)S(1)}, u32[]{:S(2)}, u32[]{:S(2)}) collective-permute-start(bf16[4,256,128]{2,1,0:T(8,128)(2,1)S(1)} %copy-done.49), channel_id=1, source_target_pairs={{0,4},{4,0},{2,6},{6,2},{1,5},{5,1},{3,7},{7,3},{8,12},{12,8},{10,... | collective-permute-start | bytes 786440 | tf_op jit(solution)/shard_map/ppermute | solution.py:84
  185.0 10.1 %collective-permute-start.26 = (bf16[256,512]{1,0:T(8,128)(2,1)}, bf16[256,512]{1,0:T(8,128)(2,1)S(1)}, u32[]{:S(2)}, u32[]{:S(2)}) collective-permute-start(bf16[256,512]{1,0:T(8,128)(2,1)} %get-tuple-element.143.refs_1_), channel_id=1, source_target_pairs={{0,1},{1,0},{2,3},{3,2},{4,5},{5,4},{6,7},{7,6},{8,9},{9,8},{10,11... | collective-permute-start | bytes 786440 | tf_op jit(solution)/shard_map/ppermute | solution.py:76
  189.8 15.2 %collective-permute-start.31 = (bf16[4,512,128]{2,1,0:T(8,128)(2,1)}, bf16[4,512,128]{2,1,0:T(8,128)(2,1)S(1)}, u32[]{:S(2)}, u32[]{:S(2)}) collective-permute-start(bf16[4,512,128]{2,1,0:T(8,128)(2,1)} %get-tuple-element.157), channel_id=1, source_target_pairs={{0,4},{4,0},{2,6},{6,2},{1,5},{5,1},{3,7},{7,3},{8,12},{12,8},{10,... | collective-permute-start | bytes 1572872 | tf_op jit(solution)/shard_map/ppermute | solution.py:84
  194.8 44.8 %reduce-scatter.6.cloned.1.call-start = ((), (), s32[]{:S(2)}) async-start(), calls=%async_computation.4 | async-start | bytes 655360 | tf_op jit(solution)/shard_map/reduce_scatter | solution.py:1118
  210.9 8.9 %collective-permute-start.32 = (bf16[256,512]{1,0:T(8,128)(2,1)}, bf16[256,512]{1,0:T(8,128)(2,1)S(1)}, u32[]{:S(2)}, u32[]{:S(2)}) collective-permute-start(bf16[256,512]{1,0:T(8,128)(2,1)} %get-tuple-element.159), channel_id=1, source_target_pairs={{0,4},{4,0},{2,6},{6,2},{1,5},{5,1},{3,7},{7,3},{8,12},{12,8},{10,... | collective-permute-start | bytes 786440 | tf_op jit(solution)/shard_map/ppermute | solution.py:84
  224.2 8.4 %collective-permute-start.33 = (bf16[256,512]{1,0:T(8,128)(2,1)}, bf16[256,512]{1,0:T(8,128)(2,1)S(1)}, u32[]{:S(2)}, u32[]{:S(2)}) collective-permute-start(bf16[256,512]{1,0:T(8,128)(2,1)} %get-tuple-element.163.refs_2_), channel_id=1, source_target_pairs={{0,1},{1,0},{2,3},{3,2},{4,5},{5,4},{6,7},{7,6},{8,9},{9,8},{10,11... | collective-permute-start | bytes 786440 | tf_op jit(solution)/shard_map/ppermute | solution.py:76
  228.5 8.6 %collective-permute-start.36 = (bf16[4,256,128]{2,1,0:T(8,128)(2,1)}, bf16[4,256,128]{2,1,0:T(8,128)(2,1)S(1)}, u32[]{:S(2)}, u32[]{:S(2)}) collective-permute-start(bf16[4,256,128]{2,1,0:T(8,128)(2,1)} %get-tuple-element.178), channel_id=1, source_target_pairs={{0,4},{4,0},{2,6},{6,2},{1,5},{5,1},{3,7},{7,3},{8,12},{12,8},{10,... | collective-permute-start | bytes 786440 | tf_op jit(solution)/shard_map/ppermute | solution.py:84
  241.4 11.9 %collective-permute-start.40 = (bf16[1280,128]{1,0:T(8,128)(2,1)}, bf16[1280,128]{1,0:T(8,128)(2,1)S(1)}, u32[]{:S(2)}, u32[]{:S(2)}) collective-permute-start(bf16[1280,128]{1,0:T(8,128)(2,1)} %shard_map.203.refs_1_), channel_id=1, source_target_pairs={{0,2},{2,0},{4,6},{6,4},{1,3},{3,1},{5,7},{7,5},{8,10},{10,8},{12,... | collective-permute-start | bytes 983048 | tf_op jit(solution)/shard_map/ppermute | solution.py:80
  241.4 11.9 %collective-permute-start.41 = (bf16[1280,128]{1,0:T(8,128)(2,1)}, bf16[1280,128]{1,0:T(8,128)(2,1)S(1)}, u32[]{:S(2)}, u32[]{:S(2)}) collective-permute-start(bf16[1280,128]{1,0:T(8,128)(2,1)} %shard_map.203.refs_1_), channel_id=1, source_target_pairs={{0,4},{4,0},{2,6},{6,2},{1,5},{5,1},{3,7},{7,3},{8,12},{12,8},{10,... | collective-permute-start | bytes 983048 | tf_op jit(solution)/shard_map/ppermute | solution.py:84
  243.6 9.7 %collective-permute-start.38 = (bf16[304,128]{1,0:T(8,128)(2,1)}, bf16[304,128]{1,0:T(8,128)(2,1)S(1)}, u32[]{:S(2)}, u32[]{:S(2)}) collective-permute-start(bf16[304,128]{1,0:T(8,128)(2,1)} %get-tuple-element.182), channel_id=1, source_target_pairs={{0,16},{8,24},{16,0},{24,8},{1,17},{9,25},{17,1},{25,9},{2,18},{10... | collective-permute-start | bytes 233480 | tf_op jit(solution)/shard_map/ppermute | solution.py:563
  (76 other events, 265.4 us)
Sparse Core Ops, SparseCore 0:
  10.9 65.8 all-gather.2
  152.5 19.9 reduce-scatter.3
  194.9 17.9 reduce-scatter.7
  215.1 19.9 reduce-scatter.5

commit v5 on v4

--- a/solution.py
+++ b/solution.py
@@ -875,6 +875,11 @@
 def last_total_kernel(place, own, one, two, three, out):
     total = own[...].astype(f32) + one[...].astype(f32)
     out[...] = (total + (two[...].astype(f32) + three[...].astype(f32))).astype(bf16)
+
+
+def small_kernel(place, one, two, three, four, out):
+    total = one[256:].astype(f32) + two[256:].astype(f32)
+    out[...] = total + (three[256:].astype(f32) + four[256:].astype(f32))
 
 
 def halve(place, groups, after=()):
@@ -1166,7 +1171,7 @@
     grad_fc1, grad_fc2 = hidden_out(
         place, upper, 0, w_fc1.shape, w_fc2.shape, outs_hidden, 512, after=[last]
     )
-    total = sum(part[256:].astype(f32) for part in last_parts)
+    (total,) = run(small_kernel, [((48, lanes), f32)], place, last_parts, after=[grad_fc1])
     grad_gains = total[:4].reshape(gains.shape)
     grad_biases = total[4:12].reshape(biases.shape)
     rest_q = total[12:20].reshape(2, 2, 4, 64)
@@ -1174,7 +1179,7 @@
     grad_b_qv = lax.dynamic_slice_in_dim(rest_q, z * 16, 16, 3)
     grad_b_fc1 = lax.dynamic_slice_in_dim(rest_f, z * 16, 16, 2)
 
-    grad_qkv, grad_proj = heads_out(place, last_parts, 0, w_qkv.shape, w_proj.shape, outs_heads, 0)
+    grad_qkv, grad_proj = heads_out(place, last_parts, 0, w_qkv.shape, w_proj.shape, outs_heads, 0, after=[grad_fc1])
     return (
         output, grad_x, grad_qkv, grad_b_qv, grad_proj, grad_fc1, grad_b_fc1, grad_fc2, grad_gains, grad_biases
     )

time: 283 us -> 295 us (1.042)
  waiting for transfers between devices: 95.3 us -> 105 us
    ppermute x11, waiting for transfers between devices: 40.5 us -> 49.6 us  [swap_x(): return lax.ppermute(values, 'ctx', [(0, 2), (2, 0), (1, 3), (3, 1)])]
    pallas_call x28 -> x29, Pallas kernels: 93.4 us -> 95 us  [run(): return list(call(place, *arrays))]
  transfers between devices with their start and end apart: 50 -> 50, of which waited for: 30 -> 31; matrix products, arithmetic and copies ran while one was open for 4% -> 3% of each run, Pallas kernels for 23% -> 25%
where the time goes in v5:
time: 295 us; the launch traced here: 293 us
  waiting for transfers between devices  105 us (36%)
  Pallas kernels  103 us (35%)
  starting transfers between devices  35.6 us (12%)
  local copies, waits for them, and re-layouts  30.1 us (10%)
  between operations  16.8 us (6%)
  other arithmetic  3 us (1%)
    pallas_call x29, Pallas kernels, run(): return list(call(place, *arrays))  95 us
    ppermute x11, waiting for transfers between devices, swap_x(): return lax.ppermute(values, 'ctx', [(0, 2), (2, 0), (1, 3), (3, 1)])  49.6 us
    ppermute x9, waiting for transfers between devices, swap_tp(): return lax.ppermute(values, 'tp', [(0, 1), (1, 0)])  32.9 us
    unnamed x102, local copies, waits for them, and re-layouts  19.9 us
    ppermute x6, starting transfers between devices, shift(): lax.ppermute(values, 'shard', [(z, (z + step) % 4) for z in range(4)])  11.6 us
    ppermute x9, starting transfers between devices, swap_tp(): return lax.ppermute(values, 'tp', [(0, 1), (1, 0)])  10.7 us
    ppermute x11, starting transfers between devices, swap_x(): return lax.ppermute(values, 'ctx', [(0, 2), (2, 0), (1, 3), (3, 1)])  10.6 us
    ppermute x6, waiting for transfers between devices, shift(): lax.ppermute(values, 'shard', [(z, (z + step) % 4) for z in range(4)])  9.24 us
  transfers between devices with their start and end apart: 50, of which 31 were waited for; matrix products, arithmetic and copies ran while one was open for 3% of the time, Pallas kernels for 25%

profile of v5, /device:TPU:0, one launch (start us, length us, event | category | flops | bytes accessed | tf_op | source)
XLA Modules:
  0.0 293.3 jit_solution(11789443724906613217)
XLA Ops:
  39.5 3.1 %shard_map.179 = (f32[256,512]{1,0:T(8,128)}, bf16[256,512]{1,0:T(8,128)(2,1)}, bf16[256,256]{1,0:T(8,128)(2,1)}, bf16[256,512]{1,0:T(8,128)(2,1)}, bf16[4,4,32,768]{3,2,1,0:T(8,128)(2,1)}, /*index=5*/f32[256,512]{1,0:T(8,128)}) custom-call(s32[3]{0:T(128)} %pad_add_fusion.refs_0_, bf16[256,512]{1,0:T(8,128)(2,1)} %copy-done.10, ...), custom_call_target="tpu_custom_call" | custom-call | flops 1048576 | bytes 1024 | tf_op jit(solution)/shard_map/pallas_call | solution.py:405
  43.3 12.1 %collective-permute-done.8.refs_4_.refs_12_ = bf16[256,512]{1,0:T(8,128)(2,1)S(1)} collective-permute-done((bf16[256,512]{1,0:T(8,128)(2,1)}, bf16[256,512]{1,0:T(8,128)(2,1)S(1)}, u32[]{:S(2)}, u32[]{:S(2)}) %collective-permute-start.8) | collective-permute-done | bytes 262176 | tf_op jit(solution)/shard_map/ppermute | solution.py:84
  57.6 4.8 %shard_map.180 = (bf16[256,256]{1,0:T(8,128)(2,1)}, f32[256,128]{1,0:T(8,128)}, bf16[256,512]{1,0:T(8,128)(2,1)}, bf16[4,64,512]{2,1,0:T(8,128)(2,1)}) custom-call(s32[3]{0:T(128)} %pad_add_fusion.refs_0_, bf16[256,256]{1,0:T(8,128)(2,1)} %get-tuple-element.104.refs_1_.refs_9_, bf16[256,512]{1,0:T(8,128)(2,1)} %get-tuple-element.105.refs_2_.refs_10_, ...), custom_call_target="tpu_custom_call" | custom-call | flops 1048576 | bytes 1024 | tf_op jit(solution)/shard_map/pallas_call | solution.py:405
  63.9 6.9 %collective-permute-done.10.refs_3_ = bf16[256,512]{1,0:T(8,128)(2,1)S(1)} collective-permute-done((bf16[256,512]{1,0:T(8,128)(2,1)}, bf16[256,512]{1,0:T(8,128)(2,1)S(1)}, u32[]{:S(2)}, u32[]{:S(2)}) %collective-permute-start.10) | collective-permute-done | bytes 262176 | tf_op jit(solution)/shard_map/ppermute | solution.py:76
  70.9 5.9 %all-gather.3.cloned.1.call-done = bf16[20480,128]{1,0:T(8,128)(2,1)} async-done(((bf16[1280,128]{1,0:T(8,128)(2,1)}), bf16[20480,128]{1,0:T(8,128)(2,1)}) %all-gather.3.cloned.1.call-update) | async-done | bytes 5242896 | tf_op jit(solution)/shard_map/all_gather | solution.py:554
  76.8 4.3 %shard_map.182 = (f32[256,512]{1,0:T(8,128)}, bf16[256,512]{1,0:T(8,128)(2,1)}, f32[256,1024]{1,0:T(8,128)}, bf16[256,512]{1,0:T(8,128)(2,1)}) custom-call(s32[3]{0:T(128)} %pad_add_fusion.refs_0_, f32[256,512]{1,0:T(8,128)} %get-tuple-element.103.refs_1_.refs_4_, bf16[256,512]{1,0:T(8,128)(2,1)} %get-tuple-element.106.refs_2_, bf16[256,512]{1,0:T(8,128)(2,1)} %copy-done.41, ...), custom_call_target="tpu_custom_call" | custom-call | flops 1048576 | bytes 1024 | tf_op jit(solution)/shard_map/pallas_call | solution.py:405
  82.5 7.2 %collective-permute-done.11.refs_3_ = bf16[256,512]{1,0:T(8,128)(2,1)S(1)} collective-permute-done((bf16[256,512]{1,0:T(8,128)(2,1)}, bf16[256,512]{1,0:T(8,128)(2,1)S(1)}, u32[]{:S(2)}, u32[]{:S(2)}) %collective-permute-start.11) | collective-permute-done | bytes 262176 | tf_op jit(solution)/shard_map/ppermute | solution.py:76
  90.4 3.2 %shard_map.183 = (f32[256,512]{1,0:T(8,128)}, bf16[256,512]{1,0:T(8,128)(2,1)}, bf16[256,256]{1,0:T(8,128)(2,1)}, bf16[256,512]{1,0:T(8,128)(2,1)}, bf16[4,4,32,768]{3,2,1,0:T(8,128)(2,1)}) custom-call(s32[3]{0:T(128)} %pad_add_fusion.refs_0_, f32[256,512]{1,0:T(8,128)} %get-tuple-element.107.refs_1_.refs_3_, bf16[256,512]{1,0:T(8,128)(2,1)} %get-tuple-element.108.refs_2_, ...), custom_call_target="tpu_custom_call" | custom-call | flops 1048576 | bytes 1024 | tf_op jit(solution)/shard_map/pallas_call | solution.py:405
  94.5 7.1 %collective-permute-done.13.refs_4_.refs_12_ = bf16[256,512]{1,0:T(8,128)(2,1)S(1)} collective-permute-done((bf16[256,512]{1,0:T(8,128)(2,1)}, bf16[256,512]{1,0:T(8,128)(2,1)S(1)}, u32[]{:S(2)}, u32[]{:S(2)}) %collective-permute-start.13) | collective-permute-done | bytes 262176 | tf_op jit(solution)/shard_map/ppermute | solution.py:84
  103.7 4.9 %shard_map.184 = (bf16[256,256]{1,0:T(8,128)(2,1)}, f32[256,128]{1,0:T(8,128)}, bf16[256,512]{1,0:T(8,128)(2,1)}, bf16[4,64,512]{2,1,0:T(8,128)(2,1)}) custom-call(s32[3]{0:T(128)} %pad_add_fusion.refs_0_, bf16[256,256]{1,0:T(8,128)(2,1)} %get-tuple-element.110.refs_1_.refs_9_, bf16[256,512]{1,0:T(8,128)(2,1)} %get-tuple-element.111.refs_2_.refs_10_, ...), custom_call_target="tpu_custom_call" | custom-call | flops 1048576 | bytes 1024 | tf_op jit(solution)/shard_map/pallas_call | solution.py:405
  110.2 7.1 %collective-permute-done.15.refs_3_ = bf16[256,512]{1,0:T(8,128)(2,1)S(1)} collective-permute-done((bf16[256,512]{1,0:T(8,128)(2,1)}, bf16[256,512]{1,0:T(8,128)(2,1)S(1)}, u32[]{:S(2)}, u32[]{:S(2)}) %collective-permute-start.15) | collective-permute-done | bytes 262176 | tf_op jit(solution)/shard_map/ppermute | solution.py:76
  117.9 4.3 %shard_map.185 = (f32[256,512]{1,0:T(8,128)}, bf16[256,512]{1,0:T(8,128)(2,1)}, f32[256,1024]{1,0:T(8,128)}, bf16[256,512]{1,0:T(8,128)(2,1)}) custom-call(s32[3]{0:T(128)} %pad_add_fusion.refs_0_, f32[256,512]{1,0:T(8,128)} %get-tuple-element.109.refs_1_.refs_4_, bf16[256,512]{1,0:T(8,128)(2,1)} %get-tuple-element.112.refs_2_, bf16[256,512]{1,0:T(8,128)(2,1)} %copy-done.42, ...), custom_call_target="tpu_custom_call" | custom-call | flops 1048576 | bytes 1024 | tf_op jit(solution)/shard_map/pallas_call | solution.py:405
  122.2 5.3 %shard_map.186 = (bf16[256,512]{1,0:T(8,128)(2,1)}, f32[1,512]{1,0:T(1,128)}, f32[4,1,256]{2,1,0:T(1,128)}, bf16[2,4,512,128]{3,2,1,0:T(8,128)(2,1)}, bf16[4,512...) custom-call(s32[3]{0:T(128)} %pad_add_fusion.refs_0_, f32[256,512]{1,0:T(8,128)} %get-tuple-element.115.refs_1_.refs_4_, ...), custom_call_target="tpu_custom_call" | custom-call | flops 1048576 | bytes 1024 | tf_op jit(solution)/shard_map/pallas_call | solution.py:405
  137.3 9.2 %shard_map.188 = (f32[256,512]{1,0:T(8,128)}, f32[3,512]{1,0:T(4,128)}, bf16[4,64,512]{2,1,0:T(8,128)(2,1)}, bf16[256,256]{1,0:T(8,128)(2,1)}, bf16[2,256,512]{2...) custom-call(s32[3]{0:T(128)} %pad_add_fusion.refs_0_, bf16[256,512]{1,0:T(8,128)(2,1)} %get-tuple-element.118.refs_1_, ...), custom_call_target="tpu_custom_call" | custom-call | flops 1048576 | bytes 1024 | tf_op jit(solution)/shard_map/pallas_call | solution.py:405
  157.4 6.6 %collective-permute-done.22.refs_3_ = bf16[256,512]{1,0:T(8,128)(2,1)S(1)} collective-permute-done((bf16[256,512]{1,0:T(8,128)(2,1)}, bf16[256,512]{1,0:T(8,128)(2,1)S(1)}, u32[]{:S(2)}, u32[]{:S(2)}) %collective-permute-start.22) | collective-permute-done | bytes 262176 | tf_op jit(solution)/shard_map/ppermute | solution.py:84
  164.6 3.1 %shard_map.191 = (bf16[256,512]{1,0:T(8,128)(2,1)}, f32[2,256]{1,0:T(2,128)}, bf16[2,4,256,128]{3,2,1,0:T(8,128)(2,1)}, bf16[4,256,128]{2,1,0:T(8,128)(2,1)}, bf16[4,256,128]{2,1,0:T(8,128)(2,1)}) custom-call(s32[3]{0:T(128)} %pad_add_fusion.refs_0_, bf16[256,256]{1,0:T(8,128)(2,1)} %get-tuple-element.127.refs_1_, ...), custom_call_target="tpu_custom_call" | custom-call | flops 1048576 | bytes 1024 | tf_op jit(solution)/shard_map/pallas_call | solution.py:405
  172.7 4.0 %collective-permute-done.23.refs_3_ = bf16[256,512]{1,0:T(8,128)(2,1)S(1)} collective-permute-done((bf16[256,512]{1,0:T(8,128)(2,1)}, bf16[256,512]{1,0:T(8,128)(2,1)S(1)}, u32[]{:S(2)}, u32[]{:S(2)}) %collective-permute-start.23) | collective-permute-done | bytes 262176 | tf_op jit(solution)/shard_map/ppermute | solution.py:76
  177.4 6.0 %shard_map.193 = (f32[256,512]{1,0:T(8,128)}, f32[2,512]{1,0:T(2,128)}, bf16[256,512]{1,0:T(8,128)(2,1)}, f32[1,512]{1,0:T(1,128)}, f32[4,1,256]{2,1,0:T(1,128)}...) custom-call(s32[3]{0:T(128)} %pad_add_fusion.refs_0_, ...), custom_call_target="tpu_custom_call" | custom-call | flops 1048576 | bytes 1024 | tf_op jit(solution)/shard_map/pallas_call | solution.py:405
  195.8 9.2 %shard_map.196 = (f32[256,512]{1,0:T(8,128)}, f32[3,512]{1,0:T(4,128)}, bf16[4,64,512]{2,1,0:T(8,128)(2,1)}, bf16[256,256]{1,0:T(8,128)(2,1)}, bf16[2,256,512]{2...) custom-call(s32[3]{0:T(128)} %pad_add_fusion.refs_0_, bf16[256,512]{1,0:T(8,128)(2,1)} %get-tuple-element.143.refs_1_, ...), custom_call_target="tpu_custom_call" | custom-call | flops 1048576 | bytes 1024 | tf_op jit(solution)/shard_map/pallas_call | solution.py:405
  211.9 7.9 %collective-permute-done.32.refs_3_ = bf16[256,512]{1,0:T(8,128)(2,1)S(1)} collective-permute-done((bf16[256,512]{1,0:T(8,128)(2,1)}, bf16[256,512]{1,0:T(8,128)(2,1)S(1)}, u32[]{:S(2)}, u32[]{:S(2)}) %collective-permute-start.32) | collective-permute-done | bytes 262176 | tf_op jit(solution)/shard_map/ppermute | solution.py:84
  220.6 3.1 %shard_map.199 = (bf16[256,512]{1,0:T(8,128)(2,1)}, f32[2,256]{1,0:T(2,128)}, bf16[2,4,256,128]{3,2,1,0:T(8,128)(2,1)}, bf16[4,256,128]{2,1,0:T(8,128)(2,1)}, bf16[4,256,128]{2,1,0:T(8,128)(2,1)}) custom-call(s32[3]{0:T(128)} %pad_add_fusion.refs_0_, bf16[256,256]{1,0:T(8,128)(2,1)} %get-tuple-element.154.refs_1_, ...), custom_call_target="tpu_custom_call" | custom-call | flops 1048576 | bytes 1024 | tf_op jit(solution)/shard_map/pallas_call | solution.py:405
  229.5 3.1 %collective-permute-done.33.refs_3_ = bf16[256,512]{1,0:T(8,128)(2,1)S(1)} collective-permute-done((bf16[256,512]{1,0:T(8,128)(2,1)}, bf16[256,512]{1,0:T(8,128)(2,1)S(1)}, u32[]{:S(2)}, u32[]{:S(2)}) %collective-permute-start.33) | collective-permute-done | bytes 262176 | tf_op jit(solution)/shard_map/ppermute | solution.py:76
  242.3 8.2 %collective-permute-done.41.refs_6_.refs_3_ = bf16[1280,128]{1,0:T(8,128)(2,1)S(1)} collective-permute-done((bf16[1280,128]{1,0:T(8,128)(2,1)}, bf16[1280,128]{1,0:T(8,128)(2,1)S(1)}, u32[]{:S(2)}, u32[]{:S(2)}) %collective-permute-start.41) | collective-permute-done | bytes 327712 | tf_op jit(solution)/shard_map/ppermute | solution.py:84
  255.9 6.2 %collective-permute-done.38.refs_3_ = bf16[304,128]{1,0:T(8,128)(2,1)S(1)} collective-permute-done((bf16[304,128]{1,0:T(8,128)(2,1)}, bf16[304,128]{1,0:T(8,128)(2,1)S(1)}, u32[]{:S(2)}, u32[]{:S(2)}) %collective-permute-start.38) | collective-permute-done | bytes 77856 | tf_op jit(solution)/shard_map/ppermute | solution.py:563
  (240 shorter events, 133.9 us)
Async XLA Ops:
  7.2 69.6 %all-gather.3.cloned.1.call-start = ((), (), s32[]{:S(2)}) async-start(), calls=%async_computation.6 | async-start | bytes 5570560 | tf_op jit(solution)/shard_map/all_gather | solution.py:554
  10.0 229.6 %reduce-scatter.4.cloned.1.call-start = ((), (), s32[]{:S(2)}) async-start(), calls=%async_computation.3 | async-start | bytes 655360 | tf_op jit(solution)/shard_map/reduce_scatter | solution.py:1123
  14.7 10.2 %collective-permute-start.1 = (bf16[288,128]{1,0:T(8,128)(2,1)}, bf16[288,128]{1,0:T(8,128)(2,1)S(1)}, u32[]{:S(2)}, u32[]{:S(2)}) collective-permute-start(bf16[288,128]{1,0:T(8,128)(2,1)} %get-tuple-element.102), channel_id=1, source_target_pairs={{0,8},{8,16},{16,24},{24,0},{1,9},{9,17},{17,25},{25,1},{2,10},{10... | collective-permute-start | bytes 221192 | tf_op jit(solution)/shard_map/ppermute | solution.py:563
  42.6 12.7 %collective-permute-start.8 = (bf16[256,512]{1,0:T(8,128)(2,1)}, bf16[256,512]{1,0:T(8,128)(2,1)S(1)}, u32[]{:S(2)}, u32[]{:S(2)}) collective-permute-start(bf16[256,512]{1,0:T(8,128)(2,1)} %get-tuple-element.105.refs_2_.refs_10_), channel_id=1, source_target_pairs={{0,4},{4,0},{2,6},{6,2},{1,5},{5,1},{3,7},{7,3},{8,12},{12,8},{10,... | collective-permute-start | bytes 786440 | tf_op jit(solution)/shard_map/ppermute | solution.py:84
  43.3 12.1 %collective-permute-start.7 = (bf16[256,512]{1,0:T(8,128)(2,1)}, bf16[256,512]{1,0:T(8,128)(2,1)S(1)}, u32[]{:S(2)}, u32[]{:S(2)}) collective-permute-start(bf16[256,512]{1,0:T(8,128)(2,1)} %get-tuple-element.105.refs_2_.refs_10_), channel_id=1, source_target_pairs={{0,2},{2,0},{4,6},{6,4},{1,3},{3,1},{5,7},{7,5},{8,10},{10,8},{12,... | collective-permute-start | bytes 786440 | tf_op jit(solution)/shard_map/ppermute | solution.py:80
  62.3 8.6 %collective-permute-start.10 = (bf16[256,512]{1,0:T(8,128)(2,1)}, bf16[256,512]{1,0:T(8,128)(2,1)S(1)}, u32[]{:S(2)}, u32[]{:S(2)}) collective-permute-start(bf16[256,512]{1,0:T(8,128)(2,1)} %get-tuple-element.106.refs_2_), channel_id=1, source_target_pairs={{0,1},{1,0},{2,3},{3,2},{4,5},{5,4},{6,7},{7,6},{8,9},{9,8},{10,11... | collective-permute-start | bytes 786440 | tf_op jit(solution)/shard_map/ppermute | solution.py:76
  81.0 8.7 %collective-permute-start.11 = (bf16[256,512]{1,0:T(8,128)(2,1)}, bf16[256,512]{1,0:T(8,128)(2,1)S(1)}, u32[]{:S(2)}, u32[]{:S(2)}) collective-permute-start(bf16[256,512]{1,0:T(8,128)(2,1)} %get-tuple-element.108.refs_2_), channel_id=1, source_target_pairs={{0,1},{1,0},{2,3},{3,2},{4,5},{5,4},{6,7},{7,6},{8,9},{9,8},{10,11... | collective-permute-start | bytes 786440 | tf_op jit(solution)/shard_map/ppermute | solution.py:76
  108.7 8.6 %collective-permute-start.15 = (bf16[256,512]{1,0:T(8,128)(2,1)}, bf16[256,512]{1,0:T(8,128)(2,1)S(1)}, u32[]{:S(2)}, u32[]{:S(2)}) collective-permute-start(bf16[256,512]{1,0:T(8,128)(2,1)} %get-tuple-element.112.refs_2_), channel_id=1, source_target_pairs={{0,1},{1,0},{2,3},{3,2},{4,5},{5,4},{6,7},{7,6},{8,9},{9,8},{10,11... | collective-permute-start | bytes 786440 | tf_op jit(solution)/shard_map/ppermute | solution.py:76
  128.1 8.5 %collective-permute-start.17 = (bf16[256,512]{1,0:T(8,128)(2,1)}, bf16[256,512]{1,0:T(8,128)(2,1)S(1)}, u32[]{:S(2)}, u32[]{:S(2)}) collective-permute-start(bf16[256,512]{1,0:T(8,128)(2,1)} %get-tuple-element.118.refs_1_), channel_id=1, source_target_pairs={{0,1},{1,0},{2,3},{3,2},{4,5},{5,4},{6,7},{7,6},{8,9},{9,8},{10,11... | collective-permute-start | bytes 786440 | tf_op jit(solution)/shard_map/ppermute | solution.py:76
  134.0 15.4 %collective-permute-start.21 = (bf16[4,512,128]{2,1,0:T(8,128)(2,1)}, bf16[4,512,128]{2,1,0:T(8,128)(2,1)S(1)}, u32[]{:S(2)}, u32[]{:S(2)}) collective-permute-start(bf16[4,512,128]{2,1,0:T(8,128)(2,1)} %get-tuple-element.130), channel_id=1, source_target_pairs={{0,4},{4,0},{2,6},{6,2},{1,5},{5,1},{3,7},{7,3},{8,12},{12,8},{10,... | collective-permute-start | bytes 1572872 | tf_op jit(solution)/shard_map/ppermute | solution.py:84
  146.5 9.8 %collective-permute-start.16 = (bf16[128,512]{1,0:T(8,128)(2,1)S(1)}, bf16[128,512]{1,0:T(8,128)(2,1)S(1)}, u32[]{:S(2)}, u32[]{:S(2)}) collective-permute-start(bf16[128,512]{1,0:T(8,128)(2,1)S(1)} %slice.53), channel_id=1, source_target_pairs={{0,1},{1,0},{2,3},{3,2},{4,5},{5,4},{6,7},{7,6},{8,9},{9,8},{10,11... | collective-permute-start | bytes 393224 | tf_op jit(solution)/shard_map/ppermute | solution.py:76
  152.4 87.2 %reduce-scatter.8.cloned.1.call-start = ((), (), s32[]{:S(2)}) async-start(), calls=%async_computation.5 | async-start | bytes 327680 | tf_op jit(solution)/shard_map/reduce_scatter | solution.py:1106
  155.3 8.6 %collective-permute-start.22 = (bf16[256,512]{1,0:T(8,128)(2,1)}, bf16[256,512]{1,0:T(8,128)(2,1)S(1)}, u32[]{:S(2)}, u32[]{:S(2)}) collective-permute-start(bf16[256,512]{1,0:T(8,128)(2,1)} %get-tuple-element.132), channel_id=1, source_target_pairs={{0,4},{4,0},{2,6},{6,2},{1,5},{5,1},{3,7},{7,3},{8,12},{12,8},{10,... | collective-permute-start | bytes 786440 | tf_op jit(solution)/shard_map/ppermute | solution.py:84
  185.0 10.1 %collective-permute-start.26 = (bf16[256,512]{1,0:T(8,128)(2,1)}, bf16[256,512]{1,0:T(8,128)(2,1)S(1)}, u32[]{:S(2)}, u32[]{:S(2)}) collective-permute-start(bf16[256,512]{1,0:T(8,128)(2,1)} %get-tuple-element.143.refs_1_), channel_id=1, source_target_pairs={{0,1},{1,0},{2,3},{3,2},{4,5},{5,4},{6,7},{7,6},{8,9},{9,8},{10,11... | collective-permute-start | bytes 786440 | tf_op jit(solution)/shard_map/ppermute | solution.py:76
  189.8 15.2 %collective-permute-start.31 = (bf16[4,512,128]{2,1,0:T(8,128)(2,1)}, bf16[4,512,128]{2,1,0:T(8,128)(2,1)S(1)}, u32[]{:S(2)}, u32[]{:S(2)}) collective-permute-start(bf16[4,512,128]{2,1,0:T(8,128)(2,1)} %get-tuple-element.157), channel_id=1, source_target_pairs={{0,4},{4,0},{2,6},{6,2},{1,5},{5,1},{3,7},{7,3},{8,12},{12,8},{10,... | collective-permute-start | bytes 1572872 | tf_op jit(solution)/shard_map/ppermute | solution.py:84
  194.8 44.8 %reduce-scatter.6.cloned.1.call-start = ((), (), s32[]{:S(2)}) async-start(), calls=%async_computation.4 | async-start | bytes 655360 | tf_op jit(solution)/shard_map/reduce_scatter | solution.py:1123
  210.9 8.9 %collective-permute-start.32 = (bf16[256,512]{1,0:T(8,128)(2,1)}, bf16[256,512]{1,0:T(8,128)(2,1)S(1)}, u32[]{:S(2)}, u32[]{:S(2)}) collective-permute-start(bf16[256,512]{1,0:T(8,128)(2,1)} %get-tuple-element.159), channel_id=1, source_target_pairs={{0,4},{4,0},{2,6},{6,2},{1,5},{5,1},{3,7},{7,3},{8,12},{12,8},{10,... | collective-permute-start | bytes 786440 | tf_op jit(solution)/shard_map/ppermute | solution.py:84
  224.2 8.4 %collective-permute-start.33 = (bf16[256,512]{1,0:T(8,128)(2,1)}, bf16[256,512]{1,0:T(8,128)(2,1)S(1)}, u32[]{:S(2)}, u32[]{:S(2)}) collective-permute-start(bf16[256,512]{1,0:T(8,128)(2,1)} %get-tuple-element.163.refs_2_), channel_id=1, source_target_pairs={{0,1},{1,0},{2,3},{3,2},{4,5},{5,4},{6,7},{7,6},{8,9},{9,8},{10,11... | collective-permute-start | bytes 786440 | tf_op jit(solution)/shard_map/ppermute | solution.py:76
  228.5 8.6 %collective-permute-start.36 = (bf16[4,256,128]{2,1,0:T(8,128)(2,1)}, bf16[4,256,128]{2,1,0:T(8,128)(2,1)S(1)}, u32[]{:S(2)}, u32[]{:S(2)}) collective-permute-start(bf16[4,256,128]{2,1,0:T(8,128)(2,1)} %get-tuple-element.178), channel_id=1, source_target_pairs={{0,4},{4,0},{2,6},{6,2},{1,5},{5,1},{3,7},{7,3},{8,12},{12,8},{10,... | collective-permute-start | bytes 786440 | tf_op jit(solution)/shard_map/ppermute | solution.py:84
  241.4 9.1 %collective-permute-start.41 = (bf16[1280,128]{1,0:T(8,128)(2,1)}, bf16[1280,128]{1,0:T(8,128)(2,1)S(1)}, u32[]{:S(2)}, u32[]{:S(2)}) collective-permute-start(bf16[1280,128]{1,0:T(8,128)(2,1)} %shard_map.203.refs_1_), channel_id=1, source_target_pairs={{0,4},{4,0},{2,6},{6,2},{1,5},{5,1},{3,7},{7,3},{8,12},{12,8},{10,... | collective-permute-start | bytes 983048 | tf_op jit(solution)/shard_map/ppermute | solution.py:84
  242.3 19.8 %collective-permute-start.40 = (bf16[1280,128]{1,0:T(8,128)(2,1)}, bf16[1280,128]{1,0:T(8,128)(2,1)S(1)}, u32[]{:S(2)}, u32[]{:S(2)}) collective-permute-start(bf16[1280,128]{1,0:T(8,128)(2,1)} %shard_map.203.refs_1_), channel_id=1, source_target_pairs={{0,2},{2,0},{4,6},{6,4},{1,3},{3,1},{5,7},{7,5},{8,10},{10,8},{12,... | collective-permute-start | bytes 983048 | tf_op jit(solution)/shard_map/ppermute | solution.py:80
  250.5 20.3 %collective-permute-start.45 = (bf16[1280,128]{1,0:T(8,128)(2,1)S(1)}, bf16[1280,128]{1,0:T(8,128)(2,1)S(1)}, u32[]{:S(2)}, u32[]{:S(2)}) collective-permute-start(bf16[1280,128]{1,0:T(8,128)(2,1)S(1)} %collective-permute-done.41.refs_6_.refs_3_), channel_id=1, source_target_pairs={{0,2},{2,0},{4,6},{6,4},{1,3},{3,1},{5,7},{7,5},{8,10},{10,8},{12,... | collective-permute-start | bytes 983048 | tf_op jit(solution)/shard_map/ppermute | solution.py:80
  251.1 11.0 %collective-permute-start.38 = (bf16[304,128]{1,0:T(8,128)(2,1)}, bf16[304,128]{1,0:T(8,128)(2,1)S(1)}, u32[]{:S(2)}, u32[]{:S(2)}) collective-permute-start(bf16[304,128]{1,0:T(8,128)(2,1)} %get-tuple-element.182), channel_id=1, source_target_pairs={{0,16},{8,24},{16,0},{24,8},{1,17},{9,25},{17,1},{25,9},{2,18},{10... | collective-permute-start | bytes 233480 | tf_op jit(solution)/shard_map/ppermute | solution.py:563
  266.7 9.3 %collective-permute-start.42 = (bf16[304,128]{1,0:T(8,128)(2,1)}, bf16[304,128]{1,0:T(8,128)(2,1)S(1)}, u32[]{:S(2)}, u32[]{:S(2)}) collective-permute-start(bf16[304,128]{1,0:T(8,128)(2,1)} %shard_map.204.refs_5_.refs_7_.refs_1_), channel_id=1, source_target_pairs={{0,2},{2,0},{4,6},{6,4},{1,3},{3,1},{5,7},{7,5},{8,10},{10,8},{12,... | collective-permute-start | bytes 233480 | tf_op jit(solution)/shard_map/ppermute | solution.py:80
  (76 other events, 272.3 us)
Sparse Core Ops, SparseCore 0:
  10.9 65.8 all-gather.2
  152.5 19.9 reduce-scatter.3
  194.9 17.9 reduce-scatter.7
  215.1 19.9 reduce-scatter.5
